TPU v7x, 128 devices: a whole 4x4x4 slice. The times are simulated.
128 devices in a mesh: wide: 64 (over x, z, y), narrow: 2 (over core).
Axes of the slice: x: 4, y: 4, z: 4, core: 2. Of those that a mesh axis runs over, the one named last changes fastest.
Arguments:
- node_feats: bfloat16 [65536, 256], P('wide'), may hold values from -6 to 6
- send_block: int32 [64, 64, 2, 2], P('wide', None, 'narrow'), may hold values from 0 to 7
- recv_block: int32 [64, 2, 64, 2], P('wide', 'narrow'), may hold values from 0 to 15
- tile_count: int32 [64, 2, 64], P('wide', 'narrow'), may hold values from 0 to 2, as said below
- mask_bits: int32 [64, 2, 64, 2, 9, 128], P('wide', 'narrow'), may hold values from 0 to 32767, as said below
- degree: int32 [262144], P(('wide', 'narrow')), may hold values from 64 to 512
- weight_in: bfloat16 [256, 512], replicated, may hold values from -0.375 to 0.375
- weight_out: bfloat16 [512, 256], replicated, may hold values from -0.25 to 0.25
- norm_gain: float32 [256], replicated, may hold values from 0.1 to 1.9
- cotangent: bfloat16 [65536, 256], P('wide'), may hold values from -6 to 6
Outputs:
- updated: bfloat16 [65536, 256], P('wide')
- grad_nodes: float32 [65536, 256], P('wide')
- grad_weight_in: float32 [256, 512], replicated
- grad_weight_out: float32 [512, 256], replicated
- grad_gain: float32 [256], replicated
Inputs may be any that keep to these rules, and one draw needn't show every extreme that they name: `tile_count`: at most 2; in every draw some hyperedge device holds 2 tiles from every node owner. `mask_bits`: no bit stands for a row at or past 128.
All inputs are finite; a program needn't handle non-finite values.
Results may differ from a plain program's by a relative error of at most 0.008.
Values may be sent and summed in bfloat16 or wider, within the bound.
No kernel may reach another device: no remote copies, remote signals or barrier semaphores. Data moves between devices by JAX's collectives and lax.ppermute only.
A program may use at most 192 MiB of HBM per device.

v0:
```python
import jax
import jax.numpy as jnp
from jax import lax
from jax.sharding import PartitionSpec as P


def unpack_bits(mask_words):
    tile_rows = mask_words.shape[-1]
    row_index = jnp.arange(tile_rows)
    picked = jnp.take(mask_words, row_index // 15, axis=-2)
    shifted = jnp.right_shift(picked, (row_index % 15)[:, None])
    return jnp.bitwise_and(shifted, 1).astype(jnp.bfloat16)


def shards(
    node_feats,
    send_block,
    recv_block,
    tile_count,
    mask_bits,
    degree,
    weight_in,
    weight_out,
    norm_gain,
    cotangent,
):
    wide_count = lax.axis_size("wide")
    tile_rows = mask_bits.shape[-1]
    features = node_feats.shape[1]
    node_blocks = node_feats.shape[0] // tile_rows
    edge_blocks = degree.shape[0] // tile_rows
    capacity = send_block.shape[3]
    my_sends = send_block[0, :, 0, :]
    my_edges = recv_block[0, 0]
    live_slots = jnp.arange(capacity)[None, :] < tile_count[0, 0][:, None]
    live_words = mask_bits[0, 0] * live_slots[:, :, None, None].astype(jnp.int32)
    tile_masks = unpack_bits(live_words)
    edge_hot = (my_edges[:, :, None] == jnp.arange(edge_blocks)).astype(jnp.float32)
    node_hot = (my_sends[:, :, None] == jnp.arange(node_blocks)).astype(jnp.float32)

    def fetch_rows(row_data):
        packed = row_data.reshape(node_blocks, tile_rows, features)[my_sends]
        return lax.all_to_all(packed, "wide", split_axis=0, concat_axis=0, tiled=True)

    def collect_edges(arrived):
        products = jnp.einsum(
            "skrc,skrf->skcf", tile_masks, arrived, preferred_element_type=jnp.float32
        )
        return jnp.einsum("skb,skcf->bcf", edge_hot, products).reshape(
            edge_blocks * tile_rows, features
        )

    def spread_nodes(values):
        picked = values.reshape(edge_blocks, tile_rows, features)[my_edges]
        arrived, arrived_words = (
            lax.all_to_all(picked, "wide", split_axis=0, concat_axis=0, tiled=True),
            lax.all_to_all(live_words, "wide", split_axis=0, concat_axis=0, tiled=True),
        )
        products = jnp.einsum(
            "skrc,skcf->skrf",
            unpack_bits(arrived_words),
            arrived,
            preferred_element_type=jnp.float32,
        )
        partial_sum = jnp.einsum("skb,skrf->brf", node_hot, products).reshape(
            node_blocks * tile_rows, features
        )
        return lax.psum(partial_sum, "narrow")

    hyper_total = degree.shape[0] * wide_count * lax.axis_size("narrow")
    node_total = node_feats.shape[0] * wide_count
    edge_scale = lax.rsqrt(degree.astype(jnp.float32))[:, None]
    edge_feats = (collect_edges(fetch_rows(node_feats)) * edge_scale).astype(jnp.bfloat16)
    pre_act = jnp.dot(edge_feats, weight_in, preferred_element_type=jnp.float32)
    activated = jax.nn.silu(pre_act).astype(jnp.bfloat16)
    edge_out = jnp.dot(activated, weight_out, preferred_element_type=jnp.float32).astype(
        jnp.bfloat16
    )
    summed = spread_nodes(edge_out)
    inv_rms = lax.rsqrt(jnp.mean(summed * summed, axis=-1, keepdims=True) + 1e-05)
    normed = summed * inv_rms
    updated = (node_feats.astype(jnp.float32) + normed * norm_gain).astype(jnp.bfloat16)
    upstream = cotangent.astype(jnp.float32)
    d_normed = upstream * norm_gain
    d_summed = (
        inv_rms * (d_normed - normed * jnp.mean(d_normed * normed, axis=-1, keepdims=True))
    ).astype(jnp.bfloat16)
    gain_part = jnp.sum(upstream * normed, axis=0)
    gain_whole = lax.psum(gain_part, "wide")
    d_edge = collect_edges(fetch_rows(d_summed)).astype(jnp.bfloat16)
    weight_out_part = jnp.einsum("tm,tf->mf", activated, d_edge, preferred_element_type=jnp.float32)
    d_act = jnp.einsum("tf,mf->tm", d_edge, weight_out, preferred_element_type=jnp.float32)
    gate_sig = jax.nn.sigmoid(pre_act)
    d_pre = (d_act * gate_sig * (1.0 + pre_act * (1.0 - gate_sig))).astype(jnp.bfloat16)
    weight_in_part = jnp.einsum("tf,tm->fm", edge_feats, d_pre, preferred_element_type=jnp.float32)
    d_feats = (
        jnp.einsum("tm,fm->tf", d_pre, weight_in, preferred_element_type=jnp.float32) * edge_scale
    ).astype(jnp.bfloat16)
    grad_nodes = upstream + spread_nodes(d_feats)
    in_total, out_total = lax.psum((weight_in_part, weight_out_part), ("wide", "narrow"))
    edge_factor = hyper_total ** (-0.5)
    grad_weight_in = in_total * edge_factor
    grad_weight_out = out_total * edge_factor
    grad_gain = gain_whole * node_total ** (-0.5)
    return (updated, grad_nodes, grad_weight_in, grad_weight_out, grad_gain)


def solution(mesh):
    return jax.shard_map(
        shards,
        mesh=mesh,
        in_specs=(
            P("wide", None),
            P("wide", None, "narrow", None),
            P("wide", "narrow", None, None),
            P("wide", "narrow", None),
            P("wide", "narrow", None, None, None, None),
            P(("wide", "narrow")),
            P(),
            P(),
            P(),
            P("wide", None),
        ),
        out_specs=(P("wide", None), P("wide", None), P(), P(), P()),
        check_vma=False,
    )
```

profile of v0, /device:TPU:0, one launch (start us, length us, event | category | flops | bytes accessed | tf_op | source)
XLA Modules:
  0.0 826.3 jit_solution(5242801736113965606)
XLA Ops:
  7.2 0.0 copy-start
  7.2 0.8 fusion.35
  8.0 2.1 bitcast_multiply_fusion.1
  10.1 11.5 %all-to-all-start = ((s32[64,2,9,128]{3,1,2,0:T(2,128)}), s32[64,2,9,128]{3,1,2,0:T(2,128)S(1)}, u32[]{:S(2)}, u32[]{:S(2)}) async-start(s32[64,2,9,128]{3,1,2,0:T(2,128)} %bitcast_multiply_fusion.1), calls=%async_computation | async-start | bytes 1179648 | tf_op jit(solution)/shard_map/all_to_all | solution.py:57
  21.6 0.7 compare_select_fusion.1
  22.3 0.1 copy.17
  22.4 0.1 reshape.170
  22.5 7.6 gather_fusion
  30.2 5.3 all-to-all-done
  35.5 5.9 all-to-all-start.1
  41.4 0.3 all-reduce.5.cloned.1.call-start
  41.7 0.1 copy.19
  41.8 0.1 reshape.178
  42.0 0.0 copy-start.10
  42.0 15.8 %gather_fusion.5 = s32[128,64,2,128]{3,2,1,0:T(2,128)} fusion(s32[64,2,9,128]{3,1,2,0:T(2,128)} %bitcast_multiply_fusion.1, s32[1024]{0:T(1024)S(1)} %pad_clamp_fusion.2), kind=kCustom, calls=%fused_computation.1.clone | custom fusion | bytes 16777728 | tf_op jit(solution)/shard_map/jit(_take)/gather | solution.py:10
  57.9 14.8 %gather_fusion.4 = s32[128,64,2,128]{3,2,1,0:T(2,128)} fusion(s32[64,2,9,128]{3,1,2,0:T(2,128)S(1)} %all-to-all-done, s32[1024]{0:T(1024)S(1)} %pad_clamp_fusion.2), kind=kCustom, calls=%fused_computation.clone | custom fusion | bytes 16777728 | tf_op jit(solution)/shard_map/jit(_take)/gather | solution.py:10
  72.6 14.5 %fusion.11 = (bf16[64,2,128,128]{3,1,0,2:T(2,128)(2,1)}, bf16[64,2,128,128]{3,1,0,2:T(2,128)(2,1)}) fusion(s32[128,64,2,128]{3,2,1,0:T(2,128)} %gather_fusion.4, pred[128]{0:T(512)(128)(4,1)S(1)} %compare_and_fusion, s32[128]{0:T(128)S(1)} %and_select_fusion, s32[128,64,2,128]{3,2,1,0:T(2,128)} %gather_fusion.5), kind=kLoop, calls=%fused_computation.19 | loop fusion | flops 16777216 | bytes 25166464 | tf_op jit(solution)/shard_map/convert_element_type | solution.py:12
  87.2 11.8 %copy.23 = bf16[64,2,128,128]{2,3,1,0:T(8,128)(2,1)} copy(bf16[64,2,128,128]{3,1,0,2:T(2,128)(2,1)} %get-tuple-element.13) | data formatting | bytes 8388608 | tf_op jit(solution)/shard_map/convert_element_type | solution.py:12
  99.0 50.6 %all-to-all-done.1 = bf16[64,2,128,256]{3,2,1,0:T(8,128)(2,1)} async-done(((bf16[64,2,128,256]{3,2,1,0:T(8,128)(2,1)}), bf16[64,2,128,256]{3,2,1,0:T(8,128)(2,1)}, u32[]{:S(2)}, u32[]{:S(2)}) %all-to-all-start.1) | async-done | bytes 8388640 | tf_op jit(solution)/shard_map/all_to_all | solution.py:43
  149.6 7.0 fusion.46
  156.6 4.5 fusion.18
  161.1 1.2 copy.18
  162.3 0.3 fusion.17
  162.7 0.0 copy-start.12
  162.7 3.2 multiply_convert_fusion.1
  165.9 1.4 copy-done.5
  167.2 0.0 copy-done.12
  167.3 0.7 convolution_convert_fusion
  168.0 6.6 gather_fusion.1
  174.5 117.9 %all_to_all.26 = bf16[64,2,128,256]{3,2,1,0:T(8,128)(2,1)} all-to-all(bf16[64,2,128,256]{3,2,1,0:T(8,128)(2,1)} %bitcast.85), channel_id=1, replica_groups=mesh['wide'=64,'narrow'=2] {'wide'}, dimensions={0} | all-to-all | bytes 16777216 | tf_op jit(solution)/shard_map/all_to_all | solution.py:56
  292.4 0.0 copy-done.2
  292.4 11.3 %fusion.14 = bf16[64,2,128,256]{3,2,1,0:T(8,128)(2,1)} fusion(bf16[64,2,128,256]{3,2,1,0:T(8,128)(2,1)} %all_to_all.26, bf16[64,2,128,128]{3,1,0,2:T(2,128)(2,1)S(1)} %copy-done.2), kind=kOutput, calls=%fused_computation.25 | convolution fusion | flops 1073741824 | bytes 20971520 | tf_op jit(solution)/shard_map/skrc,skcf->skrf/dot_general | solution.py:59
  303.7 7.9 fusion.23
  311.7 1.3 copy.20
  313.0 0.0 all-reduce.5.cloned.1.call-update
  313.0 24.9 %all-reduce.5.cloned.1.call-done = f32[1024,256]{1,0:T(8,128)} async-done(((f32[1024,256]{1,0:T(8,128)}), f32[1024,256]{1,0:T(8,128)}) %all-reduce.5.cloned.1.call-update) | async-done | bytes 1048592 | tf_op jit(solution)/shard_map/psum | solution.py:68
  337.9 1.4 multiply_reduce_fusion
  339.3 1.7 fusion.34
  341.1 2.4 fusion.33
  343.5 6.6 gather_fusion.2
  350.1 108.8 %all_to_all.27 = bf16[64,2,128,256]{3,2,1,0:T(8,128)(2,1)} all-to-all(bf16[64,2,128,256]{3,2,1,0:T(8,128)(2,1)} %bitcast.84), channel_id=1, replica_groups=mesh['wide'=64,'narrow'=2] {'wide'}, dimensions={0} | all-to-all | bytes 16777216 | tf_op jit(solution)/shard_map/all_to_all | solution.py:43
  458.9 9.0 %fusion.47 = bf16[64,2,128,256]{3,2,1,0:T(8,128)(2,1)} fusion(bf16[64,2,128,128]{2,3,1,0:T(8,128)(2,1)S(1)} %copy-done.3, bf16[64,2,128,256]{3,2,1,0:T(8,128)(2,1)} %all_to_all.27), kind=kOutput, calls=%fused_computation.77 | convolution fusion | flops 1073741824 | bytes 20971520 | tf_op jit(solution)/shard_map/skrc,skrf->skcf/dot_general | solution.py:46
  467.9 8.1 bitcast_convert_fusion
  476.0 0.4 copy.21
  476.4 1.8 multiply_convert_fusion
  478.2 0.7 fusion.16
  478.9 0.6 copy-done.13
  479.5 6.6 gather_fusion.3
  486.1 13.2 %all-to-all-start.4 = ((bf16[64,2,128,256]{3,2,1,0:T(8,128)(2,1)}), bf16[64,2,128,256]{3,2,1,0:T(8,128)(2,1)}, u32[]{:S(2)}, u32[]{:S(2)}) async-start(bf16[64,2,128,256]{3,2,1,0:T(8,128)(2,1)} %bitcast.83), calls=%async_computation.4 | async-start | bytes 16777216 | tf_op jit(solution)/shard_map/all_to_all | solution.py:56
  499.3 0.0 all-reduce.9.cloned.1.call-start
  499.3 3.1 fusion.49
  502.5 3.1 fusion.48
  505.6 0.0 all-reduce.9.cloned.1.call-update
  505.6 0.0 all-reduce.7.cloned.1.call-start
  505.7 104.7 %all-to-all-done.4 = bf16[64,2,128,256]{3,2,1,0:T(8,128)(2,1)} async-done(((bf16[64,2,128,256]{3,2,1,0:T(8,128)(2,1)}), bf16[64,2,128,256]{3,2,1,0:T(8,128)(2,1)}, u32[]{:S(2)}, u32[]{:S(2)}) %all-to-all-start.4) | async-done | bytes 8388640 | tf_op jit(solution)/shard_map/all_to_all | solution.py:56
  610.4 12.2 %fusion.12 = bf16[64,2,128,256]{3,2,1,0:T(8,128)(2,1)} fusion(bf16[64,2,128,256]{3,2,1,0:T(8,128)(2,1)} %all-to-all-done.4, bf16[64,2,128,128]{3,1,0,2:T(2,128)(2,1)} %get-tuple-element.12), kind=kOutput, calls=%fused_computation.23 | convolution fusion | flops 1073741824 | bytes 20971520 | tf_op jit(solution)/shard_map/skrc,skcf->skrf/dot_general | solution.py:59
  622.5 7.9 fusion.26
  630.4 1.3 copy.22
  631.7 0.0 all-reduce.7.cloned.1.call-update
  631.7 181.3 %psum.39 = f32[256]{0:T(256)S(1)} all-reduce(f32[256]{0:T(256)S(1)} %get-tuple-element.6), channel_id=1, replica_groups=mesh['wide'=64,'narrow'=2] {'wide'}, use_global_device_ids=true, to_apply=%region_7.9 | all-reduce | flops 256 | bytes 2048 | tf_op jit(solution)/shard_map/psum | solution.py:89
  813.0 0.6 broadcast_multiply_fusion.3
  813.6 1.9 broadcast_multiply_fusion.1
  815.5 1.9 broadcast_multiply_fusion
  817.3 2.3 convert_add_fusion
  (35 shorter events, 0.1 us)
Async XLA Ops:
  7.2 155.5 %copy-start = (bf16[256,512]{1,0:T(8,128)(2,1)S(1)}, bf16[256,512]{1,0:T(8,128)(2,1)}, u32[]{:S(2)}) copy-start(bf16[256,512]{1,0:T(8,128)(2,1)} %param.18) | copy-start | bytes 786436
  10.1 25.4 %all-to-all-start = ((s32[64,2,9,128]{3,1,2,0:T(2,128)}), s32[64,2,9,128]{3,1,2,0:T(2,128)S(1)}, u32[]{:S(2)}, u32[]{:S(2)}) async-start(s32[64,2,9,128]{3,1,2,0:T(2,128)} %bitcast_multiply_fusion.1), calls=%async_computation | async-start | bytes 1179648 | tf_op jit(solution)/shard_map/all_to_all | solution.py:57
  35.5 6.3 copy-start.9
  35.5 114.1 %all-to-all-start.1 = ((bf16[64,2,128,256]{3,2,1,0:T(8,128)(2,1)}), bf16[64,2,128,256]{3,2,1,0:T(8,128)(2,1)}, u32[]{:S(2)}, u32[]{:S(2)}) async-start(bf16[64,2,128,256]{3,2,1,0:T(8,128)(2,1)} %bitcast.82), calls=%async_computation.1 | async-start | bytes 16777216 | tf_op jit(solution)/shard_map/all_to_all | solution.py:43
  41.4 296.5 %all-reduce.5.cloned.1.call-start = ((), (), s32[]{:S(2)}) async-start(), calls=%async_computation.5 | async-start | bytes 2097152 | tf_op jit(solution)/shard_map/psum | solution.py:68
  42.0 15.8 %copy-start.10 = (s32[2048]{0:T(1024)S(1)}, s32[2048]{0:T(1024)}, u32[]{:S(2)}) copy-start(s32[2048]{0:T(1024)} %param.17) | copy-start | bytes 24580
  162.7 3.2 copy-start.6
  162.7 4.6 copy-start.12
  165.9 1.4 copy-start.5
  174.5 117.9 %copy-start.2 = (bf16[64,2,128,128]{3,1,0,2:T(2,128)(2,1)S(1)}, bf16[64,2,128,128]{3,1,0,2:T(2,128)(2,1)}, u32[]{:S(2)}) copy-start(bf16[64,2,128,128]{3,1,0,2:T(2,128)(2,1)} %get-tuple-element.12) | copy-start | bytes 12582916
  292.4 11.3 %copy-start.8 = (s32[1,64,1,2]{1,3,2,0:T(2,128)S(1)}, s32[1,64,1,2]{1,3,2,0:T(2,128)}, u32[]{:S(2)}) copy-start(s32[1,64,1,2]{1,3,2,0:T(2,128)} %param.13) | copy-start | bytes 1540
  303.7 35.6 %copy-start.4 = (bf16[1024,256]{1,0:T(8,128)(2,1)S(1)}, bf16[1024,256]{1,0:T(8,128)(2,1)}, u32[]{:S(2)}) copy-start(bf16[1024,256]{1,0:T(8,128)(2,1)} %param.21) | copy-start | bytes 1572868
  303.7 35.6 %copy-start.11 = (f32[256]{0:T(256)S(1)}, f32[256]{0:T(256)}, u32[]{:S(2)}) copy-start(f32[256]{0:T(256)} %param.20) | copy-start | bytes 3076
  303.7 37.4 %copy-start.1 = (bf16[1024,256]{1,0:T(8,128)(2,1)S(1)}, bf16[1024,256]{1,0:T(8,128)(2,1)}, u32[]{:S(2)}) copy-start(bf16[1024,256]{1,0:T(8,128)(2,1)} %param.12) | copy-start | bytes 1572868
  350.1 108.8 %copy-start.3 = (bf16[64,2,128,128]{2,3,1,0:T(8,128)(2,1)S(1)}, bf16[64,2,128,128]{2,3,1,0:T(8,128)(2,1)}, u32[]{:S(2)}) copy-start(bf16[64,2,128,128]{2,3,1,0:T(8,128)(2,1)} %copy.23) | copy-start | bytes 12582916
  467.9 8.4 %copy-start.14 = (f32[2048,512]{1,0:T(8,128)S(1)}, f32[2048,512]{1,0:T(8,128)}, u32[]{:S(2)}) copy-start(f32[2048,512]{1,0:T(8,128)} %get-tuple-element.15) | copy-start | bytes 12582916
  478.2 1.3 copy-start.13
  486.1 16.4 %copy-start.7 = (bf16[2048,256]{1,0:T(8,128)(2,1)S(1)}, bf16[2048,256]{1,0:T(8,128)(2,1)}, u32[]{:S(2)}) copy-start(bf16[2048,256]{1,0:T(8,128)(2,1)} %copy-done.6) | copy-start | bytes 3145732
  486.1 124.3 %all-to-all-start.4 = ((bf16[64,2,128,256]{3,2,1,0:T(8,128)(2,1)}), bf16[64,2,128,256]{3,2,1,0:T(8,128)(2,1)}, u32[]{:S(2)}, u32[]{:S(2)}) async-start(bf16[64,2,128,256]{3,2,1,0:T(8,128)(2,1)} %bitcast.83), calls=%async_computation.4 | async-start | bytes 16777216 | tf_op jit(solution)/shard_map/all_to_all | solution.py:56
  499.3 314.3 %all-reduce.9.cloned.1.call-start = ((), (), s32[]{:S(2)}) async-start(), calls=%async_computation.7 | async-start | bytes 2097152 | tf_op jit(solution)/shard_map/psum | solution.py:100
  505.6 311.7 %all-reduce.7.cloned.1.call-start = ((), (), s32[]{:S(2)}) async-start(), calls=%async_computation.6 | async-start | bytes 2097152 | tf_op jit(solution)/shard_map/psum | solution.py:68
Sparse Core Ops, SparseCore 0:
  313.1 24.7 all-reduce.4
  506.5 232.2 all-reduce.8
  741.8 24.4 all-reduce.6
where the time goes:
time: 831 us; the launch traced here: 826 us
  blocking collectives  408 us (49%)
  waiting for transfers between devices  186 us (22%)
  matrix products  80.5 us (10%)
  local copies, waits for them, and re-layouts  76.3 us (9%)
  starting transfers between devices  31 us (4%)
  other arithmetic  30.8 us (4%)
  between operations  14.2 us (2%)
    psum x1, blocking collectives, shards(): gain_whole = lax.psum(gain_part, 'wide')  181 us
    all_to_all x1, blocking collectives, spread_nodes(): lax.all_to_all(picked, 'wide', split_axis=0, concat_axis=0, tiled=True)  118 us
    all_to_all x1, blocking collectives, fetch_rows(): lax.all_to_all(packed, 'wide', split_axis=0, concat_axis=0, tiled=True)  109 us
    all_to_all x1, waiting for transfers between devices, spread_nodes(): lax.all_to_all(picked, 'wide', split_axis=0, concat_axis=0, tiled=True)  105 us
    all_to_all x1, waiting for transfers between devices, fetch_rows(): lax.all_to_all(packed, 'wide', split_axis=0, concat_axis=0, tiled=True)  50.6 us
    gather x2, local copies, waits for them, and re-layouts, unpack_bits(): picked = jnp.take(mask_words, row_index // 15, axis=-2)  30.6 us
    psum x2, waiting for transfers between devices, spread_nodes(): return lax.psum(partial_sum, 'narrow')  24.9 us
    dot_general x2, matrix products, spread_nodes(): jnp.einsum('skrc,skcf->skrf', unpack_bits(arrived_words), arrived, prefer...  23.5 us
  transfers between devices with their start and end apart: 6, of which 4 were waited for; matrix products, arithmetic and copies ran while one was open for 12% of the time, Pallas kernels for 0%

commit v1 on v0

v1 whole, which is shorter than its diff:
```python
import functools

import jax
import jax.numpy as jnp
from jax import lax
from jax.experimental import pallas as pl
from jax.experimental.pallas import tpu as pltpu
from jax.sharding import PartitionSpec as P

F32 = jnp.float32
BF16 = jnp.bfloat16
TILE = 128
STEP_OWNERS = 4
PARAMS = pltpu.CompilerParams(vmem_limit_bytes=52 * 1024 * 1024)


def dot(a, b, dims=((1,), (0,))):
    return lax.dot_general(a, b, (dims, ((), ())), preferred_element_type=F32)


def rows_at(block):
    return pl.ds(pl.multiple_of(block * TILE, TILE), TILE)


def unpack_kernel(count_ref, words_ref, bit_ref, mask_ref, mask_t_ref):
    step = pl.program_id(0)
    tiles = words_ref.shape[0]
    row = lax.broadcasted_iota(jnp.int32, (8, TILE), 0)
    for tile in range(tiles):
        slot = tile % 2
        live = count_ref[step * (tiles // 2) + tile // 2] > slot
        words = jnp.where(live, words_ref[tile], 0)
        groups = []
        for first in range(0, TILE, 8):
            low, high = first // 15, (first + 7) // 15
            picked = jnp.broadcast_to(words[low : low + 1], (8, TILE))
            if high != low:
                later = jnp.broadcast_to(words[high : high + 1], (8, TILE))
                picked = jnp.where(row + first >= high * 15, later, picked)
            hit = jnp.bitwise_and(picked, bit_ref[first : first + 8]) != 0
            groups.append(jnp.where(hit, 1.0, 0.0).astype(F32))
        mask = jnp.concatenate(groups, axis=0)
        mask_ref[tile] = mask.astype(BF16)
        mask_t_ref[tile] = mask.T.astype(BF16)


def unpack(count, words):
    tiles = words.shape[0]
    per = 8
    bit = jnp.left_shift(1, lax.broadcasted_iota(jnp.int32, (TILE, TILE), 0) % 15)
    out = jax.ShapeDtypeStruct((tiles, TILE, TILE), BF16)
    block = pl.BlockSpec((per, TILE, TILE), lambda i, c: (i, 0, 0))
    return pl.pallas_call(
        unpack_kernel,
        out_shape=(out, out),
        grid_spec=pltpu.PrefetchScalarGridSpec(
            num_scalar_prefetch=1,
            grid=(tiles // per,),
            in_specs=[
                pl.BlockSpec((per,) + words.shape[1:], lambda i, c: (i, 0, 0)),
                pl.BlockSpec((TILE, TILE), lambda i, c: (0, 0)),
            ],
            out_specs=(block, block),
        ),
        compiler_params=PARAMS,
        cost_estimate=pl.CostEstimate(flops=tiles * 2**18, bytes_accessed=tiles * 2**17, transcendentals=0),
        name="unpack_masks",
    )(count, words, bit)


def select_kernel(send_ref, rows_ref, out_ref):
    step = pl.program_id(0)
    for owner in range(STEP_OWNERS):
        for slot in range(2):
            block = send_ref[(step * STEP_OWNERS + owner) * 2 + slot]
            out_ref[owner, slot * TILE : (slot + 1) * TILE] = rows_ref[rows_at(block)]


def select(send, rows, owners):
    features = rows.shape[1]
    return pl.pallas_call(
        select_kernel,
        out_shape=jax.ShapeDtypeStruct((owners, 2 * TILE, features), BF16),
        grid_spec=pltpu.PrefetchScalarGridSpec(
            num_scalar_prefetch=1,
            grid=(owners // STEP_OWNERS,),
            in_specs=[pl.BlockSpec(rows.shape, lambda i, c: (0, 0))],
            out_specs=pl.BlockSpec((STEP_OWNERS, 2 * TILE, features), lambda i, c: (i, 0, 0)),
        ),
        compiler_params=PARAMS,
        name="select_blocks",
    )(send, rows)


def collect_step(step, recv_ref, arrived_ref, mask_t_ref, acc):
    for owner in range(STEP_OWNERS):
        for slot in range(2):
            tile = owner * 2 + slot
            where = rows_at(recv_ref[step * STEP_OWNERS * 2 + tile])
            acc[where] += dot(mask_t_ref[tile], arrived_ref[owner, slot * TILE : (slot + 1) * TILE])


def spread_step(step, recv_ref, mask_ref, values, out_ref):
    for owner in range(STEP_OWNERS):
        for slot in range(2):
            tile = owner * 2 + slot
            where = rows_at(recv_ref[step * STEP_OWNERS * 2 + tile])
            out_ref[owner, slot * TILE : (slot + 1) * TILE] = dot(mask_ref[tile], values[where]).astype(BF16)


def forward_kernel(
    steps, recv_ref, arrived_ref, mask_t_ref, mask_ref, scale_ref, w_in_ref, w_out_ref,
    out_ref, feats_ref, act_ref, gate_ref, acc, values,
):
    step = pl.program_id(0)

    @pl.when(step == 0)
    def _():
        acc[...] = jnp.zeros_like(acc)

    @pl.when(step < steps)
    def _():
        collect_step(step, recv_ref, arrived_ref, mask_t_ref, acc)

    @pl.when(step == steps - 1)
    def _():
        chunk = 256

        def body(i, carry):
            at = pl.ds(pl.multiple_of(i * chunk, chunk), chunk)
            feats = (acc[at] * scale_ref[at]).astype(BF16)
            feats_ref[at] = feats
            pre = dot(feats, w_in_ref[...])
            sig = jax.nn.sigmoid(pre)
            act = (pre * sig).astype(BF16)
            act_ref[at] = act
            gate_ref[at] = sig * (1.0 + pre * (1.0 - sig))
            values[at] = dot(act, w_out_ref[...]).astype(BF16)
            return carry

        lax.fori_loop(0, acc.shape[0] // chunk, body, 0)

    @pl.when(step >= steps)
    def _():
        spread_step(step - steps, recv_ref, mask_ref, values, out_ref)


def backward_kernel(
    steps, recv_ref, arrived_ref, mask_t_ref, mask_ref, scale_ref, w_in_ref, w_out_ref,
    feats_ref, act_ref, gate_ref, out_ref, acc, values, grads,
):
    step = pl.program_id(0)
    width = feats_ref.shape[1]
    inner = act_ref.shape[1]

    @pl.when(step == 0)
    def _():
        acc[...] = jnp.zeros_like(acc)
        grads[...] = jnp.zeros_like(grads)

    @pl.when(step < steps)
    def _():
        collect_step(step, recv_ref, arrived_ref, mask_t_ref, acc)

    @pl.when(step == steps - 1)
    def _():
        chunk = 256

        def body(i, carry):
            at = pl.ds(pl.multiple_of(i * chunk, chunk), chunk)
            d_edge = acc[at].astype(BF16)
            d_act = dot(d_edge, w_out_ref[...], ((1,), (1,)))
            d_pre = (d_act * gate_ref[at]).astype(BF16)
            values[at] = (dot(d_pre, w_in_ref[...], ((1,), (1,))) * scale_ref[at]).astype(BF16)
            grads[:inner] += dot(act_ref[at], d_edge, ((0,), (0,)))
            in_part = dot(feats_ref[at], d_pre, ((0,), (0,)))
            for piece in range(inner // width):
                first = inner + piece * width
                grads[first : first + width] += in_part[:, piece * width : (piece + 1) * width]
            return carry

        lax.fori_loop(0, acc.shape[0] // chunk, body, 0)

    @pl.when(step >= steps)
    def _():
        spread_step(step - steps, recv_ref, mask_ref, values, out_ref)
        extra = out_ref.shape[1] - 2 * TILE
        for owner in range(STEP_OWNERS):
            first = ((step - steps) * STEP_OWNERS + owner) * extra
            out_ref[owner, 2 * TILE :] = grads[pl.ds(pl.multiple_of(first, extra), extra)].astype(BF16)


def edge_specs(steps, arrived, scale, w_in, w_out):
    per = STEP_OWNERS * 2
    whole = lambda shape: pl.BlockSpec(shape, lambda i, c: (0,) * len(shape))
    return [
        pl.BlockSpec((STEP_OWNERS,) + arrived.shape[1:], lambda i, c: (jnp.minimum(i, steps - 1), 0, 0)),
        pl.BlockSpec((per, TILE, TILE), lambda i, c: (jnp.minimum(i, steps - 1), 0, 0)),
        pl.BlockSpec((per, TILE, TILE), lambda i, c: (jnp.maximum(i - steps, 0), 0, 0)),
        whole(scale.shape),
        whole(w_in.shape),
        whole(w_out.shape),
    ], whole


def edges_forward(recv, arrived, mask_t, mask, scale, w_in, w_out):
    owners = arrived.shape[0]
    steps = owners // STEP_OWNERS
    edges, width, inner = scale.shape[0], w_in.shape[0], w_in.shape[1]
    specs, whole = edge_specs(steps, arrived, scale, w_in, w_out)
    return pl.pallas_call(
        functools.partial(forward_kernel, steps),
        out_shape=(
            jax.ShapeDtypeStruct((owners, 2 * TILE, width), BF16),
            jax.ShapeDtypeStruct((edges, width), BF16),
            jax.ShapeDtypeStruct((edges, inner), BF16),
            jax.ShapeDtypeStruct((edges, inner), F32),
        ),
        grid_spec=pltpu.PrefetchScalarGridSpec(
            num_scalar_prefetch=1,
            grid=(2 * steps,),
            in_specs=specs,
            out_specs=(
                pl.BlockSpec((STEP_OWNERS, 2 * TILE, width), lambda i, c: (jnp.maximum(i - steps, 0), 0, 0)),
                whole((edges, width)),
                whole((edges, inner)),
                whole((edges, inner)),
            ),
            scratch_shapes=[pltpu.VMEM((edges, width), F32), pltpu.VMEM((edges, width), BF16)],
        ),
        compiler_params=PARAMS,
        name="edges_forward",
    )(recv, arrived, mask_t, mask, scale, w_in, w_out)


def edges_backward(recv, arrived, mask_t, mask, scale, w_in, w_out, feats, act, gate):
    owners = arrived.shape[0]
    steps = owners // STEP_OWNERS
    edges, width, inner = scale.shape[0], w_in.shape[0], w_in.shape[1]
    grad_rows = 2 * inner
    extra = grad_rows // owners
    specs, whole = edge_specs(steps, arrived, scale, w_in, w_out)
    return pl.pallas_call(
        functools.partial(backward_kernel, steps),
        out_shape=jax.ShapeDtypeStruct((owners, 2 * TILE + extra, width), BF16),
        grid_spec=pltpu.PrefetchScalarGridSpec(
            num_scalar_prefetch=1,
            grid=(2 * steps,),
            in_specs=specs + [whole(feats.shape), whole(act.shape), whole(gate.shape)],
            out_specs=pl.BlockSpec(
                (STEP_OWNERS, 2 * TILE + extra, width), lambda i, c: (jnp.maximum(i - steps, 0), 0, 0)
            ),
            scratch_shapes=[
                pltpu.VMEM((edges, width), F32),
                pltpu.VMEM((edges, width), BF16),
                pltpu.VMEM((grad_rows, width), F32),
            ],
        ),
        compiler_params=PARAMS,
        name="edges_backward",
    )(recv, arrived, mask_t, mask, scale, w_in, w_out, feats, act, gate)


def gather_sum_kernel(send_ref, arrived_ref, out_ref):
    step = pl.program_id(0)
    nodes = out_ref.shape[0] - (arrived_ref.shape[1] - 2 * TILE)

    @pl.when(step == 0)
    def _():
        out_ref[...] = jnp.zeros_like(out_ref)

    for owner in range(STEP_OWNERS):
        for slot in range(2):
            where = rows_at(send_ref[(step * STEP_OWNERS + owner) * 2 + slot])
            out_ref[where] += arrived_ref[owner, slot * TILE : (slot + 1) * TILE].astype(F32)
        if arrived_ref.shape[1] > 2 * TILE:
            out_ref[nodes:] += arrived_ref[owner, 2 * TILE :].astype(F32)


def gather_sum(send, arrived, nodes):
    owners, rows, width = arrived.shape
    total = nodes + rows - 2 * TILE
    return pl.pallas_call(
        gather_sum_kernel,
        out_shape=jax.ShapeDtypeStruct((total, width), F32),
        grid_spec=pltpu.PrefetchScalarGridSpec(
            num_scalar_prefetch=1,
            grid=(owners // STEP_OWNERS,),
            in_specs=[pl.BlockSpec((STEP_OWNERS, rows, width), lambda i, c: (i, 0, 0))],
            out_specs=pl.BlockSpec((total, width), lambda i, c: (0, 0)),
        ),
        compiler_params=PARAMS,
        name="node_sums",
    )(send, arrived)


def norm_kernel(
    send_ref, mine_ref, other_ref, feats_ref, cot_ref, gain_ref, updated_ref, part_ref, out_ref, d_summed
):
    step = pl.program_id(0)

    @pl.when(step == 0)
    def _():
        gain = gain_ref[...]

        def body(i, part):
            at = rows_at(i)
            summed = mine_ref[at] + other_ref[at]
            inv_rms = lax.rsqrt(jnp.mean(summed * summed, axis=-1, keepdims=True) + 1e-05)
            normed = summed * inv_rms
            updated_ref[at] = (feats_ref[at].astype(F32) + normed * gain).astype(BF16)
            upstream = cot_ref[at].astype(F32)
            d_normed = upstream * gain
            inner = jnp.mean(d_normed * normed, axis=-1, keepdims=True)
            d_summed[at] = (inv_rms * (d_normed - normed * inner)).astype(BF16)
            return part + jnp.sum((upstream * normed).reshape(TILE // 8, 8, -1), axis=0)

        part_ref[...] = lax.fori_loop(0, mine_ref.shape[0] // TILE, body, jnp.zeros_like(part_ref))

    select_kernel(send_ref, d_summed, out_ref)


def norm_and_select(send, mine, other, feats, cot, gain, owners):
    nodes, width = feats.shape
    whole = lambda shape: pl.BlockSpec(shape, lambda i, c: (0,) * len(shape))
    return pl.pallas_call(
        norm_kernel,
        out_shape=(
            jax.ShapeDtypeStruct((nodes, width), BF16),
            jax.ShapeDtypeStruct((8, width), F32),
            jax.ShapeDtypeStruct((owners, 2 * TILE, width), BF16),
        ),
        grid_spec=pltpu.PrefetchScalarGridSpec(
            num_scalar_prefetch=1,
            grid=(owners // STEP_OWNERS,),
            in_specs=[whole((nodes, width))] * 4 + [whole((1, width))],
            out_specs=(
                whole((nodes, width)),
                whole((8, width)),
                pl.BlockSpec((STEP_OWNERS, 2 * TILE, width), lambda i, c: (i, 0, 0)),
            ),
            scratch_shapes=[pltpu.VMEM((nodes, width), BF16)],
        ),
        compiler_params=PARAMS,
        name="norm_and_select",
    )(send, mine, other, feats, cot, gain)


def exchange(rows):
    return lax.all_to_all(rows, "wide", split_axis=0, concat_axis=0, tiled=True)


def swap(rows):
    return lax.ppermute(rows, "narrow", [(0, 1), (1, 0)])


def shards(
    node_feats,
    send_block,
    recv_block,
    tile_count,
    mask_bits,
    degree,
    weight_in,
    weight_out,
    norm_gain,
    cotangent,
):
    owners = lax.axis_size("wide")
    nodes, width = node_feats.shape
    inner = weight_in.shape[1]
    send = send_block.reshape(-1)
    recv = recv_block.reshape(-1)
    count = tile_count.reshape(-1)
    words = mask_bits.reshape((-1,) + mask_bits.shape[4:])
    scale = lax.rsqrt(degree.astype(F32))[:, None]
    gain = norm_gain[None, :]

    mask, mask_t = unpack(count, words)
    arrived = exchange(select(send, node_feats, owners))
    products, feats, act, gate = edges_forward(recv, arrived, mask_t, mask, scale, weight_in, weight_out)
    mine = gather_sum(send, exchange(products), nodes)
    updated, part, picked = norm_and_select(send, mine, swap(mine), node_feats, cotangent, gain, owners)
    products = edges_backward(
        recv, exchange(picked), mask_t, mask, scale, weight_in, weight_out, feats, act, gate
    )
    mine = gather_sum(send, exchange(products), nodes)
    both = mine + swap(mine)
    grad_nodes = cotangent.astype(F32) + both[:nodes]

    core = lax.axis_index("narrow")
    extra = mine.shape[0] - nodes
    half = lax.dynamic_slice_in_dim(both[nodes:], core * (extra // 2), extra // 2, 0)
    chunk = jnp.concatenate([half.reshape(extra, width // 2), part.sum(0).reshape(-1, width // 2)], 0)
    chunk = jnp.pad(chunk, ((0, -chunk.shape[0] % 8), (0, 0)))
    everyone = exchange(jnp.broadcast_to(chunk[None], (owners,) + chunk.shape))
    grad_gain = everyone[:, extra : extra + width // (width // 2)].sum(0).reshape(width)
    halves = everyone[:, :extra].reshape(owners, extra // 2, width)
    theirs = swap(halves)
    lower = jnp.where(core == 0, halves, theirs)
    upper = jnp.where(core == 0, theirs, halves)
    grads = jnp.concatenate([lower, upper], 1).reshape(2 * inner, width)
    pieces = inner // width
    grad_out = grads[:inner]
    grad_in = grads[inner:].reshape(pieces, width, width).transpose(1, 0, 2).reshape(width, inner)

    edge_factor = (degree.shape[0] * owners * lax.axis_size("narrow")) ** (-0.5)
    return (
        updated,
        grad_nodes,
        grad_in * edge_factor,
        grad_out * edge_factor,
        grad_gain * (nodes * owners) ** (-0.5),
    )


def solution(mesh):
    return jax.shard_map(
        shards,
        mesh=mesh,
        in_specs=(
            P("wide", None),
            P("wide", None, "narrow", None),
            P("wide", "narrow", None, None),
            P("wide", "narrow", None),
            P("wide", "narrow", None, None, None, None),
            P(("wide", "narrow")),
            P(),
            P(),
            P(),
            P("wide", None),
        ),
        out_specs=(P("wide", None), P("wide", None), P(), P(), P()),
        check_vma=False,
    )
```

time: 831 us -> 614 us (0.74)
  Pallas kernels: 0 us -> 111 us
  matrix products: 80.5 us -> 0 us
  local copies, waits for them, and re-layouts: 76.3 us -> 8.04 us
  blocking collectives: 408 us -> 345 us
  waiting for transfers between devices: 186 us -> 124 us
  other arithmetic: 30.8 us -> 4.36 us
  starting transfers between devices: 31 us -> 17.2 us
  between operations: 14.2 us -> 0.86 us
    psum x1 -> x0, blocking collectives: 181 us -> none  [shards(): gain_whole = lax.psum(gain_part, 'wide')]
    all_to_all x2 -> x3, blocking collectives: 227 us -> 345 us  [exchange(): return lax.all_to_all(rows, 'wide', split_axis=0, concat_axis=0, tiled=True)]
    pallas_call x0 -> x7, Pallas kernels: none -> 111 us  [the longest x1 32.4 us: edges_backward(): pl.pallas_call(functools.partial(backward_kernel, steps), out_shape=jax.S...]
    dot_general x14 -> x0, matrix products: 80.5 us -> none  [the longest x2 23.5 us: spread_nodes(): jnp.einsum('skrc,skcf->skrf', unpack_bits(arrived_words), arrived, prefer...]
    gather x6 -> x0, local copies, waits for them, and re-layouts: 57.9 us -> none  [the longest x2 30.6 us: unpack_bits(): picked = jnp.take(mask_words, row_index // 15, axis=-2)]
    all_to_all x3 -> x2, waiting for transfers between devices: 161 us -> 119 us  [exchange(): return lax.all_to_all(rows, 'wide', split_axis=0, concat_axis=0, tiled=True)]
    psum x3 -> x0, waiting for transfers between devices: 24.9 us -> none  [the longest x2 24.9 us: spread_nodes(): return lax.psum(partial_sum, 'narrow')]
    convert_element_type x4 -> x0, other arithmetic: 18.1 us -> none  [the longest x1 14.5 us: unpack_bits(): return jnp.bitwise_and(shifted, 1).astype(jnp.bfloat16)]
  transfers between devices with their start and end apart: 6 -> 5, of which waited for: 4 -> 5; matrix products, arithmetic and copies ran while one was open for 12% -> 1% of each run, Pallas kernels for 0% -> 1%
where the time goes in v1:
time: 614 us; the launch traced here: 611 us
  blocking collectives  345 us (56%)
  waiting for transfers between devices  124 us (20%)
  Pallas kernels  111 us (18%)
  starting transfers between devices  17.2 us (3%)
  local copies, waits for them, and re-layouts  8.04 us (1%)
    all_to_all x3, blocking collectives, exchange(): return lax.all_to_all(rows, 'wide', split_axis=0, concat_axis=0, tiled=True)  345 us
    all_to_all x2, waiting for transfers between devices, exchange(): return lax.all_to_all(rows, 'wide', split_axis=0, concat_axis=0, tiled=True)  119 us
    pallas_call x1, Pallas kernels, edges_backward(): pl.pallas_call(functools.partial(backward_kernel, steps), out_shape=jax.S...  32.4 us
    pallas_call x1, Pallas kernels, edges_forward(): pl.pallas_call(functools.partial(forward_kernel, steps), out_shape=(jax.S...  31.8 us
    pallas_call x2, Pallas kernels, gather_sum(): pl.pallas_call(gather_sum_kernel, out_shape=jax.ShapeDtypeStruct((total,...  20.6 us
    all_to_all x2, starting transfers between devices, exchange(): return lax.all_to_all(rows, 'wide', split_axis=0, concat_axis=0, tiled=True)  17 us
  transfers between devices with their start and end apart: 5, of which 5 were waited for; matrix products, arithmetic and copies ran while one was open for 1% of the time, Pallas kernels for 1%

profile of v1, /device:TPU:0, one launch (start us, length us, event | category | flops | bytes accessed | tf_op | source)
XLA Modules:
  0.0 611.1 jit_solution(15141498504306620879)
XLA Ops:
  0.6 0.8 copy.19
  1.4 0.1 reshape.47.send_ref
  1.5 0.0 copy-start.2
  1.6 1.0 copy-done.2
  2.6 7.5 %select_blocks.1 = bf16[64,256,256]{2,1,0:T(8,128)(2,1)} custom-call(s32[128]{0:T(128)S(1)} %reshape.47.send_ref, bf16[1024,256]{1,0:T(8,128)(2,1)S(1)} %copy-done.2), custom_call_target="tpu_custom_call" | custom-call | tf_op jit(solution)/shard_map/select_blocks/pallas_call | solution.py:81
  10.1 0.0 copy-start.13
  10.1 0.0 copy-start.12
  10.1 0.0 copy-start.11
  10.1 0.0 copy-start.5
  10.1 0.0 copy-start.6
  10.2 11.9 %all-to-all-start = ((bf16[64,256,256]{2,1,0:T(8,128)(2,1)}), bf16[64,256,256]{2,1,0:T(8,128)(2,1)}, u32[]{:S(2)}, u32[]{:S(2)}) async-start(bf16[64,256,256]{2,1,0:T(8,128)(2,1)} %select_blocks.1), calls=%async_computation | async-start | bytes 16777216 | tf_op jit(solution)/shard_map/all_to_all | solution.py:350
  22.1 0.0 copy-done.13
  22.1 0.1 copy.20
  22.2 0.1 reshape.48.recv_ref
  22.3 0.0 copy-done.12
  22.3 1.3 copy.22.scale_ref
  23.7 0.0 copy-done.11
  23.7 0.1 copy.21
  23.9 0.1 select_shift-left_fusion.bit_ref
  24.0 0.0 copy-done.9
  24.0 7.9 %unpack_masks.1 = (bf16[128,128,128]{2,1,0:T(8,128)(2,1)}, bf16[128,128,128]{2,1,0:T(8,128)(2,1)}) custom-call(s32[64]{0:T(128)S(1)} %bitcast.20, s32[128,9,128]{2,1,0:T(8,128)S(1)} %bitcast.18, s32[128,128]{1,0:T(8,128)S(1)} %select_shift-left_fusion.bit_ref), custom_call_target="tpu_custom_call" | custom-call | flops 33554432 | bytes 16777216 | tf_op jit(solution)/shard_map/unpack_masks/pallas_call | solution.py:53
  31.9 102.7 %all-to-all-done.arrived_ref = bf16[64,256,256]{2,1,0:T(8,128)(2,1)} async-done(((bf16[64,256,256]{2,1,0:T(8,128)(2,1)}), bf16[64,256,256]{2,1,0:T(8,128)(2,1)}, u32[]{:S(2)}, u32[]{:S(2)}) %all-to-all-start) | async-done | bytes 8388640 | tf_op jit(solution)/shard_map/all_to_all | solution.py:350
  134.6 0.0 copy-done.5
  134.6 0.0 copy-done.6
  134.6 31.8 %edges_forward.1 = (bf16[64,256,256]{2,1,0:T(8,128)(2,1)}, bf16[2048,256]{1,0:T(8,128)(2,1)S(1)}, bf16[2048,512]{1,0:T(8,128)(2,1)}, f32[2048,512]{1,0:T(8,128)}) custom-call(s32[128]{0:T(128)S(1)} %reshape.48.recv_ref, bf16[64,256,256]{2,1,0:T(8,128)(2,1)} %all-to-all-done.arrived_ref, bf16[128,128,128]{2,1,0:T(8,128)(2,1)} %get-tuple-element.14.mask_t_ref, ...), custom_call_target="tpu_custom_call" | custom-call | tf_op jit(solution)/shard_map/edges_forward/pallas_call | solution.py:211
  166.4 0.0 copy-start.7
  166.4 1.0 copy-done.7
  167.4 122.5 %all_to_all.25.arrived_ref = bf16[64,256,256]{2,1,0:T(8,128)(2,1)} all-to-all(bf16[64,256,256]{2,1,0:T(8,128)(2,1)} %get-tuple-element.16), channel_id=1, replica_groups=mesh['wide'=64,'narrow'=2] {'wide'}, dimensions={0} | all-to-all | bytes 16777216 | tf_op jit(solution)/shard_map/all_to_all | solution.py:350
  289.9 0.0 copy-start.3
  289.9 0.0 copy-start.4
  289.9 0.0 copy-start.8
  289.9 10.2 %node_sums.2.mine_ref = f32[1024,256]{1,0:T(8,128)S(1)} custom-call(s32[128]{0:T(128)S(1)} %reshape.47.send_ref, bf16[64,256,256]{2,1,0:T(8,128)(2,1)} %all_to_all.25.arrived_ref), custom_call_target="tpu_custom_call" | custom-call | tf_op jit(solution)/shard_map/node_sums/pallas_call | solution.py:283
  300.1 0.0 copy-start.1
  300.1 0.1 collective-permute-start
  300.2 2.6 collective-permute-done.other_ref
  302.9 0.0 copy-start.10
  302.9 0.0 copy-done.1
  302.9 1.0 copy-done.10
  303.8 0.0 copy-done.3
  303.8 0.0 copy-done.4
  303.9 0.0 copy-done.8
  303.9 10.8 %norm_and_select.1 = (bf16[1024,256]{1,0:T(8,128)(2,1)}, f32[8,256]{1,0:T(8,128)S(1)}, bf16[64,256,256]{2,1,0:T(8,128)(2,1)}) custom-call(s32[128]{0:T(128)S(1)} %reshape.47.send_ref, f32[1024,256]{1,0:T(8,128)} %copy-done.1, f32[1024,256]{1,0:T(8,128)} %copy-done.10, bf16[1024,256]{1,0:T(8,128)(2,1)S(1)} %copy-done.3, bf16[1024,256]{1,0:T(8,128)(2,1)S(1)} %copy-done.4, ...), custom_call_target="tpu_custom_call" | custom-call | tf_op jit(solution)/shard_map/norm_and_select/pallas_call | solution.py:326
  314.7 0.0 copy-start
  314.7 103.5 %all_to_all.26.arrived_ref = bf16[64,256,256]{2,1,0:T(8,128)(2,1)} all-to-all(bf16[64,256,256]{2,1,0:T(8,128)(2,1)} %get-tuple-element.18), channel_id=1, replica_groups=mesh['wide'=64,'narrow'=2] {'wide'}, dimensions={0} | all-to-all | bytes 16777216 | tf_op jit(solution)/shard_map/all_to_all | solution.py:350
  418.2 0.0 copy-done
  418.2 32.4 %edges_backward.1 = bf16[64,272,256]{2,1,0:T(8,128)(2,1)} custom-call(s32[128]{0:T(128)S(1)} %reshape.48.recv_ref, bf16[64,256,256]{2,1,0:T(8,128)(2,1)} %all_to_all.26.arrived_ref, bf16[128,128,128]{2,1,0:T(8,128)(2,1)} %get-tuple-element.14.mask_t_ref, bf16[128,128,128]{2,1,0:T(8,128)(2,1)} %get-tuple-element.15.mask_ref, f32[2048,1]{1,0:T(8,128)S(1)} %copy-done, ...), custom_call_target="tpu_custom_call" | custom-call | tf_op jit(solution)/shard_map/edges_backward/pallas_call | solution.py:243
  450.5 119.2 %all_to_all.27.arrived_ref = bf16[64,272,256]{2,1,0:T(8,128)(2,1)} all-to-all(bf16[64,272,256]{2,1,0:T(8,128)(2,1)} %edges_backward.1), channel_id=1, replica_groups=mesh['wide'=64,'narrow'=2] {'wide'}, dimensions={0} | all-to-all | bytes 17825792 | tf_op jit(solution)/shard_map/all_to_all | solution.py:350
  569.7 10.4 %node_sums.3 = f32[1040,256]{1,0:T(8,128)S(1)} custom-call(s32[128]{0:T(128)S(1)} %reshape.47.send_ref, bf16[64,272,256]{2,1,0:T(8,128)(2,1)} %all_to_all.27.arrived_ref), custom_call_target="tpu_custom_call" | custom-call | tf_op jit(solution)/shard_map/node_sums/pallas_call | solution.py:283
  580.1 0.1 collective-permute-start.1
  580.2 2.8 collective-permute-done.1
  583.0 1.5 add.19
  584.6 0.9 broadcast_in_dim.14
  585.5 5.0 all-to-all-start.4
  590.6 16.2 %all-to-all-done.4 = f32[64,24,128]{2,1,0:T(8,128)S(1)} async-done(((f32[64,24,128]{2,1,0:T(8,128)}), f32[64,24,128]{2,1,0:T(8,128)S(1)}, u32[]{:S(2)}, u32[]{:S(2)}) %all-to-all-start.4) | async-done | bytes 786464 | tf_op jit(solution)/shard_map/all_to_all | solution.py:350
  606.8 0.1 reshape.53
  606.9 0.1 collective-permute-start.2
  607.0 1.1 slice_add_fusion
  608.1 0.1 slice_reduce_fusion
  608.2 0.6 multiply_bitcast_fusion
  608.8 0.1 collective-permute-done.2
  608.9 0.1 broadcast_select_fusion
  609.0 0.9 fusion.2
  609.9 0.4 copy.24
  610.3 0.8 copy.25
  (10 shorter events, 0.1 us)
Async XLA Ops:
  1.5 1.0 copy-start.2
  10.1 11.9 %copy-start.13 = (s32[1,1,64,2]{2,3,1,0:T(2,128)S(1)}, s32[1,1,64,2]{2,3,1,0:T(2,128)}, u32[]{:S(2)}) copy-start(s32[1,1,64,2]{2,3,1,0:T(2,128)} %param.12) | copy-start | bytes 1540
  10.1 12.2 %copy-start.12 = (s32[2048]{0:T(1024)S(1)}, s32[2048]{0:T(1024)}, u32[]{:S(2)}) copy-start(s32[2048]{0:T(1024)} %param.15) | copy-start | bytes 24580
  10.1 13.6 %copy-start.11 = (s32[1,1,64,2,9,128]{5,3,4,2,1,0:T(2,128)S(1)}, s32[1,1,64,2,9,128]{5,3,4,2,1,0:T(2,128)}, u32[]{:S(2)}) copy-start(s32[1,1,64,2,9,128]{5,3,4,2,1,0:T(2,128)} %param.14) | copy-start | bytes 1769476
  10.1 13.9 %copy-start.9 = (s32[1,1,64]{2,1,0:T(1,128)S(1)}, s32[1,1,64]{2,1,0:T(1,128)}, u32[]{:S(2)}) copy-start(s32[1,1,64]{2,1,0:T(1,128)} %param.13) | copy-start | bytes 772
  10.1 124.5 %copy-start.5 = (bf16[256,512]{1,0:T(8,128)(2,1)S(1)}, bf16[256,512]{1,0:T(8,128)(2,1)}, u32[]{:S(2)}) copy-start(bf16[256,512]{1,0:T(8,128)(2,1)} %w_in_ref.3) | copy-start | bytes 786436
  10.1 124.4 %copy-start.6 = (bf16[512,256]{1,0:T(8,128)(2,1)S(1)}, bf16[512,256]{1,0:T(8,128)(2,1)}, u32[]{:S(2)}) copy-start(bf16[512,256]{1,0:T(8,128)(2,1)} %w_out_ref.3) | copy-start | bytes 786436
  10.2 124.4 %all-to-all-start = ((bf16[64,256,256]{2,1,0:T(8,128)(2,1)}), bf16[64,256,256]{2,1,0:T(8,128)(2,1)}, u32[]{:S(2)}, u32[]{:S(2)}) async-start(bf16[64,256,256]{2,1,0:T(8,128)(2,1)} %select_blocks.1), calls=%async_computation | async-start | bytes 16777216 | tf_op jit(solution)/shard_map/all_to_all | solution.py:350
  166.4 1.0 copy-start.7
  289.9 14.0 %copy-start.3 = (bf16[1024,256]{1,0:T(8,128)(2,1)S(1)}, bf16[1024,256]{1,0:T(8,128)(2,1)}, u32[]{:S(2)}) copy-start(bf16[1024,256]{1,0:T(8,128)(2,1)} %feats_ref.1) | copy-start | bytes 1572868
  289.9 14.0 %copy-start.4 = (bf16[1024,256]{1,0:T(8,128)(2,1)S(1)}, bf16[1024,256]{1,0:T(8,128)(2,1)}, u32[]{:S(2)}) copy-start(bf16[1024,256]{1,0:T(8,128)(2,1)} %cot_ref.1) | copy-start | bytes 1572868
  289.9 14.0 %copy-start.8 = (f32[256]{0:T(256)S(1)}, f32[256]{0:T(256)}, u32[]{:S(2)}) copy-start(f32[256]{0:T(256)} %param.18) | copy-start | bytes 3076
  300.1 2.8 copy-start.1
  300.1 2.7 collective-permute-start
  302.9 1.0 copy-start.10
  314.7 103.5 %copy-start = (f32[2048,1]{1,0:T(8,128)S(1)}, f32[2048,1]{1,0:T(8,128)}, u32[]{:S(2)}) copy-start(f32[2048,1]{1,0:T(8,128)} %copy.22.scale_ref) | copy-start | bytes 24580
  580.1 2.9 collective-permute-start.1
  585.5 21.2 %all-to-all-start.4 = ((f32[64,24,128]{2,1,0:T(8,128)}), f32[64,24,128]{2,1,0:T(8,128)S(1)}, u32[]{:S(2)}, u32[]{:S(2)}) async-start(f32[64,24,128]{2,1,0:T(8,128)} %broadcast_in_dim.14), calls=%async_computation.4 | async-start | bytes 1572864 | tf_op jit(solution)/shard_map/all_to_all | solution.py:350
  606.9 2.0 collective-permute-start.2

commit v2 on v1

v2 whole, which is shorter than its diff:
```python
import functools

import jax
import jax.numpy as jnp
from jax import lax
from jax.experimental import pallas as pl
from jax.experimental.pallas import tpu as pltpu
from jax.sharding import PartitionSpec as P

F32 = jnp.float32
BF16 = jnp.bfloat16
TILE = 128
STEP_OWNERS = 4
PARAMS = pltpu.CompilerParams(vmem_limit_bytes=52 * 1024 * 1024)


SMEM = pl.BlockSpec(memory_space=pltpu.SMEM)
VMEM = pl.BlockSpec(memory_space=pltpu.VMEM)
ANY = pl.BlockSpec(memory_space=pl.ANY)


def dot(a, b, dims=((1,), (0,))):
    return lax.dot_general(a, b, (dims, ((), ())), preferred_element_type=F32)


def rows_at(block):
    return pl.ds(pl.multiple_of(block * TILE, TILE), TILE)


def unpack_kernel(count_ref, words_ref, bit_ref, mask_ref, mask_t_ref):
    step = pl.program_id(0)
    tiles = words_ref.shape[0]
    row = lax.broadcasted_iota(jnp.int32, (8, TILE), 0)
    for tile in range(tiles):
        slot = tile % 2
        live = count_ref[step * (tiles // 2) + tile // 2] > slot
        words = jnp.where(live, words_ref[tile], 0)
        groups = []
        for first in range(0, TILE, 8):
            low, high = first // 15, (first + 7) // 15
            picked = jnp.broadcast_to(words[low : low + 1], (8, TILE))
            if high != low:
                later = jnp.broadcast_to(words[high : high + 1], (8, TILE))
                picked = jnp.where(row + first >= high * 15, later, picked)
            hit = jnp.bitwise_and(picked, bit_ref[first : first + 8]) != 0
            groups.append(jnp.where(hit, 1.0, 0.0).astype(F32))
        mask = jnp.concatenate(groups, axis=0)
        mask_ref[tile] = mask.astype(BF16)
        mask_t_ref[tile] = mask.T.astype(BF16)


def unpack(count, words):
    tiles = words.shape[0]
    per = 8
    bit = jnp.left_shift(1, lax.broadcasted_iota(jnp.int32, (TILE, TILE), 0) % 15)
    out = jax.ShapeDtypeStruct((tiles, TILE, TILE), BF16)
    block = pl.BlockSpec((per, TILE, TILE), lambda i, c: (i, 0, 0))
    return pl.pallas_call(
        unpack_kernel,
        out_shape=(out, out),
        grid_spec=pltpu.PrefetchScalarGridSpec(
            num_scalar_prefetch=1,
            grid=(tiles // per,),
            in_specs=[
                pl.BlockSpec((per,) + words.shape[1:], lambda i, c: (i, 0, 0)),
                pl.BlockSpec((TILE, TILE), lambda i, c: (0, 0)),
            ],
            out_specs=(block, block),
        ),
        compiler_params=PARAMS,
        cost_estimate=pl.CostEstimate(flops=tiles * 2**18, bytes_accessed=tiles * 2**17, transcendentals=0),
        name="unpack_masks",
    )(count, words, bit)


def copy(src, dst, sem):
    return pltpu.make_async_copy(src, dst, sem)


def send_blocks(send_ref, rows_ref, out_ref, sem):
    def body(i, carry):
        copy(rows_ref.at[rows_at(send_ref[i])], out_ref.at[i], sem).start()
        return carry

    lax.fori_loop(0, out_ref.shape[0], body, 0, unroll=8)
    copy(out_ref, out_ref, sem).wait()


def select(send, rows, owners):
    tiles, features = 2 * owners, rows.shape[1]
    out = pl.pallas_call(
        send_blocks,
        out_shape=jax.ShapeDtypeStruct((tiles, TILE, features), BF16),
        in_specs=[SMEM, VMEM],
        out_specs=ANY,
        scratch_shapes=[pltpu.SemaphoreType.DMA],
        compiler_params=PARAMS,
        name="select_blocks",
    )(send, rows)
    return out.reshape(owners, 2 * TILE, features)


def part(ref, i, size):
    return ref.at[pl.ds(i * size, size)]


def start_all(src, dst, sems, size):
    def body(i, carry):
        copy(part(src, i, size), part(dst, i, size), sems.at[i]).start()
        return carry

    lax.fori_loop(0, src.shape[0] // size, body, 0)


def collect(recv_ref, arrived, mask_t, arrived_sems, mask_sems, arrived_ref, mask_t_ref, acc):
    per = 2 * STEP_OWNERS

    def body(i, carry):
        copy(part(arrived_ref, i, STEP_OWNERS), part(arrived, i, STEP_OWNERS), arrived_sems.at[i]).wait()
        copy(part(mask_t_ref, i, per), part(mask_t, i, per), mask_sems.at[i]).wait()
        for tile in range(per):
            where = rows_at(recv_ref[i * per + tile])
            rows = arrived[i * STEP_OWNERS + tile // 2, tile % 2 * TILE : (tile % 2 + 1) * TILE]
            acc[where] += dot(mask_t[i * per + tile], rows)
        return carry

    lax.fori_loop(0, arrived.shape[0] // STEP_OWNERS, body, 0)


def spread(recv_ref, mask, mask_sems, mask_ref, values, made, out_ref, sem, grads=None):
    per = 2 * STEP_OWNERS

    def body(i, carry):
        copy(part(mask_ref, i, per), part(mask, i, per), mask_sems.at[i]).wait()
        for tile in range(per):
            where = rows_at(recv_ref[i * per + tile])
            owner = i * STEP_OWNERS + tile // 2
            made[owner, tile % 2 * TILE : (tile % 2 + 1) * TILE] = dot(mask[i * per + tile], values[where]).astype(BF16)
            if grads is not None and tile % 2:
                extra = made.shape[1] - 2 * TILE
                made[owner, 2 * TILE :] = grads[pl.ds(pl.multiple_of(owner * extra, extra), extra)].astype(BF16)
        copy(part(made, i, STEP_OWNERS), part(out_ref, i, STEP_OWNERS), sem).start()
        return carry

    lax.fori_loop(0, made.shape[0] // STEP_OWNERS, body, 0)


def forward_kernel(
    recv_ref, arrived_ref, mask_t_ref, mask_ref, scale_ref, w_in_ref, w_out_ref,
    out_ref, feats_ref, act_ref, gate_ref,
    arrived, mask_t, mask, made, acc, values, feats, act, gate, sems, out_sems,
):
    per = 2 * STEP_OWNERS
    start_all(arrived_ref, arrived, sems.at[0], STEP_OWNERS)
    start_all(mask_t_ref, mask_t, sems.at[1], per)
    start_all(mask_ref, mask, sems.at[2], per)
    acc[...] = jnp.zeros_like(acc)
    collect(recv_ref, arrived, mask_t, sems.at[0], sems.at[1], arrived_ref, mask_t_ref, acc)
    chunk = 256

    def body(i, carry):
        at = pl.ds(pl.multiple_of(i * chunk, chunk), chunk)
        rows = (acc[at] * scale_ref[at]).astype(BF16)
        feats[at] = rows
        pre = dot(rows, w_in_ref[...])
        sig = jax.nn.sigmoid(pre)
        hidden = (pre * sig).astype(BF16)
        act[at] = hidden
        gate[at] = sig * (1.0 + pre * (1.0 - sig))
        values[at] = dot(hidden, w_out_ref[...]).astype(BF16)
        for k, (mine, out) in enumerate(((feats, feats_ref), (act, act_ref), (gate, gate_ref))):
            copy(mine.at[at], out.at[at], out_sems.at[k]).start()
        return carry

    lax.fori_loop(0, acc.shape[0] // chunk, body, 0)
    spread(recv_ref, mask, sems.at[2], mask_ref, values, made, out_ref, out_sems.at[3])
    for k, (mine, out) in enumerate(((feats, feats_ref), (act, act_ref), (gate, gate_ref), (made, out_ref))):
        copy(mine, out, out_sems.at[k]).wait()


def backward_kernel(
    recv_ref, arrived_ref, mask_t_ref, mask_ref, scale_ref, w_in_ref, w_out_ref,
    feats_ref, act_ref, gate_ref, out_ref,
    arrived, mask_t, mask, made, acc, values, feats, act, gate, grads, sems, in_sems,
):
    width, inner = feats.shape[1], act.shape[1]
    per = 2 * STEP_OWNERS
    start_all(arrived_ref, arrived, sems.at[0], STEP_OWNERS)
    start_all(mask_t_ref, mask_t, sems.at[1], per)
    kept = ((feats_ref, feats), (act_ref, act), (gate_ref, gate))
    for k, (src, dst) in enumerate(kept):
        copy(src, dst, in_sems.at[k]).start()
    start_all(mask_ref, mask, sems.at[2], per)
    acc[...] = jnp.zeros_like(acc)
    grads[...] = jnp.zeros_like(grads)
    collect(recv_ref, arrived, mask_t, sems.at[0], sems.at[1], arrived_ref, mask_t_ref, acc)
    for k, (src, dst) in enumerate(kept):
        copy(src, dst, in_sems.at[k]).wait()
    chunk = 256

    def body(i, carry):
        at = pl.ds(pl.multiple_of(i * chunk, chunk), chunk)
        d_edge = acc[at].astype(BF16)
        d_act = dot(d_edge, w_out_ref[...], ((1,), (1,)))
        d_pre = (d_act * gate[at]).astype(BF16)
        values[at] = (dot(d_pre, w_in_ref[...], ((1,), (1,))) * scale_ref[at]).astype(BF16)
        grads[:inner] += dot(act[at], d_edge, ((0,), (0,)))
        in_part = dot(feats[at], d_pre, ((0,), (0,)))
        for piece in range(inner // width):
            first = inner + piece * width
            grads[first : first + width] += in_part[:, piece * width : (piece + 1) * width]
        return carry

    lax.fori_loop(0, acc.shape[0] // chunk, body, 0)
    spread(recv_ref, mask, sems.at[2], mask_ref, values, made, out_ref, in_sems.at[3], grads)
    copy(made, out_ref, in_sems.at[3]).wait()


def edge_scratch(owners, rows, edges, width, inner):
    tiles = 2 * owners
    steps = owners // STEP_OWNERS
    return [
        pltpu.VMEM((owners, 2 * TILE, width), BF16),
        pltpu.VMEM((tiles, TILE, TILE), BF16),
        pltpu.VMEM((tiles, TILE, TILE), BF16),
        pltpu.VMEM((owners, rows, width), BF16),
        pltpu.VMEM((edges, width), F32),
        pltpu.VMEM((edges, width), BF16),
        pltpu.VMEM((edges, width), BF16),
        pltpu.VMEM((edges, inner), BF16),
        pltpu.VMEM((edges, inner), F32),
    ], [pltpu.SemaphoreType.DMA((3, steps)), pltpu.SemaphoreType.DMA((4,))]


def edges_forward(recv, arrived, mask_t, mask, scale, w_in, w_out):
    owners = arrived.shape[0]
    edges, width, inner = scale.shape[0], w_in.shape[0], w_in.shape[1]
    buffers, sems = edge_scratch(owners, 2 * TILE, edges, width, inner)
    return pl.pallas_call(
        forward_kernel,
        out_shape=(
            jax.ShapeDtypeStruct((owners, 2 * TILE, width), BF16),
            jax.ShapeDtypeStruct((edges, width), BF16),
            jax.ShapeDtypeStruct((edges, inner), BF16),
            jax.ShapeDtypeStruct((edges, inner), F32),
        ),
        in_specs=[SMEM, ANY, ANY, ANY, VMEM, VMEM, VMEM],
        out_specs=(ANY,) * 4,
        scratch_shapes=buffers + sems,
        compiler_params=PARAMS,
        name="edges_forward",
    )(recv, arrived, mask_t, mask, scale, w_in, w_out)


def edges_backward(recv, arrived, mask_t, mask, scale, w_in, w_out, feats, act, gate):
    owners = arrived.shape[0]
    edges, width, inner = scale.shape[0], w_in.shape[0], w_in.shape[1]
    grad_rows = 2 * inner
    extra = grad_rows // owners
    buffers, sems = edge_scratch(owners, 2 * TILE + extra, edges, width, inner)
    return pl.pallas_call(
        backward_kernel,
        out_shape=jax.ShapeDtypeStruct((owners, 2 * TILE + extra, width), BF16),
        in_specs=[SMEM, ANY, ANY, ANY, VMEM, VMEM, VMEM, ANY, ANY, ANY],
        out_specs=ANY,
        scratch_shapes=buffers + [pltpu.VMEM((grad_rows, width), F32)] + sems,
        compiler_params=PARAMS,
        name="edges_backward",
    )(recv, arrived, mask_t, mask, scale, w_in, w_out, feats, act, gate)


def gather_sum_kernel(send_ref, arrived_ref, out_ref, arrived, sems):
    per = 2 * STEP_OWNERS
    blocks = arrived_ref.at[:, pl.ds(0, 2 * TILE)]
    start_all(blocks, arrived, sems, STEP_OWNERS)
    out_ref[...] = jnp.zeros_like(out_ref)

    def body(i, carry):
        copy(part(blocks, i, STEP_OWNERS), part(arrived, i, STEP_OWNERS), sems.at[i]).wait()
        for tile in range(per):
            where = rows_at(send_ref[i * per + tile])
            rows = arrived[i * STEP_OWNERS + tile // 2, tile % 2 * TILE : (tile % 2 + 1) * TILE]
            out_ref[where] += rows.astype(F32)
        return carry

    lax.fori_loop(0, arrived.shape[0] // STEP_OWNERS, body, 0)


def gather_sum(send, arrived, nodes):
    owners, _, width = arrived.shape
    return pl.pallas_call(
        gather_sum_kernel,
        out_shape=jax.ShapeDtypeStruct((nodes, width), F32),
        in_specs=[SMEM, ANY],
        out_specs=VMEM,
        scratch_shapes=[
            pltpu.VMEM((owners, 2 * TILE, width), BF16),
            pltpu.SemaphoreType.DMA((owners // STEP_OWNERS,)),
        ],
        compiler_params=PARAMS,
        name="node_sums",
    )(send, arrived)


def tail_sum_kernel(arrived_ref, out_ref, tails, sem):
    move = copy(arrived_ref.at[:, pl.ds(2 * TILE, tails.shape[1])], tails, sem)
    move.start()
    move.wait()
    out_ref[...] = jnp.sum(tails[...].astype(F32), axis=0)


def tail_sum(arrived):
    owners, rows, width = arrived.shape
    extra = rows - 2 * TILE
    return pl.pallas_call(
        tail_sum_kernel,
        out_shape=jax.ShapeDtypeStruct((extra, width), F32),
        in_specs=[ANY],
        out_specs=VMEM,
        scratch_shapes=[pltpu.VMEM((owners, extra, width), BF16), pltpu.SemaphoreType.DMA],
        compiler_params=PARAMS,
        name="weight_sums",
    )(arrived)


def norm_kernel(
    send_ref, mine_ref, other_ref, feats_ref, cot_ref, gain_ref, updated_ref, part_ref, out_ref, d_summed, sem
):
    gain = gain_ref[...]

    def body(i, part):
        at = rows_at(i)
        summed = mine_ref[at] + other_ref[at]
        inv_rms = lax.rsqrt(jnp.mean(summed * summed, axis=-1, keepdims=True) + 1e-05)
        normed = summed * inv_rms
        updated_ref[at] = (feats_ref[at].astype(F32) + normed * gain).astype(BF16)
        upstream = cot_ref[at].astype(F32)
        d_normed = upstream * gain
        inner = jnp.mean(d_normed * normed, axis=-1, keepdims=True)
        d_summed[at] = (inv_rms * (d_normed - normed * inner)).astype(BF16)
        return part + jnp.sum((upstream * normed).reshape(TILE // 8, 8, -1), axis=0)

    part_ref[...] = lax.fori_loop(0, mine_ref.shape[0] // TILE, body, jnp.zeros_like(part_ref))
    send_blocks(send_ref, d_summed, out_ref, sem)


def norm_and_select(send, mine, other, feats, cot, gain, owners):
    nodes, width = feats.shape
    updated, gain_part, out = pl.pallas_call(
        norm_kernel,
        out_shape=(
            jax.ShapeDtypeStruct((nodes, width), BF16),
            jax.ShapeDtypeStruct((8, width), F32),
            jax.ShapeDtypeStruct((2 * owners, TILE, width), BF16),
        ),
        in_specs=[SMEM] + [VMEM] * 5,
        out_specs=(VMEM, VMEM, ANY),
        scratch_shapes=[pltpu.VMEM((nodes, width), BF16), pltpu.SemaphoreType.DMA],
        compiler_params=PARAMS,
        name="norm_and_select",
    )(send, mine, other, feats, cot, gain)
    return updated, gain_part, out.reshape(owners, 2 * TILE, width)


def exchange(rows):
    return lax.all_to_all(rows, "wide", split_axis=0, concat_axis=0, tiled=True)


def swap(rows):
    return lax.ppermute(rows, "narrow", [(0, 1), (1, 0)])


def shards(
    node_feats,
    send_block,
    recv_block,
    tile_count,
    mask_bits,
    degree,
    weight_in,
    weight_out,
    norm_gain,
    cotangent,
):
    owners = lax.axis_size("wide")
    nodes, width = node_feats.shape
    inner = weight_in.shape[1]
    send = send_block.reshape(-1)
    recv = recv_block.reshape(-1)
    count = tile_count.reshape(-1)
    words = mask_bits.reshape((-1,) + mask_bits.shape[4:])
    scale = lax.rsqrt(degree.astype(F32))[:, None]
    gain = norm_gain[None, :]

    mask, mask_t = unpack(count, words)
    arrived = exchange(select(send, node_feats, owners))
    products, feats, act, gate = edges_forward(recv, arrived, mask_t, mask, scale, weight_in, weight_out)
    mine = gather_sum(send, exchange(products), nodes)
    updated, gain_part, picked = norm_and_select(send, mine, swap(mine), node_feats, cotangent, gain, owners)
    products = edges_backward(
        recv, exchange(picked), mask_t, mask, scale, weight_in, weight_out, feats, act, gate
    )
    arrived = exchange(products)
    weight_sums = tail_sum(arrived)
    weight_sums = weight_sums + swap(weight_sums)
    core = lax.axis_index("narrow")
    extra = weight_sums.shape[0]
    half = lax.dynamic_slice_in_dim(weight_sums, core * (extra // 2), extra // 2, 0)
    chunk = jnp.concatenate([half.reshape(extra, width // 2), gain_part.sum(0).reshape(-1, width // 2)], 0)
    chunk = jnp.pad(chunk, ((0, -chunk.shape[0] % 8), (0, 0)))
    everyone = exchange(jnp.broadcast_to(chunk[None], (owners,) + chunk.shape))
    mine = gather_sum(send, arrived, nodes)
    grad_nodes = cotangent.astype(F32) + (mine + swap(mine))

    grad_gain = everyone[:, extra : extra + 2].sum(0).reshape(width)
    halves = everyone[:, :extra].reshape(owners, extra // 2, width)
    theirs = swap(halves)
    lower = jnp.where(core == 0, halves, theirs)
    upper = jnp.where(core == 0, theirs, halves)
    grads = jnp.concatenate([lower, upper], 1).reshape(2 * inner, width)
    pieces = inner // width
    grad_out = grads[:inner]
    grad_in = grads[inner:].reshape(pieces, width, width).transpose(1, 0, 2).reshape(width, inner)

    edge_factor = (degree.shape[0] * owners * lax.axis_size("narrow")) ** (-0.5)
    return (
        updated,
        grad_nodes,
        grad_in * edge_factor,
        grad_out * edge_factor,
        grad_gain * (nodes * owners) ** (-0.5),
    )


def solution(mesh):
    return jax.shard_map(
        shards,
        mesh=mesh,
        in_specs=(
            P("wide", None),
            P("wide", None, "narrow", None),
            P("wide", "narrow", None, None),
            P("wide", "narrow", None),
            P("wide", "narrow", None, None, None, None),
            P(("wide", "narrow")),
            P(),
            P(),
            P(),
            P("wide", None),
        ),
        out_specs=(P("wide", None), P("wide", None), P(), P(), P()),
        check_vma=False,
    )
```

time: 614 us -> 564 us (0.919)
  Pallas kernels: 111 us -> 68.1 us
    pallas_call x5 -> x6, Pallas kernels: 92.4 us -> 52.9 us  [the longest x1 20.5 us: edges_forward(): pl.pallas_call(forward_kernel, out_shape=(jax.ShapeDtypeStruct((owners, 2...]
  transfers between devices with their start and end apart: 5 -> 6, of which waited for: 5 -> 4; matrix products, arithmetic and copies ran while one was open for 1% -> 1% of each run, Pallas kernels for 1% -> 2%
where the time goes in v2:
time: 564 us; the launch traced here: 562 us
  blocking collectives  345 us (61%)
  waiting for transfers between devices  118 us (21%)
  Pallas kernels  68.1 us (12%)
  starting transfers between devices  17.3 us (3%)
  local copies, waits for them, and re-layouts  8.03 us (1%)
    all_to_all x3, blocking collectives, exchange(): return lax.all_to_all(rows, 'wide', split_axis=0, concat_axis=0, tiled=True)  345 us
    all_to_all x2, waiting for transfers between devices, exchange(): return lax.all_to_all(rows, 'wide', split_axis=0, concat_axis=0, tiled=True)  115 us
    pallas_call x1, Pallas kernels, edges_forward(): pl.pallas_call(forward_kernel, out_shape=(jax.ShapeDtypeStruct((owners, 2...  20.5 us
    pallas_call x1, Pallas kernels, edges_backward(): pl.pallas_call(backward_kernel, out_shape=jax.ShapeDtypeStruct((owners, 2...  19 us
    all_to_all x2, starting transfers between devices, exchange(): return lax.all_to_all(rows, 'wide', split_axis=0, concat_axis=0, tiled=True)  17 us
  transfers between devices with their start and end apart: 6, of which 4 were waited for; matrix products, arithmetic and copies ran while one was open for 1% of the time, Pallas kernels for 2%

profile of v2, /device:TPU:0, one launch (start us, length us, event | category | flops | bytes accessed | tf_op | source)
XLA Modules:
  0.0 562.0 jit_solution(15345149835811352944)
XLA Ops:
  0.6 0.8 copy.19
  1.4 0.1 reshape.53.send_ref
  1.5 0.0 copy-start.2
  1.6 1.0 copy-done.2
  2.6 3.8 select_blocks.1
  6.4 0.0 copy-start.13
  6.4 0.0 copy-start.12
  6.4 0.0 copy-start.11
  6.4 0.0 copy-start.9
  6.4 0.0 copy-start.5
  6.4 0.0 copy-start.6
  6.4 11.9 %all-to-all-start = ((bf16[64,256,256]{2,1,0:T(8,128)(2,1)}), bf16[64,256,256]{2,1,0:T(8,128)(2,1)}, u32[]{:S(2)}, u32[]{:S(2)}) async-start(bf16[64,256,256]{2,1,0:T(8,128)(2,1)} %bitcast.23), calls=%async_computation | async-start | bytes 16777216 | tf_op jit(solution)/shard_map/all_to_all | solution.py:366
  18.4 0.0 copy-done.13
  18.4 0.1 copy.20
  18.5 0.1 reshape.54.recv_ref
  18.6 0.0 copy-done.12
  18.6 1.3 copy.22.scale_ref
  20.0 0.0 copy-done.11
  20.0 0.1 copy.21
  20.1 0.1 select_shift-left_fusion.bit_ref
  20.3 0.0 copy-done.9
  20.3 7.9 %unpack_masks.1 = (bf16[128,128,128]{2,1,0:T(8,128)(2,1)}, bf16[128,128,128]{2,1,0:T(8,128)(2,1)}) custom-call(s32[64]{0:T(128)S(1)} %bitcast.22, s32[128,9,128]{2,1,0:T(8,128)S(1)} %bitcast.20, s32[128,128]{1,0:T(8,128)S(1)} %select_shift-left_fusion.bit_ref), custom_call_target="tpu_custom_call" | custom-call | flops 33554432 | bytes 16777216 | tf_op jit(solution)/shard_map/unpack_masks/pallas_call | solution.py:58
  28.2 102.7 %all-to-all-done.arrived_ref = bf16[64,256,256]{2,1,0:T(8,128)(2,1)} async-done(((bf16[64,256,256]{2,1,0:T(8,128)(2,1)}), bf16[64,256,256]{2,1,0:T(8,128)(2,1)}, u32[]{:S(2)}, u32[]{:S(2)}) %all-to-all-start) | async-done | bytes 8388640 | tf_op jit(solution)/shard_map/all_to_all | solution.py:366
  130.9 0.0 copy-done.5
  130.9 0.0 copy-done.6
  130.9 20.5 %edges_forward.1 = (bf16[64,256,256]{2,1,0:T(8,128)(2,1)}, bf16[2048,256]{1,0:T(8,128)(2,1)S(1)}, bf16[2048,512]{1,0:T(8,128)(2,1)}, f32[2048,512]{1,0:T(8,128)}) custom-call(s32[128]{0:T(128)S(1)} %reshape.54.recv_ref, bf16[64,256,256]{2,1,0:T(8,128)(2,1)} %all-to-all-done.arrived_ref, bf16[128,128,128]{2,1,0:T(8,128)(2,1)} %get-tuple-element.14.mask_t_ref, ...), custom_call_target="tpu_custom_call" | custom-call | tf_op jit(solution)/shard_map/edges_forward/pallas_call | solution.py:239
  151.4 0.0 copy-start.7
  151.4 1.0 copy-done.7
  152.4 122.5 %all_to_all.25.arrived_ref = bf16[64,256,256]{2,1,0:T(8,128)(2,1)} all-to-all(bf16[64,256,256]{2,1,0:T(8,128)(2,1)} %get-tuple-element.16), channel_id=1, replica_groups=mesh['wide'=64,'narrow'=2] {'wide'}, dimensions={0} | all-to-all | bytes 16777216 | tf_op jit(solution)/shard_map/all_to_all | solution.py:366
  274.9 0.0 copy-start.3
  274.9 4.2 node_sums.2.mine_ref
  279.1 0.0 copy-start.1
  279.1 0.1 collective-permute-start
  279.2 2.6 collective-permute-done.other_ref
  281.8 0.0 copy-done.1
  281.8 1.0 copy-done.10
  282.8 0.0 copy-done.3
  282.8 0.0 copy-done.4
  282.8 0.0 copy-done.8
  282.8 7.3 %norm_and_select.1 = (bf16[1024,256]{1,0:T(8,128)(2,1)}, f32[8,256]{1,0:T(8,128)S(1)}, bf16[128,128,256]{2,1,0:T(8,128)(2,1)}) custom-call(s32[128]{0:T(128)S(1)} %reshape.53.send_ref, f32[1024,256]{1,0:T(8,128)} %copy-done.1, f32[1024,256]{1,0:T(8,128)} %copy-done.10, bf16[1024,256]{1,0:T(8,128)(2,1)S(1)} %copy-done.3, bf16[1024,256]{1,0:T(8,128)(2,1)S(1)} %copy-done.4, ...), custom_call_target="tpu_custom_call" | custom-call | tf_op jit(solution)/shard_map/norm_and_select/pallas_call | solution.py:349
  290.1 0.0 copy-start
  290.1 103.5 %all_to_all.26.arrived_ref = bf16[64,256,256]{2,1,0:T(8,128)(2,1)} all-to-all(bf16[64,256,256]{2,1,0:T(8,128)(2,1)} %bitcast.24), channel_id=1, replica_groups=mesh['wide'=64,'narrow'=2] {'wide'}, dimensions={0} | all-to-all | bytes 16777216 | tf_op jit(solution)/shard_map/all_to_all | solution.py:366
  393.6 0.0 copy-done
  393.6 19.0 %edges_backward.1 = bf16[64,272,256]{2,1,0:T(8,128)(2,1)} custom-call(s32[128]{0:T(128)S(1)} %reshape.54.recv_ref, bf16[64,256,256]{2,1,0:T(8,128)(2,1)} %all_to_all.26.arrived_ref, bf16[128,128,128]{2,1,0:T(8,128)(2,1)} %get-tuple-element.14.mask_t_ref, bf16[128,128,128]{2,1,0:T(8,128)(2,1)} %get-tuple-element.15.mask_ref, f32[2048,1]{1,0:T(8,128)S(1)} %copy-done, ...), custom_call_target="tpu_custom_call" | custom-call | tf_op jit(solution)/shard_map/edges_backward/pallas_call | solution.py:261
  412.7 119.1 %all_to_all.27.arrived_ref = bf16[64,272,256]{2,1,0:T(8,128)(2,1)} all-to-all(bf16[64,272,256]{2,1,0:T(8,128)(2,1)} %edges_backward.1), channel_id=1, replica_groups=mesh['wide'=64,'narrow'=2] {'wide'}, dimensions={0} | all-to-all | bytes 17825792 | tf_op jit(solution)/shard_map/all_to_all | solution.py:366
  531.8 1.2 weight_sums.1
  533.0 0.1 collective-permute-start.2
  533.1 1.1 collective-permute-done.2
  534.3 0.9 broadcast_in_dim.14
  535.2 5.0 all-to-all-start.4
  540.2 4.2 node_sums.3
  544.4 0.1 collective-permute-start.1
  544.5 11.9 %all-to-all-done.4 = f32[64,24,128]{2,1,0:T(8,128)S(1)} async-done(((f32[64,24,128]{2,1,0:T(8,128)}), f32[64,24,128]{2,1,0:T(8,128)S(1)}, u32[]{:S(2)}, u32[]{:S(2)}) %all-to-all-start.4) | async-done | bytes 786464 | tf_op jit(solution)/shard_map/all_to_all | solution.py:366
  556.5 0.1 reshape.61
  556.6 0.1 collective-permute-start.3
  556.7 0.1 slice_reduce_fusion
  556.8 0.6 multiply_bitcast_fusion
  557.4 0.0 collective-permute-done.1
  557.4 2.5 add_add_fusion
  559.8 0.0 collective-permute-done.3
  559.8 0.1 broadcast_select_fusion
  559.9 0.9 fusion.2
  560.8 0.4 copy.24
  561.2 0.8 copy.25
  (11 shorter events, 0.1 us)
Async XLA Ops:
  1.5 1.0 copy-start.2
  6.4 12.0 %copy-start.13 = (s32[1,1,64,2]{2,3,1,0:T(2,128)S(1)}, s32[1,1,64,2]{2,3,1,0:T(2,128)}, u32[]{:S(2)}) copy-start(s32[1,1,64,2]{2,3,1,0:T(2,128)} %param.12) | copy-start | bytes 1540
  6.4 12.2 %copy-start.12 = (s32[2048]{0:T(1024)S(1)}, s32[2048]{0:T(1024)}, u32[]{:S(2)}) copy-start(s32[2048]{0:T(1024)} %param.15) | copy-start | bytes 24580
  6.4 13.6 %copy-start.11 = (s32[1,1,64,2,9,128]{5,3,4,2,1,0:T(2,128)S(1)}, s32[1,1,64,2,9,128]{5,3,4,2,1,0:T(2,128)}, u32[]{:S(2)}) copy-start(s32[1,1,64,2,9,128]{5,3,4,2,1,0:T(2,128)} %param.14) | copy-start | bytes 1769476
  6.4 13.9 %copy-start.9 = (s32[1,1,64]{2,1,0:T(1,128)S(1)}, s32[1,1,64]{2,1,0:T(1,128)}, u32[]{:S(2)}) copy-start(s32[1,1,64]{2,1,0:T(1,128)} %param.13) | copy-start | bytes 772
  6.4 124.5 %copy-start.5 = (bf16[256,512]{1,0:T(8,128)(2,1)S(1)}, bf16[256,512]{1,0:T(8,128)(2,1)}, u32[]{:S(2)}) copy-start(bf16[256,512]{1,0:T(8,128)(2,1)} %w_in_ref.3) | copy-start | bytes 786436
  6.4 124.4 %copy-start.6 = (bf16[512,256]{1,0:T(8,128)(2,1)S(1)}, bf16[512,256]{1,0:T(8,128)(2,1)}, u32[]{:S(2)}) copy-start(bf16[512,256]{1,0:T(8,128)(2,1)} %w_out_ref.3) | copy-start | bytes 786436
  6.4 124.4 %all-to-all-start = ((bf16[64,256,256]{2,1,0:T(8,128)(2,1)}), bf16[64,256,256]{2,1,0:T(8,128)(2,1)}, u32[]{:S(2)}, u32[]{:S(2)}) async-start(bf16[64,256,256]{2,1,0:T(8,128)(2,1)} %bitcast.23), calls=%async_computation | async-start | bytes 16777216 | tf_op jit(solution)/shard_map/all_to_all | solution.py:366
  151.4 1.0 copy-start.7
  274.9 7.9 %copy-start.3 = (bf16[1024,256]{1,0:T(8,128)(2,1)S(1)}, bf16[1024,256]{1,0:T(8,128)(2,1)}, u32[]{:S(2)}) copy-start(bf16[1024,256]{1,0:T(8,128)(2,1)} %feats_ref.1) | copy-start | bytes 1572868
  274.9 7.9 %copy-start.4 = (bf16[1024,256]{1,0:T(8,128)(2,1)S(1)}, bf16[1024,256]{1,0:T(8,128)(2,1)}, u32[]{:S(2)}) copy-start(bf16[1024,256]{1,0:T(8,128)(2,1)} %cot_ref.1) | copy-start | bytes 1572868
  274.9 7.9 %copy-start.8 = (f32[256]{0:T(256)S(1)}, f32[256]{0:T(256)}, u32[]{:S(2)}) copy-start(f32[256]{0:T(256)} %param.18) | copy-start | bytes 3076
  279.1 2.8 copy-start.1
  279.1 2.7 collective-permute-start
  281.8 1.0 copy-start.10
  290.1 103.5 %copy-start = (f32[2048,1]{1,0:T(8,128)S(1)}, f32[2048,1]{1,0:T(8,128)}, u32[]{:S(2)}) copy-start(f32[2048,1]{1,0:T(8,128)} %copy.22.scale_ref) | copy-start | bytes 24580
  533.0 1.3 collective-permute-start.2
  535.2 21.2 %all-to-all-start.4 = ((f32[64,24,128]{2,1,0:T(8,128)}), f32[64,24,128]{2,1,0:T(8,128)S(1)}, u32[]{:S(2)}, u32[]{:S(2)}) async-start(f32[64,24,128]{2,1,0:T(8,128)} %broadcast_in_dim.14), calls=%async_computation.4 | async-start | bytes 1572864 | tf_op jit(solution)/shard_map/all_to_all | solution.py:366
  544.4 12.9 %collective-permute-start.1 = (f32[1024,256]{1,0:T(8,128)S(1)}, f32[1024,256]{1,0:T(8,128)}, u32[]{:S(2)}, u32[]{:S(2)}) collective-permute-start(f32[1024,256]{1,0:T(8,128)S(1)} %node_sums.3), channel_id=1, source_target_pairs={{0,1},{1,0},{2,3},{3,2},{4,5},{5,4},{6,7},{7,6},{8,9},{9,8},{10,11... | collective-permute-start | bytes 3145736 | tf_op jit(solution)/shard_map/ppermute | solution.py:370
  556.6 3.2 collective-permute-start.3

commit v3 on v2

--- a/solution.py
+++ b/solution.py
@@ -127,7 +127,7 @@
     lax.fori_loop(0, arrived.shape[0] // STEP_OWNERS, body, 0)
 
 
-def spread(recv_ref, mask, mask_sems, mask_ref, values, made, out_ref, sem, grads=None):
+def spread(recv_ref, mask, mask_sems, mask_ref, values, made, out_ref, sem):
     per = 2 * STEP_OWNERS
 
     def body(i, carry):
@@ -136,9 +136,6 @@
             where = rows_at(recv_ref[i * per + tile])
             owner = i * STEP_OWNERS + tile // 2
             made[owner, tile % 2 * TILE : (tile % 2 + 1) * TILE] = dot(mask[i * per + tile], values[where]).astype(BF16)
-            if grads is not None and tile % 2:
-                extra = made.shape[1] - 2 * TILE
-                made[owner, 2 * TILE :] = grads[pl.ds(pl.multiple_of(owner * extra, extra), extra)].astype(BF16)
         copy(part(made, i, STEP_OWNERS), part(out_ref, i, STEP_OWNERS), sem).start()
         return carry
 
@@ -180,8 +177,8 @@
 
 def backward_kernel(
     recv_ref, arrived_ref, mask_t_ref, mask_ref, scale_ref, w_in_ref, w_out_ref,
-    feats_ref, act_ref, gate_ref, out_ref,
-    arrived, mask_t, mask, made, acc, values, feats, act, gate, grads, sems, in_sems,
+    feats_ref, act_ref, gate_ref, out_ref, grads,
+    arrived, mask_t, mask, made, acc, values, feats, act, gate, sems, in_sems,
 ):
     width, inner = feats.shape[1], act.shape[1]
     per = 2 * STEP_OWNERS
@@ -212,18 +209,18 @@
         return carry
 
     lax.fori_loop(0, acc.shape[0] // chunk, body, 0)
-    spread(recv_ref, mask, sems.at[2], mask_ref, values, made, out_ref, in_sems.at[3], grads)
+    spread(recv_ref, mask, sems.at[2], mask_ref, values, made, out_ref, in_sems.at[3])
     copy(made, out_ref, in_sems.at[3]).wait()
 
 
-def edge_scratch(owners, rows, edges, width, inner):
+def edge_scratch(owners, edges, width, inner):
     tiles = 2 * owners
     steps = owners // STEP_OWNERS
     return [
         pltpu.VMEM((owners, 2 * TILE, width), BF16),
         pltpu.VMEM((tiles, TILE, TILE), BF16),
         pltpu.VMEM((tiles, TILE, TILE), BF16),
-        pltpu.VMEM((owners, rows, width), BF16),
+        pltpu.VMEM((owners, 2 * TILE, width), BF16),
         pltpu.VMEM((edges, width), F32),
         pltpu.VMEM((edges, width), BF16),
         pltpu.VMEM((edges, width), BF16),
@@ -235,7 +232,7 @@
 def edges_forward(recv, arrived, mask_t, mask, scale, w_in, w_out):
     owners = arrived.shape[0]
     edges, width, inner = scale.shape[0], w_in.shape[0], w_in.shape[1]
-    buffers, sems = edge_scratch(owners, 2 * TILE, edges, width, inner)
+    buffers, sems = edge_scratch(owners, edges, width, inner)
     return pl.pallas_call(
         forward_kernel,
         out_shape=(
@@ -255,15 +252,16 @@
 def edges_backward(recv, arrived, mask_t, mask, scale, w_in, w_out, feats, act, gate):
     owners = arrived.shape[0]
     edges, width, inner = scale.shape[0], w_in.shape[0], w_in.shape[1]
-    grad_rows = 2 * inner
-    extra = grad_rows // owners
-    buffers, sems = edge_scratch(owners, 2 * TILE + extra, edges, width, inner)
+    buffers, sems = edge_scratch(owners, edges, width, inner)
     return pl.pallas_call(
         backward_kernel,
-        out_shape=jax.ShapeDtypeStruct((owners, 2 * TILE + extra, width), BF16),
+        out_shape=(
+            jax.ShapeDtypeStruct((owners, 2 * TILE, width), BF16),
+            jax.ShapeDtypeStruct((2 * inner, width), F32),
+        ),
         in_specs=[SMEM, ANY, ANY, ANY, VMEM, VMEM, VMEM, ANY, ANY, ANY],
-        out_specs=ANY,
-        scratch_shapes=buffers + [pltpu.VMEM((grad_rows, width), F32)] + sems,
+        out_specs=(ANY, VMEM),
+        scratch_shapes=buffers + sems,
         compiler_params=PARAMS,
         name="edges_backward",
     )(recv, arrived, mask_t, mask, scale, w_in, w_out, feats, act, gate)
@@ -271,12 +269,11 @@
 
 def gather_sum_kernel(send_ref, arrived_ref, out_ref, arrived, sems):
     per = 2 * STEP_OWNERS
-    blocks = arrived_ref.at[:, pl.ds(0, 2 * TILE)]
-    start_all(blocks, arrived, sems, STEP_OWNERS)
+    start_all(arrived_ref, arrived, sems, STEP_OWNERS)
     out_ref[...] = jnp.zeros_like(out_ref)
 
     def body(i, carry):
-        copy(part(blocks, i, STEP_OWNERS), part(arrived, i, STEP_OWNERS), sems.at[i]).wait()
+        copy(part(arrived_ref, i, STEP_OWNERS), part(arrived, i, STEP_OWNERS), sems.at[i]).wait()
         for tile in range(per):
             where = rows_at(send_ref[i * per + tile])
             rows = arrived[i * STEP_OWNERS + tile // 2, tile % 2 * TILE : (tile % 2 + 1) * TILE]
@@ -300,27 +297,6 @@
         compiler_params=PARAMS,
         name="node_sums",
     )(send, arrived)
-
-
-def tail_sum_kernel(arrived_ref, out_ref, tails, sem):
-    move = copy(arrived_ref.at[:, pl.ds(2 * TILE, tails.shape[1])], tails, sem)
-    move.start()
-    move.wait()
-    out_ref[...] = jnp.sum(tails[...].astype(F32), axis=0)
-
-
-def tail_sum(arrived):
-    owners, rows, width = arrived.shape
-    extra = rows - 2 * TILE
-    return pl.pallas_call(
-        tail_sum_kernel,
-        out_shape=jax.ShapeDtypeStruct((extra, width), F32),
-        in_specs=[ANY],
-        out_specs=VMEM,
-        scratch_shapes=[pltpu.VMEM((owners, extra, width), BF16), pltpu.SemaphoreType.DMA],
-        compiler_params=PARAMS,
-        name="weight_sums",
-    )(arrived)
 
 
 def norm_kernel(
@@ -363,11 +339,70 @@
 
 
 def exchange(rows):
-    return lax.all_to_all(rows, "wide", split_axis=0, concat_axis=0, tiled=True)
+    owners, width = rows.shape[0], rows.shape[2]
+    tiles = rows.reshape(2 * owners, TILE, width)
+    moved = lax.all_to_all(tiles, ("wide", "narrow"), split_axis=0, concat_axis=0, tiled=True)
+    return moved.reshape(owners, 2 * TILE, width)
 
 
 def swap(rows):
     return lax.ppermute(rows, "narrow", [(0, 1), (1, 0)])
+
+
+def ring_sends(values, stride, side):
+    owners = lax.axis_size("wide")
+    moved = []
+    for offset in range(1, side):
+        pairs = []
+        for w in range(owners):
+            place = w // stride % side
+            pairs.append((w, w + ((place + offset) % side - place) * stride))
+        moved.append(lax.ppermute(values[offset - 1], "wide", pairs))
+    return moved
+
+
+def axes_of(owners):
+    side = 4
+    strides = []
+    stride = owners // side
+    while stride >= 1:
+        strides.append(stride)
+        stride //= side
+    return side, strides
+
+
+def reduce_over_chips(rows):
+    core = lax.axis_index("narrow")
+    wide = lax.axis_index("wide")
+    side, strides = axes_of(lax.axis_size("wide"))
+    half = rows.shape[0] // 2
+    theirs = swap(lax.dynamic_slice_in_dim(rows, (1 - core) * half, half, 0))
+    held = lax.dynamic_slice_in_dim(rows, core * half, half, 0) + theirs
+    for stride in strides:
+        place = wide // stride % side
+        pieces = held.reshape((side, -1) + held.shape[1:])
+        pick = lambda o: lax.dynamic_index_in_dim(pieces, (place + o) % side, 0, keepdims=False)
+        moved = ring_sends([pick(o) for o in range(1, side)], stride, side)
+        held = pick(0) + moved[0] + moved[1] + moved[2]
+    for stride in reversed(strides):
+        held = in_order([held] + ring_sends([held] * (side - 1), stride, side), wide // stride % side)
+        held = held.reshape((-1,) + held.shape[2:])
+    other = swap(held)
+    first, second = jnp.where(core == 0, held, other), jnp.where(core == 0, other, held)
+    return jnp.concatenate([first, second], 0)
+
+
+def in_order(pieces, place):
+    side = len(pieces)
+    return jnp.take(jnp.stack(pieces), (place - jnp.arange(side)) % side, axis=0)
+
+
+def sum_over_wide(row):
+    wide = lax.axis_index("wide")
+    side, strides = axes_of(lax.axis_size("wide"))
+    for stride in strides:
+        row = in_order([row] + ring_sends([row] * (side - 1), stride, side), wide // stride % side).sum(0)
+    return row
 
 
 def shards(
@@ -385,7 +420,11 @@
     owners = lax.axis_size("wide")
     nodes, width = node_feats.shape
     inner = weight_in.shape[1]
-    send = send_block.reshape(-1)
+    core = lax.axis_index("narrow")
+    my_slots = send_block[0, :, 0, :]
+    own = lax.dynamic_index_in_dim(my_slots, core, 1, keepdims=False)
+    theirs = swap(lax.dynamic_index_in_dim(my_slots, 1 - core, 1, keepdims=False))
+    send = jnp.where(core == 0, jnp.stack([own, theirs], 1), jnp.stack([theirs, own], 1)).reshape(-1)
     recv = recv_block.reshape(-1)
     count = tile_count.reshape(-1)
     words = mask_bits.reshape((-1,) + mask_bits.shape[4:])
@@ -397,27 +436,15 @@
     products, feats, act, gate = edges_forward(recv, arrived, mask_t, mask, scale, weight_in, weight_out)
     mine = gather_sum(send, exchange(products), nodes)
     updated, gain_part, picked = norm_and_select(send, mine, swap(mine), node_feats, cotangent, gain, owners)
-    products = edges_backward(
+    products, grads = edges_backward(
         recv, exchange(picked), mask_t, mask, scale, weight_in, weight_out, feats, act, gate
     )
     arrived = exchange(products)
-    weight_sums = tail_sum(arrived)
-    weight_sums = weight_sums + swap(weight_sums)
-    core = lax.axis_index("narrow")
-    extra = weight_sums.shape[0]
-    half = lax.dynamic_slice_in_dim(weight_sums, core * (extra // 2), extra // 2, 0)
-    chunk = jnp.concatenate([half.reshape(extra, width // 2), gain_part.sum(0).reshape(-1, width // 2)], 0)
-    chunk = jnp.pad(chunk, ((0, -chunk.shape[0] % 8), (0, 0)))
-    everyone = exchange(jnp.broadcast_to(chunk[None], (owners,) + chunk.shape))
+    grads, gain_part = lax.optimization_barrier((grads, gain_part))
+    grad_gain = sum_over_wide(gain_part.sum(0).reshape(-1, width // 2)).reshape(width)
+    grads = reduce_over_chips(grads)
     mine = gather_sum(send, arrived, nodes)
     grad_nodes = cotangent.astype(F32) + (mine + swap(mine))
-
-    grad_gain = everyone[:, extra : extra + 2].sum(0).reshape(width)
-    halves = everyone[:, :extra].reshape(owners, extra // 2, width)
-    theirs = swap(halves)
-    lower = jnp.where(core == 0, halves, theirs)
-    upper = jnp.where(core == 0, theirs, halves)
-    grads = jnp.concatenate([lower, upper], 1).reshape(2 * inner, width)
     pieces = inner // width
     grad_out = grads[:inner]
     grad_in = grads[inner:].reshape(pieces, width, width).transpose(1, 0, 2).reshape(width, inner)

time: 564 us -> 574 us (1.018)
  blocking collectives: 345 us -> 213 us
  waiting for transfers between devices: 118 us -> 199 us
  starting transfers between devices: 17.3 us -> 75.4 us
    all_to_all x3 -> x2, blocking collectives: 345 us -> 213 us  [exchange(): lax.all_to_all(tiles, ('wide', 'narrow'), split_axis=0, concat_axis=0, ti...]
    ppermute x0 -> x27, waiting for transfers between devices: none -> 96 us  [ring_sends(): moved.append(lax.ppermute(values[offset - 1], 'wide', pairs))]
    ppermute x0 -> x27, starting transfers between devices: none -> 54.8 us  [ring_sends(): moved.append(lax.ppermute(values[offset - 1], 'wide', pairs))]
    all_to_all x2, waiting for transfers between devices: 115 us -> 96.4 us  [exchange(): lax.all_to_all(tiles, ('wide', 'narrow'), split_axis=0, concat_axis=0, ti...]
    pallas_call x2 -> x1, Pallas kernels: 20.2 us -> 19.6 us  [edges_backward(): pl.pallas_call(backward_kernel, out_shape=(jax.ShapeDtypeStruct((owners,...]
  transfers between devices with their start and end apart: 6 -> 34, of which waited for: 4 -> 14; matrix products, arithmetic and copies ran while one was open for 1% -> 2% of each run, Pallas kernels for 2% -> 2%
where the time goes in v3:
time: 574 us; the launch traced here: 572 us
  blocking collectives  213 us (37%)
  waiting for transfers between devices  199 us (35%)
  starting transfers between devices  75.4 us (13%)
  Pallas kernels  67.4 us (12%)
  local copies, waits for them, and re-layouts  10.6 us (2%)
  other arithmetic  5.76 us (1%)
    all_to_all x2, blocking collectives, exchange(): lax.all_to_all(tiles, ('wide', 'narrow'), split_axis=0, concat_axis=0, ti...  213 us
    all_to_all x2, waiting for transfers between devices, exchange(): lax.all_to_all(tiles, ('wide', 'narrow'), split_axis=0, concat_axis=0, ti...  96.4 us
    ppermute x27, waiting for transfers between devices, ring_sends(): moved.append(lax.ppermute(values[offset - 1], 'wide', pairs))  96 us
    ppermute x27, starting transfers between devices, ring_sends(): moved.append(lax.ppermute(values[offset - 1], 'wide', pairs))  54.8 us
    pallas_call x1, Pallas kernels, edges_forward(): pl.pallas_call(forward_kernel, out_shape=(jax.ShapeDtypeStruct((owners, 2...  20.5 us
    all_to_all x2, starting transfers between devices, exchange(): lax.all_to_all(tiles, ('wide', 'narrow'), split_axis=0, concat_axis=0, ti...  19.9 us
    pallas_call x1, Pallas kernels, edges_backward(): pl.pallas_call(backward_kernel, out_shape=(jax.ShapeDtypeStruct((owners,...  19.6 us
  transfers between devices with their start and end apart: 34, of which 14 were waited for; matrix products, arithmetic and copies ran while one was open for 2% of the time, Pallas kernels for 2%

profile of v3, /device:TPU:0, one launch (start us, length us, event | category | flops | bytes accessed | tf_op | source)
XLA Modules:
  0.0 572.3 jit_solution(3361049817064439716)
XLA Ops:
  0.6 0.8 fusion.16
  1.4 1.1 collective-permute-done
  2.6 0.1 select_n.313.send_ref
  2.8 1.0 copy-done.1
  3.8 3.8 select_blocks.1
  7.7 11.7 %all-to-all-start = ((bf16[128,128,256]{2,1,0:T(8,128)(2,1)}), bf16[128,128,256]{2,1,0:T(8,128)(2,1)}, u32[]{:S(2)}, u32[]{:S(2)}) async-start(bf16[128,128,256]{2,1,0:T(8,128)(2,1)} %select_blocks.1), calls=%async_computation | async-start | bytes 16777216 | tf_op jit(solution)/shard_map/all_to_all | solution.py:344
  19.4 0.1 copy.35
  19.6 1.3 copy.36.scale_ref
  21.3 7.9 %unpack_masks.1 = (bf16[128,128,128]{2,1,0:T(8,128)(2,1)}, bf16[128,128,128]{2,1,0:T(8,128)(2,1)}) custom-call(s32[64]{0:T(128)S(1)} %bitcast.112, s32[128,9,128]{2,1,0:T(8,128)S(1)} %bitcast.110, s32[128,128]{1,0:T(8,128)S(1)} %select_shift-left_fusion.bit_ref), custom_call_target="tpu_custom_call" | custom-call | flops 33554432 | bytes 16777216 | tf_op jit(solution)/shard_map/unpack_masks/pallas_call | solution.py:58
  29.2 96.4 %all-to-all-done = bf16[128,128,256]{2,1,0:T(8,128)(2,1)} async-done(((bf16[128,128,256]{2,1,0:T(8,128)(2,1)}), bf16[128,128,256]{2,1,0:T(8,128)(2,1)}, u32[]{:S(2)}, u32[]{:S(2)}) %all-to-all-start) | async-done | bytes 8388640 | tf_op jit(solution)/shard_map/all_to_all | solution.py:344
  125.6 20.5 %edges_forward.1 = (bf16[64,256,256]{2,1,0:T(8,128)(2,1)}, bf16[2048,256]{1,0:T(8,128)(2,1)S(1)}, bf16[2048,512]{1,0:T(8,128)(2,1)}, f32[2048,512]{1,0:T(8,128)}) custom-call(s32[128]{0:T(128)S(1)} %reshape.306.recv_ref, bf16[64,256,256]{2,1,0:T(8,128)(2,1)} %bitcast.3.arrived_ref, bf16[128,128,128]{2,1,0:T(8,128)(2,1)} %get-tuple-element.19.mask_t_ref, ...), custom_call_target="tpu_custom_call" | custom-call | tf_op jit(solution)/shard_map/edges_forward/pallas_call | solution.py:236
  146.1 1.0 copy-done.6
  147.1 106.6 %all_to_all.20 = bf16[128,128,256]{2,1,0:T(8,128)(2,1)} all-to-all(bf16[128,128,256]{2,1,0:T(8,128)(2,1)} %bitcast.116), channel_id=1, replica_groups=mesh['wide'=64,'narrow'=2] {'wide','narrow'}, dimensions={0} | all-to-all | bytes 16777216 | tf_op jit(solution)/shard_map/all_to_all | solution.py:344
  253.6 4.2 node_sums.2.mine_ref
  257.9 2.6 collective-permute-done.1.other_ref
  260.6 1.0 copy-done.9
  261.6 7.3 %norm_and_select.1 = (bf16[1024,256]{1,0:T(8,128)(2,1)}, f32[8,256]{1,0:T(8,128)S(1)}, bf16[128,128,256]{2,1,0:T(8,128)(2,1)}) custom-call(s32[128]{0:T(128)S(1)} %select_n.313.send_ref, f32[1024,256]{1,0:T(8,128)} %copy-done, f32[1024,256]{1,0:T(8,128)} %copy-done.9, bf16[1024,256]{1,0:T(8,128)(2,1)S(1)} %copy-done.2, bf16[1024,256]{1,0:T(8,128)(2,1)S(1)} %copy-done.3, ...), custom_call_target="tpu_custom_call" | custom-call | tf_op jit(solution)/shard_map/norm_and_select/pallas_call | solution.py:325
  268.9 106.2 %all_to_all.21 = bf16[128,128,256]{2,1,0:T(8,128)(2,1)} all-to-all(bf16[128,128,256]{2,1,0:T(8,128)(2,1)} %get-tuple-element.23), channel_id=1, replica_groups=mesh['wide'=64,'narrow'=2] {'wide','narrow'}, dimensions={0} | all-to-all | bytes 16777216 | tf_op jit(solution)/shard_map/all_to_all | solution.py:344
  375.1 19.6 %edges_backward.1 = (bf16[64,256,256]{2,1,0:T(8,128)(2,1)}, f32[1024,256]{1,0:T(8,128)S(1)}) custom-call(s32[128]{0:T(128)S(1)} %reshape.306.recv_ref, bf16[64,256,256]{2,1,0:T(8,128)(2,1)} %bitcast.113, bf16[128,128,128]{2,1,0:T(8,128)(2,1)} %get-tuple-element.19.mask_t_ref, bf16[128,128,128]{2,1,0:T(8,128)(2,1)} %get-tuple-element.20.mask_ref, ...), custom_call_target="tpu_custom_call" | custom-call | tf_op jit(solution)/shard_map/edges_backward/pallas_call | solution.py:256
  394.7 8.2 %all-to-all-start.3 = ((bf16[128,128,256]{2,1,0:T(8,128)(2,1)}), bf16[128,128,256]{2,1,0:T(8,128)(2,1)}, u32[]{:S(2)}, u32[]{:S(2)}) async-start(bf16[128,128,256]{2,1,0:T(8,128)(2,1)} %bitcast.115), calls=%async_computation.3 | async-start | bytes 16777216 | tf_op jit(solution)/shard_map/all_to_all | solution.py:344
  403.4 1.8 collective-permute-done.3
  405.3 1.0 collective-permute-start.4
  406.3 2.7 collective-permute-start.5
  408.9 1.5 collective-permute-start.6
  410.6 0.6 collective-permute-start.23
  411.2 0.9 collective-permute-start.24
  412.1 87.5 %collective-permute-done.23 = f32[2,128]{1,0:T(2,128)S(1)} collective-permute-done((f32[2,128]{1,0:T(2,128)S(1)}, f32[2,128]{1,0:T(2,128)S(1)}, u32[]{:S(2)}, u32[]{:S(2)}) %collective-permute-start.23) | collective-permute-done | bytes 1056 | tf_op jit(solution)/shard_map/ppermute | solution.py:360
  499.6 13.5 %collective-permute-start.25 = (f32[2,128]{1,0:T(2,128)S(1)}, f32[2,128]{1,0:T(2,128)S(1)}, u32[]{:S(2)}, u32[]{:S(2)}) collective-permute-start(f32[2,128]{1,0:T(2,128)S(1)} %bitcast.137), channel_id=1, source_target_pairs={{0,96},{2,98},{4,100},{6,102},{8,104},{10,106},{12,108},{14,110},{... | collective-permute-start | bytes 3080 | tf_op jit(solution)/shard_map/ppermute | solution.py:360
  513.5 1.0 collective-permute-done.25
  514.5 0.6 gather_fusion.3
  515.1 2.4 collective-permute-start.7
  517.5 2.8 collective-permute-start.9
  520.4 2.8 collective-permute-start.27
  523.2 0.9 collective-permute-start.28
  524.2 4.6 collective-permute-start.11
  528.8 2.5 collective-permute-start.12
  531.3 0.6 gather_fusion.4
  531.9 0.8 collective-permute-done.12
  532.7 1.2 collective-permute-start.13
  533.9 3.8 collective-permute-start.14
  537.7 2.0 collective-permute-start.29
  539.8 1.5 collective-permute-done.15
  541.3 0.5 gather_fusion
  541.9 1.4 collective-permute-start.16
  543.4 1.7 collective-permute-start.17
  545.1 2.3 collective-permute-start.18
  547.4 1.4 collective-permute-done.17
  548.8 0.2 collective-permute-done.18
  549.0 0.6 gather_fusion.1
  549.7 4.9 collective-permute-start.20
  554.7 1.4 collective-permute-done.19
  556.1 1.2 collective-permute-start.31
  557.4 1.6 collective-permute-done.20
  559.0 0.6 collective-permute-done.21
  559.7 0.6 gather_fusion.2
  560.3 4.2 node_sums.3
  564.5 0.9 bitcast_select_fusion
  565.5 0.5 collective-permute-start.22
  566.0 0.6 gather_fusion.5
  566.7 0.6 multiply_bitcast_fusion
  567.2 1.0 collective-permute-done.22
  568.3 2.0 select_multiply_fusion
  570.3 0.9 copy.45
  571.1 1.2 add_add_fusion
  (103 shorter events, 2.4 us)
Async XLA Ops:
  1.4 1.1 collective-permute-start
  2.8 1.0 copy-start.1
  7.6 11.8 %copy-start.10 = (s32[1,1,64,2,9,128]{5,3,4,2,1,0:T(2,128)S(1)}, s32[1,1,64,2,9,128]{5,3,4,2,1,0:T(2,128)}, u32[]{:S(2)}) copy-start(s32[1,1,64,2,9,128]{5,3,4,2,1,0:T(2,128)} %param.16) | copy-start | bytes 1769476
  7.6 11.9 %copy-start.11 = (s32[2048]{0:T(1024)S(1)}, s32[2048]{0:T(1024)}, u32[]{:S(2)}) copy-start(s32[2048]{0:T(1024)} %param.17) | copy-start | bytes 24580
  7.7 13.3 %copy-start.12 = (s32[1,1,64,2]{2,3,1,0:T(2,128)S(1)}, s32[1,1,64,2]{2,3,1,0:T(2,128)}, u32[]{:S(2)}) copy-start(s32[1,1,64,2]{2,3,1,0:T(2,128)} %param.14) | copy-start | bytes 1540
  7.7 13.6 %copy-start.8 = (s32[1,1,64]{2,1,0:T(1,128)S(1)}, s32[1,1,64]{2,1,0:T(1,128)}, u32[]{:S(2)}) copy-start(s32[1,1,64]{2,1,0:T(1,128)} %param.15) | copy-start | bytes 772
  7.7 117.9 %copy-start.4 = (bf16[256,512]{1,0:T(8,128)(2,1)S(1)}, bf16[256,512]{1,0:T(8,128)(2,1)}, u32[]{:S(2)}) copy-start(bf16[256,512]{1,0:T(8,128)(2,1)} %w_in_ref.3) | copy-start | bytes 786436
  7.7 117.9 %copy-start.5 = (bf16[512,256]{1,0:T(8,128)(2,1)S(1)}, bf16[512,256]{1,0:T(8,128)(2,1)}, u32[]{:S(2)}) copy-start(bf16[512,256]{1,0:T(8,128)(2,1)} %w_out_ref.3) | copy-start | bytes 786436
  7.7 117.9 %all-to-all-start = ((bf16[128,128,256]{2,1,0:T(8,128)(2,1)}), bf16[128,128,256]{2,1,0:T(8,128)(2,1)}, u32[]{:S(2)}, u32[]{:S(2)}) async-start(bf16[128,128,256]{2,1,0:T(8,128)(2,1)} %select_blocks.1), calls=%async_computation | async-start | bytes 16777216 | tf_op jit(solution)/shard_map/all_to_all | solution.py:344
  146.1 1.0 copy-start.6
  253.6 7.9 %copy-start.2 = (bf16[1024,256]{1,0:T(8,128)(2,1)S(1)}, bf16[1024,256]{1,0:T(8,128)(2,1)}, u32[]{:S(2)}) copy-start(bf16[1024,256]{1,0:T(8,128)(2,1)} %feats_ref.1) | copy-start | bytes 1572868
  253.6 7.9 %copy-start.3 = (bf16[1024,256]{1,0:T(8,128)(2,1)S(1)}, bf16[1024,256]{1,0:T(8,128)(2,1)}, u32[]{:S(2)}) copy-start(bf16[1024,256]{1,0:T(8,128)(2,1)} %cot_ref.1) | copy-start | bytes 1572868
  253.6 8.0 %copy-start.7 = (f32[256]{0:T(256)S(1)}, f32[256]{0:T(256)}, u32[]{:S(2)}) copy-start(f32[256]{0:T(256)} %param.20) | copy-start | bytes 3076
  257.8 2.8 copy-start
  257.8 2.7 collective-permute-start.1
  260.6 1.0 copy-start.9
  394.7 165.6 %all-to-all-start.3 = ((bf16[128,128,256]{2,1,0:T(8,128)(2,1)}), bf16[128,128,256]{2,1,0:T(8,128)(2,1)}, u32[]{:S(2)}, u32[]{:S(2)}) async-start(bf16[128,128,256]{2,1,0:T(8,128)(2,1)} %bitcast.115), calls=%async_computation.3 | async-start | bytes 16777216 | tf_op jit(solution)/shard_map/all_to_all | solution.py:344
  403.2 2.0 collective-permute-start.3
  405.3 109.8 %collective-permute-start.4 = (f32[128,256]{1,0:T(8,128)S(1)}, f32[128,256]{1,0:T(8,128)S(1)}, u32[]{:S(2)}, u32[]{:S(2)}) collective-permute-start(f32[128,256]{1,0:T(8,128)S(1)} %get-tuple-element.34), channel_id=1, source_target_pairs={{0,32},{2,34},{4,36},{6,38},{8,40},{10,42},{12,44},{14,46},{16,48}... | collective-permute-start | bytes 393224 | tf_op jit(solution)/shard_map/ppermute | solution.py:360
  406.3 108.8 %collective-permute-start.5 = (f32[128,256]{1,0:T(8,128)S(1)}, f32[128,256]{1,0:T(8,128)S(1)}, u32[]{:S(2)}, u32[]{:S(2)}) collective-permute-start(f32[128,256]{1,0:T(8,128)S(1)} %get-tuple-element.36), channel_id=1, source_target_pairs={{0,64},{2,66},{4,68},{6,70},{8,72},{10,74},{12,76},{14,78},{16,80}... | collective-permute-start | bytes 393224 | tf_op jit(solution)/shard_map/ppermute | solution.py:360
  408.9 106.1 %collective-permute-start.6 = (f32[128,256]{1,0:T(8,128)S(1)}, f32[128,256]{1,0:T(8,128)S(1)}, u32[]{:S(2)}, u32[]{:S(2)}) collective-permute-start(f32[128,256]{1,0:T(8,128)S(1)} %get-tuple-element.35), channel_id=1, source_target_pairs={{0,96},{2,98},{4,100},{6,102},{8,104},{10,106},{12,108},{14,110},{... | collective-permute-start | bytes 393224 | tf_op jit(solution)/shard_map/ppermute | solution.py:360
  410.6 89.1 %collective-permute-start.23 = (f32[2,128]{1,0:T(2,128)S(1)}, f32[2,128]{1,0:T(2,128)S(1)}, u32[]{:S(2)}, u32[]{:S(2)}) collective-permute-start(f32[2,128]{1,0:T(2,128)S(1)} %bitcast.135), channel_id=1, source_target_pairs={{0,32},{2,34},{4,36},{6,38},{8,40},{10,42},{12,44},{14,46},{16,48}... | collective-permute-start | bytes 3080 | tf_op jit(solution)/shard_map/ppermute | solution.py:360
  411.2 102.3 %collective-permute-start.24 = (f32[2,128]{1,0:T(2,128)S(1)}, f32[2,128]{1,0:T(2,128)S(1)}, u32[]{:S(2)}, u32[]{:S(2)}) collective-permute-start(f32[2,128]{1,0:T(2,128)S(1)} %bitcast.136), channel_id=1, source_target_pairs={{0,64},{2,66},{4,68},{6,70},{8,72},{10,74},{12,76},{14,78},{16,80}... | collective-permute-start | bytes 3080 | tf_op jit(solution)/shard_map/ppermute | solution.py:360
  499.6 14.8 %collective-permute-start.25 = (f32[2,128]{1,0:T(2,128)S(1)}, f32[2,128]{1,0:T(2,128)S(1)}, u32[]{:S(2)}, u32[]{:S(2)}) collective-permute-start(f32[2,128]{1,0:T(2,128)S(1)} %bitcast.137), channel_id=1, source_target_pairs={{0,96},{2,98},{4,100},{6,102},{8,104},{10,106},{12,108},{14,110},{... | collective-permute-start | bytes 3080 | tf_op jit(solution)/shard_map/ppermute | solution.py:360
  515.1 8.0 %collective-permute-start.7 = (f32[32,256]{1,0:T(8,128)S(1)}, f32[32,256]{1,0:T(8,128)S(1)}, u32[]{:S(2)}, u32[]{:S(2)}) collective-permute-start(f32[32,256]{1,0:T(8,128)S(1)} %get-tuple-element.37), channel_id=1, source_target_pairs={{0,8},{2,10},{4,12},{6,14},{8,16},{10,18},{12,20},{14,22},{16,24},... | collective-permute-start | bytes 98312 | tf_op jit(solution)/shard_map/ppermute | solution.py:360
  517.5 6.6 %collective-permute-start.8 = (f32[32,256]{1,0:T(8,128)S(1)}, f32[32,256]{1,0:T(8,128)S(1)}, u32[]{:S(2)}, u32[]{:S(2)}) collective-permute-start(f32[32,256]{1,0:T(8,128)S(1)} %get-tuple-element.39), channel_id=1, source_target_pairs={{0,16},{2,18},{4,20},{6,22},{8,24},{10,26},{12,28},{14,30},{16,0},... | collective-permute-start | bytes 98312 | tf_op jit(solution)/shard_map/ppermute | solution.py:360
  517.5 6.6 %collective-permute-start.9 = (f32[32,256]{1,0:T(8,128)S(1)}, f32[32,256]{1,0:T(8,128)S(1)}, u32[]{:S(2)}, u32[]{:S(2)}) collective-permute-start(f32[32,256]{1,0:T(8,128)S(1)} %get-tuple-element.38), channel_id=1, source_target_pairs={{0,24},{2,26},{4,28},{6,30},{8,0},{10,2},{12,4},{14,6},{16,8},{18,... | collective-permute-start | bytes 98312 | tf_op jit(solution)/shard_map/ppermute | solution.py:360
  520.4 8.4 %collective-permute-start.26 = (f32[2,128]{1,0:T(2,128)S(1)}, f32[2,128]{1,0:T(2,128)S(1)}, u32[]{:S(2)}, u32[]{:S(2)}) collective-permute-start(f32[2,128]{1,0:T(2,128)S(1)} %select_reduce_fusion.2), channel_id=1, source_target_pairs={{0,8},{2,10},{4,12},{6,14},{8,16},{10,18},{12,20},{14,22},{16,24},... | collective-permute-start | bytes 3080 | tf_op jit(solution)/shard_map/ppermute | solution.py:360
  520.4 10.9 %collective-permute-start.27 = (f32[2,128]{1,0:T(2,128)S(1)}, f32[2,128]{1,0:T(2,128)S(1)}, u32[]{:S(2)}, u32[]{:S(2)}) collective-permute-start(f32[2,128]{1,0:T(2,128)S(1)} %select_reduce_fusion.2), channel_id=1, source_target_pairs={{0,16},{2,18},{4,20},{6,22},{8,24},{10,26},{12,28},{14,30},{16,0},... | collective-permute-start | bytes 3080 | tf_op jit(solution)/shard_map/ppermute | solution.py:360
  523.2 8.1 %collective-permute-start.28 = (f32[2,128]{1,0:T(2,128)S(1)}, f32[2,128]{1,0:T(2,128)S(1)}, u32[]{:S(2)}, u32[]{:S(2)}) collective-permute-start(f32[2,128]{1,0:T(2,128)S(1)} %select_reduce_fusion.2), channel_id=1, source_target_pairs={{0,24},{2,26},{4,28},{6,30},{8,0},{10,2},{12,4},{14,6},{16,8},{18,... | collective-permute-start | bytes 3080 | tf_op jit(solution)/shard_map/ppermute | solution.py:360
  524.1 7.8 %collective-permute-start.10 = (f32[8,256]{1,0:T(8,128)S(1)}, f32[8,256]{1,0:T(8,128)S(1)}, u32[]{:S(2)}, u32[]{:S(2)}) collective-permute-start(f32[8,256]{1,0:T(8,128)S(1)} %get-tuple-element.40), channel_id=1, source_target_pairs={{0,2},{2,4},{4,6},{6,0},{8,10},{10,12},{12,14},{14,8},{16,18},{18,... | collective-permute-start | bytes 24584 | tf_op jit(solution)/shard_map/ppermute | solution.py:360
  524.2 7.7 %collective-permute-start.11 = (f32[8,256]{1,0:T(8,128)S(1)}, f32[8,256]{1,0:T(8,128)S(1)}, u32[]{:S(2)}, u32[]{:S(2)}) collective-permute-start(f32[8,256]{1,0:T(8,128)S(1)} %get-tuple-element.42), channel_id=1, source_target_pairs={{0,4},{2,6},{4,0},{6,2},{8,12},{10,14},{12,8},{14,10},{16,20},{18,... | collective-permute-start | bytes 24584 | tf_op jit(solution)/shard_map/ppermute | solution.py:360
  528.8 3.9 collective-permute-start.12
  532.7 7.1 %collective-permute-start.13 = (f32[8,256]{1,0:T(8,128)S(1)}, f32[8,256]{1,0:T(8,128)S(1)}, u32[]{:S(2)}, u32[]{:S(2)}) collective-permute-start(f32[8,256]{1,0:T(8,128)S(1)} %fusion.6), channel_id=1, source_target_pairs={{0,2},{2,4},{4,6},{6,0},{8,10},{10,12},{12,14},{14,8},{16,18},{18,... | collective-permute-start | bytes 24584 | tf_op jit(solution)/shard_map/ppermute | solution.py:360
  533.9 5.9 %collective-permute-start.14 = (f32[8,256]{1,0:T(8,128)S(1)}, f32[8,256]{1,0:T(8,128)S(1)}, u32[]{:S(2)}, u32[]{:S(2)}) collective-permute-start(f32[8,256]{1,0:T(8,128)S(1)} %fusion.6), channel_id=1, source_target_pairs={{0,4},{2,6},{4,0},{6,2},{8,12},{10,14},{12,8},{14,10},{16,20},{18,... | collective-permute-start | bytes 24584 | tf_op jit(solution)/shard_map/ppermute | solution.py:360
  537.7 3.7 collective-permute-start.15
  537.7 28.2 %collective-permute-start.29 = (f32[2,128]{1,0:T(2,128)S(1)}, f32[2,128]{1,0:T(2,128)S(1)}, u32[]{:S(2)}, u32[]{:S(2)}) collective-permute-start(f32[2,128]{1,0:T(2,128)S(1)} %select_reduce_fusion.1), channel_id=1, source_target_pairs={{0,2},{2,4},{4,6},{6,0},{8,10},{10,12},{12,14},{14,8},{16,18},{18,... | collective-permute-start | bytes 3080 | tf_op jit(solution)/shard_map/ppermute | solution.py:360
  539.8 26.2 %collective-permute-start.30 = (f32[2,128]{1,0:T(2,128)S(1)}, f32[2,128]{1,0:T(2,128)S(1)}, u32[]{:S(2)}, u32[]{:S(2)}) collective-permute-start(f32[2,128]{1,0:T(2,128)S(1)} %select_reduce_fusion.1), channel_id=1, source_target_pairs={{0,4},{2,6},{4,0},{6,2},{8,12},{10,14},{12,8},{14,10},{16,20},{18,... | collective-permute-start | bytes 3080 | tf_op jit(solution)/shard_map/ppermute | solution.py:360
  541.9 5.5 collective-permute-start.16
  543.4 5.4 collective-permute-start.17
  545.1 3.9 collective-permute-start.18
  549.7 6.5 %collective-permute-start.19 = (f32[128,256]{1,0:T(8,128)S(1)}, f32[128,256]{1,0:T(8,128)S(1)}, u32[]{:S(2)}, u32[]{:S(2)}) collective-permute-start(f32[128,256]{1,0:T(8,128)S(1)} %bitcast_select_fusion.1), channel_id=1, source_target_pairs={{0,32},{2,34},{4,36},{6,38},{8,40},{10,42},{12,44},{14,46},{16,48}... | collective-permute-start | bytes 393224 | tf_op jit(solution)/shard_map/ppermute | solution.py:360
  549.7 9.3 %collective-permute-start.20 = (f32[128,256]{1,0:T(8,128)S(1)}, f32[128,256]{1,0:T(8,128)S(1)}, u32[]{:S(2)}, u32[]{:S(2)}) collective-permute-start(f32[128,256]{1,0:T(8,128)S(1)} %bitcast_select_fusion.1), channel_id=1, source_target_pairs={{0,64},{2,66},{4,68},{6,70},{8,72},{10,74},{12,76},{14,78},{16,80}... | collective-permute-start | bytes 393224 | tf_op jit(solution)/shard_map/ppermute | solution.py:360
  554.6 5.0 collective-permute-start.21
  556.1 9.9 %collective-permute-start.31 = (f32[2,128]{1,0:T(2,128)S(1)}, f32[2,128]{1,0:T(2,128)S(1)}, u32[]{:S(2)}, u32[]{:S(2)}) collective-permute-start(f32[2,128]{1,0:T(2,128)S(1)} %select_reduce_fusion.1), channel_id=1, source_target_pairs={{0,6},{2,0},{4,2},{6,4},{8,14},{10,8},{12,10},{14,12},{16,22},{18,... | collective-permute-start | bytes 3080 | tf_op jit(solution)/shard_map/ppermute | solution.py:360
  564.4 6.7 %collective-permute-start.2 = (f32[1024,256]{1,0:T(8,128)S(1)}, f32[1024,256]{1,0:T(8,128)S(1)}, u32[]{:S(2)}, u32[]{:S(2)}) collective-permute-start(f32[1024,256]{1,0:T(8,128)S(1)} %node_sums.3), channel_id=1, source_target_pairs={{0,1},{1,0},{2,3},{3,2},{4,5},{5,4},{6,7},{7,6},{8,9},{9,8},{10,11... | collective-permute-start | bytes 3145736 | tf_op jit(solution)/shard_map/ppermute | solution.py:349
  565.5 2.8 collective-permute-start.22

commit v4 on v2

--- a/solution.py
+++ b/solution.py
@@ -10,6 +10,7 @@
 F32 = jnp.float32
 BF16 = jnp.bfloat16
 TILE = 128
+LANES = 128
 STEP_OWNERS = 4
 PARAMS = pltpu.CompilerParams(vmem_limit_bytes=52 * 1024 * 1024)
 
@@ -97,7 +98,7 @@
         compiler_params=PARAMS,
         name="select_blocks",
     )(send, rows)
-    return out.reshape(owners, 2 * TILE, features)
+    return out
 
 
 def part(ref, i, size):
@@ -134,15 +135,18 @@
         copy(part(mask_ref, i, per), part(mask, i, per), mask_sems.at[i]).wait()
         for tile in range(per):
             where = rows_at(recv_ref[i * per + tile])
-            owner = i * STEP_OWNERS + tile // 2
-            made[owner, tile % 2 * TILE : (tile % 2 + 1) * TILE] = dot(mask[i * per + tile], values[where]).astype(BF16)
-            if grads is not None and tile % 2:
-                extra = made.shape[1] - 2 * TILE
-                made[owner, 2 * TILE :] = grads[pl.ds(pl.multiple_of(owner * extra, extra), extra)].astype(BF16)
-        copy(part(made, i, STEP_OWNERS), part(out_ref, i, STEP_OWNERS), sem).start()
-        return carry
-
-    lax.fori_loop(0, made.shape[0] // STEP_OWNERS, body, 0)
+            product = dot(mask[i * per + tile], values[where]).astype(BF16)
+            for h in range(product.shape[1] // LANES):
+                made[i * per + tile, h * TILE : (h + 1) * TILE] = product[:, h * LANES : (h + 1) * LANES]
+            if grads is not None:
+                first = product.shape[1] // LANES * TILE
+                extra = made.shape[1] - first
+                at = pl.ds(pl.multiple_of((i * per + tile) * extra, extra), extra)
+                made[i * per + tile, first:] = grads[at].astype(BF16)
+        copy(part(made, i, per), part(out_ref, i, per), sem).start()
+        return carry
+
+    lax.fori_loop(0, made.shape[0] // per, body, 0)
 
 
 def forward_kernel(
@@ -204,11 +208,11 @@
         d_act = dot(d_edge, w_out_ref[...], ((1,), (1,)))
         d_pre = (d_act * gate[at]).astype(BF16)
         values[at] = (dot(d_pre, w_in_ref[...], ((1,), (1,))) * scale_ref[at]).astype(BF16)
-        grads[:inner] += dot(act[at], d_edge, ((0,), (0,)))
-        in_part = dot(feats[at], d_pre, ((0,), (0,)))
-        for piece in range(inner // width):
-            first = inner + piece * width
-            grads[first : first + width] += in_part[:, piece * width : (piece + 1) * width]
+        first = 0
+        for grad in (dot(act[at], d_edge, ((0,), (0,))), dot(feats[at], d_pre, ((0,), (0,)))):
+            for lane in range(0, grad.shape[1], LANES):
+                grads[first : first + grad.shape[0]] += grad[:, lane : lane + LANES]
+                first += grad.shape[0]
         return carry
 
     lax.fori_loop(0, acc.shape[0] // chunk, body, 0)
@@ -223,7 +227,7 @@
         pltpu.VMEM((owners, 2 * TILE, width), BF16),
         pltpu.VMEM((tiles, TILE, TILE), BF16),
         pltpu.VMEM((tiles, TILE, TILE), BF16),
-        pltpu.VMEM((owners, rows, width), BF16),
+        pltpu.VMEM((tiles, rows, LANES), BF16),
         pltpu.VMEM((edges, width), F32),
         pltpu.VMEM((edges, width), BF16),
         pltpu.VMEM((edges, width), BF16),
@@ -235,11 +239,12 @@
 def edges_forward(recv, arrived, mask_t, mask, scale, w_in, w_out):
     owners = arrived.shape[0]
     edges, width, inner = scale.shape[0], w_in.shape[0], w_in.shape[1]
-    buffers, sems = edge_scratch(owners, 2 * TILE, edges, width, inner)
+    rows = width // LANES * TILE
+    buffers, sems = edge_scratch(owners, rows, edges, width, inner)
     return pl.pallas_call(
         forward_kernel,
         out_shape=(
-            jax.ShapeDtypeStruct((owners, 2 * TILE, width), BF16),
+            jax.ShapeDtypeStruct((2 * owners, rows, LANES), BF16),
             jax.ShapeDtypeStruct((edges, width), BF16),
             jax.ShapeDtypeStruct((edges, inner), BF16),
             jax.ShapeDtypeStruct((edges, inner), F32),
@@ -255,15 +260,15 @@
 def edges_backward(recv, arrived, mask_t, mask, scale, w_in, w_out, feats, act, gate):
     owners = arrived.shape[0]
     edges, width, inner = scale.shape[0], w_in.shape[0], w_in.shape[1]
-    grad_rows = 2 * inner
-    extra = grad_rows // owners
-    buffers, sems = edge_scratch(owners, 2 * TILE + extra, edges, width, inner)
+    grad_rows = 2 * inner * width // LANES
+    rows = width // LANES * TILE + grad_rows // (2 * owners)
+    buffers, sems = edge_scratch(owners, rows, edges, width, inner)
     return pl.pallas_call(
         backward_kernel,
-        out_shape=jax.ShapeDtypeStruct((owners, 2 * TILE + extra, width), BF16),
+        out_shape=jax.ShapeDtypeStruct((2 * owners, rows, LANES), BF16),
         in_specs=[SMEM, ANY, ANY, ANY, VMEM, VMEM, VMEM, ANY, ANY, ANY],
         out_specs=ANY,
-        scratch_shapes=buffers + [pltpu.VMEM((grad_rows, width), F32)] + sems,
+        scratch_shapes=buffers + [pltpu.VMEM((grad_rows, LANES), F32)] + sems,
         compiler_params=PARAMS,
         name="edges_backward",
     )(recv, arrived, mask_t, mask, scale, w_in, w_out, feats, act, gate)
@@ -271,31 +276,30 @@
 
 def gather_sum_kernel(send_ref, arrived_ref, out_ref, arrived, sems):
     per = 2 * STEP_OWNERS
-    blocks = arrived_ref.at[:, pl.ds(0, 2 * TILE)]
-    start_all(blocks, arrived, sems, STEP_OWNERS)
+    start_all(arrived_ref, arrived, sems, per)
     out_ref[...] = jnp.zeros_like(out_ref)
 
     def body(i, carry):
-        copy(part(blocks, i, STEP_OWNERS), part(arrived, i, STEP_OWNERS), sems.at[i]).wait()
+        copy(part(arrived_ref, i, per), part(arrived, i, per), sems.at[i]).wait()
         for tile in range(per):
             where = rows_at(send_ref[i * per + tile])
-            rows = arrived[i * STEP_OWNERS + tile // 2, tile % 2 * TILE : (tile % 2 + 1) * TILE]
-            out_ref[where] += rows.astype(F32)
-        return carry
-
-    lax.fori_loop(0, arrived.shape[0] // STEP_OWNERS, body, 0)
-
-
-def gather_sum(send, arrived, nodes):
-    owners, _, width = arrived.shape
+            for h in range(out_ref.shape[1] // LANES):
+                rows = arrived[i * per + tile, h * TILE : (h + 1) * TILE]
+                out_ref[where, h * LANES : (h + 1) * LANES] += rows.astype(F32)
+        return carry
+
+    lax.fori_loop(0, arrived.shape[0] // per, body, 0)
+
+
+def gather_sum(send, arrived, nodes, width):
     return pl.pallas_call(
         gather_sum_kernel,
         out_shape=jax.ShapeDtypeStruct((nodes, width), F32),
         in_specs=[SMEM, ANY],
         out_specs=VMEM,
         scratch_shapes=[
-            pltpu.VMEM((owners, 2 * TILE, width), BF16),
-            pltpu.SemaphoreType.DMA((owners // STEP_OWNERS,)),
+            pltpu.VMEM(arrived.shape, BF16),
+            pltpu.SemaphoreType.DMA((arrived.shape[0] // (2 * STEP_OWNERS),)),
         ],
         compiler_params=PARAMS,
         name="node_sums",
@@ -303,21 +307,21 @@
 
 
 def tail_sum_kernel(arrived_ref, out_ref, tails, sem):
-    move = copy(arrived_ref.at[:, pl.ds(2 * TILE, tails.shape[1])], tails, sem)
+    first = arrived_ref.shape[1] - tails.shape[1]
+    move = copy(arrived_ref.at[:, pl.ds(first, tails.shape[1])], tails, sem)
     move.start()
     move.wait()
     out_ref[...] = jnp.sum(tails[...].astype(F32), axis=0)
 
 
-def tail_sum(arrived):
-    owners, rows, width = arrived.shape
-    extra = rows - 2 * TILE
+def tail_sum(arrived, rows):
+    tiles, total, lanes = arrived.shape
     return pl.pallas_call(
         tail_sum_kernel,
-        out_shape=jax.ShapeDtypeStruct((extra, width), F32),
+        out_shape=jax.ShapeDtypeStruct((total - rows, lanes), F32),
         in_specs=[ANY],
         out_specs=VMEM,
-        scratch_shapes=[pltpu.VMEM((owners, extra, width), BF16), pltpu.SemaphoreType.DMA],
+        scratch_shapes=[pltpu.VMEM((tiles, total - rows, lanes), BF16), pltpu.SemaphoreType.DMA],
         compiler_params=PARAMS,
         name="weight_sums",
     )(arrived)
@@ -359,11 +363,11 @@
         compiler_params=PARAMS,
         name="norm_and_select",
     )(send, mine, other, feats, cot, gain)
-    return updated, gain_part, out.reshape(owners, 2 * TILE, width)
-
-
-def exchange(rows):
-    return lax.all_to_all(rows, "wide", split_axis=0, concat_axis=0, tiled=True)
+    return updated, gain_part, out
+
+
+def exchange(tiles):
+    return lax.all_to_all(tiles, ("wide", "narrow"), split_axis=0, concat_axis=0, tiled=True)
 
 
 def swap(rows):
@@ -385,7 +389,11 @@
     owners = lax.axis_size("wide")
     nodes, width = node_feats.shape
     inner = weight_in.shape[1]
-    send = send_block.reshape(-1)
+    core = lax.axis_index("narrow")
+    my_slots = send_block[0, :, 0, :]
+    own = lax.dynamic_index_in_dim(my_slots, core, 1, keepdims=False)
+    theirs = swap(lax.dynamic_index_in_dim(my_slots, 1 - core, 1, keepdims=False))
+    send = jnp.where(core == 0, jnp.stack([own, theirs], 1), jnp.stack([theirs, own], 1)).reshape(-1)
     recv = recv_block.reshape(-1)
     count = tile_count.reshape(-1)
     words = mask_bits.reshape((-1,) + mask_bits.shape[4:])
@@ -393,34 +401,32 @@
     gain = norm_gain[None, :]
 
     mask, mask_t = unpack(count, words)
-    arrived = exchange(select(send, node_feats, owners))
+    by_owner = lambda tiles: tiles.reshape(owners, 2 * TILE, width)
+    arrived = by_owner(exchange(select(send, node_feats, owners)))
     products, feats, act, gate = edges_forward(recv, arrived, mask_t, mask, scale, weight_in, weight_out)
-    mine = gather_sum(send, exchange(products), nodes)
+    mine = gather_sum(send, exchange(products), nodes, width)
     updated, gain_part, picked = norm_and_select(send, mine, swap(mine), node_feats, cotangent, gain, owners)
-    products = edges_backward(
-        recv, exchange(picked), mask_t, mask, scale, weight_in, weight_out, feats, act, gate
+    arrived = by_owner(exchange(picked))
+    products = edges_backward(recv, arrived, mask_t, mask, scale, weight_in, weight_out, feats, act, gate)
+    arrived = exchange(products)
+
+    weight_sums = tail_sum(arrived, width // LANES * TILE)
+    extra = weight_sums.shape[0]
+    chunk = jnp.concatenate([weight_sums, gain_part.sum(0).reshape(-1, LANES)], 0)
+    chunk = jnp.pad(chunk, ((0, -chunk.shape[0] % 8), (0, 0)))
+    everyone = lax.all_to_all(
+        jnp.broadcast_to(chunk[None], (owners,) + chunk.shape), "wide", split_axis=0, concat_axis=0, tiled=True
     )
-    arrived = exchange(products)
-    weight_sums = tail_sum(arrived)
-    weight_sums = weight_sums + swap(weight_sums)
-    core = lax.axis_index("narrow")
-    extra = weight_sums.shape[0]
-    half = lax.dynamic_slice_in_dim(weight_sums, core * (extra // 2), extra // 2, 0)
-    chunk = jnp.concatenate([half.reshape(extra, width // 2), gain_part.sum(0).reshape(-1, width // 2)], 0)
-    chunk = jnp.pad(chunk, ((0, -chunk.shape[0] % 8), (0, 0)))
-    everyone = exchange(jnp.broadcast_to(chunk[None], (owners,) + chunk.shape))
-    mine = gather_sum(send, arrived, nodes)
+    mine = gather_sum(send, arrived, nodes, width)
     grad_nodes = cotangent.astype(F32) + (mine + swap(mine))
 
-    grad_gain = everyone[:, extra : extra + 2].sum(0).reshape(width)
-    halves = everyone[:, :extra].reshape(owners, extra // 2, width)
-    theirs = swap(halves)
-    lower = jnp.where(core == 0, halves, theirs)
-    upper = jnp.where(core == 0, theirs, halves)
-    grads = jnp.concatenate([lower, upper], 1).reshape(2 * inner, width)
-    pieces = inner // width
-    grad_out = grads[:inner]
-    grad_in = grads[inner:].reshape(pieces, width, width).transpose(1, 0, 2).reshape(width, inner)
+    grad_gain = everyone[:, extra : extra + width // LANES].sum(0).reshape(width)
+    held = everyone[:, :extra]
+    theirs = swap(held)
+    grads = jnp.stack([jnp.where(core == 0, held, theirs), jnp.where(core == 0, theirs, held)], 1)
+    grads = grads.reshape(-1, LANES)
+    grad_out = jnp.concatenate(jnp.split(grads[: inner * width // LANES], width // LANES), 1)
+    grad_in = jnp.concatenate(jnp.split(grads[inner * width // LANES :], inner // LANES), 1)
 
     edge_factor = (degree.shape[0] * owners * lax.axis_size("narrow")) ** (-0.5)
     return (

time: 564 us -> 549 us (0.973)
  blocking collectives: 345 us -> 213 us
  waiting for transfers between devices: 118 us -> 224 us
  starting transfers between devices: 17.3 us -> 29.1 us
    all_to_all x3 -> x2, blocking collectives: 345 us -> 213 us  [exchange(): lax.all_to_all(tiles, ('wide', 'narrow'), split_axis=0, concat_axis=0, ti...]
    all_to_all x2 -> x3, waiting for transfers between devices: 115 us -> 220 us  [the longest x2 209 us: exchange(): lax.all_to_all(tiles, ('wide', 'narrow'), split_axis=0, concat_axis=0, ti...]
    all_to_all x2 -> x3, starting transfers between devices: 17 us -> 28.9 us  [the longest x2 19.8 us: exchange(): lax.all_to_all(tiles, ('wide', 'narrow'), split_axis=0, concat_axis=0, ti...]
  transfers between devices with their start and end apart: 6 -> 7, of which waited for: 4 -> 5; matrix products, arithmetic and copies ran while one was open for 1% -> 1% of each run, Pallas kernels for 2% -> 2%
where the time goes in v4:
time: 549 us; the launch traced here: 547 us
  waiting for transfers between devices  224 us (41%)
  blocking collectives  213 us (39%)
  Pallas kernels  68.3 us (12%)
  starting transfers between devices  29.1 us (5%)
  local copies, waits for them, and re-layouts  6.78 us (1%)
    all_to_all x2, blocking collectives, exchange(): lax.all_to_all(tiles, ('wide', 'narrow'), split_axis=0, concat_axis=0, ti...  213 us
    all_to_all x2, waiting for transfers between devices, exchange(): lax.all_to_all(tiles, ('wide', 'narrow'), split_axis=0, concat_axis=0, ti...  209 us
    pallas_call x1, Pallas kernels, edges_forward(): pl.pallas_call(forward_kernel, out_shape=(jax.ShapeDtypeStruct((2 * owner...  20.5 us
    all_to_all x2, starting transfers between devices, exchange(): lax.all_to_all(tiles, ('wide', 'narrow'), split_axis=0, concat_axis=0, ti...  19.8 us
    pallas_call x1, Pallas kernels, edges_backward(): pl.pallas_call(backward_kernel, out_shape=jax.ShapeDtypeStruct((2 * owner...  19 us
    all_to_all x1, waiting for transfers between devices, shards(): lax.all_to_all(jnp.broadcast_to(chunk[None], (owners,) + chunk.shape), 'w...  11.2 us
  transfers between devices with their start and end apart: 7, of which 5 were waited for; matrix products, arithmetic and copies ran while one was open for 1% of the time, Pallas kernels for 2%

profile of v4, /device:TPU:0, one launch (start us, length us, event | category | flops | bytes accessed | tf_op | source)
XLA Modules:
  0.0 546.6 jit_solution(13817411846306876131)
XLA Ops:
  0.6 0.8 dynamic-slice_bitcast_fusion.1
  1.4 0.0 collective-permute-start
  1.4 1.1 collective-permute-done
  2.5 0.1 copy.19
  2.6 0.1 select_n.42.send_ref
  2.8 0.0 copy-start.2
  2.8 1.0 copy-done.2
  3.8 3.8 select_blocks.1
  7.6 0.0 copy-start.13
  7.6 0.0 copy-start.12
  7.6 0.0 copy-start.11
  7.6 0.0 copy-start.9
  7.6 0.0 copy-start.5
  7.7 0.0 copy-start.6
  7.7 11.7 %all-to-all-start = ((bf16[128,128,256]{2,1,0:T(8,128)(2,1)}), bf16[128,128,256]{2,1,0:T(8,128)(2,1)}, u32[]{:S(2)}, u32[]{:S(2)}) async-start(bf16[128,128,256]{2,1,0:T(8,128)(2,1)} %select_blocks.1), calls=%async_computation | async-start | bytes 16777216 | tf_op jit(solution)/shard_map/all_to_all | solution.py:370
  19.4 0.0 copy-done.13
  19.4 0.1 copy.20
  19.5 0.1 reshape.49.recv_ref
  19.6 0.0 copy-done.12
  19.6 1.3 copy.22.scale_ref
  21.0 0.0 copy-done.11
  21.0 0.1 copy.21
  21.2 0.1 select_shift-left_fusion.bit_ref
  21.3 0.0 copy-done.9
  21.3 7.9 %unpack_masks.1 = (bf16[128,128,128]{2,1,0:T(8,128)(2,1)}, bf16[128,128,128]{2,1,0:T(8,128)(2,1)}) custom-call(s32[64]{0:T(128)S(1)} %bitcast.30, s32[128,9,128]{2,1,0:T(8,128)S(1)} %bitcast.28, s32[128,128]{1,0:T(8,128)S(1)} %select_shift-left_fusion.bit_ref), custom_call_target="tpu_custom_call" | custom-call | flops 33554432 | bytes 16777216 | tf_op jit(solution)/shard_map/unpack_masks/pallas_call | solution.py:59
  29.2 96.3 %all-to-all-done = bf16[128,128,256]{2,1,0:T(8,128)(2,1)} async-done(((bf16[128,128,256]{2,1,0:T(8,128)(2,1)}), bf16[128,128,256]{2,1,0:T(8,128)(2,1)}, u32[]{:S(2)}, u32[]{:S(2)}) %all-to-all-start) | async-done | bytes 8388640 | tf_op jit(solution)/shard_map/all_to_all | solution.py:370
  125.5 0.0 copy-done.5
  125.5 0.0 copy-done.6
  125.5 20.5 %edges_forward.1 = (bf16[128,256,128]{2,1,0:T(8,128)(2,1)}, bf16[2048,256]{1,0:T(8,128)(2,1)S(1)}, bf16[2048,512]{1,0:T(8,128)(2,1)}, f32[2048,512]{1,0:T(8,128)}) custom-call(s32[128]{0:T(128)S(1)} %reshape.49.recv_ref, bf16[64,256,256]{2,1,0:T(8,128)(2,1)} %bitcast.3.arrived_ref, bf16[128,128,128]{2,1,0:T(8,128)(2,1)} %get-tuple-element.14.mask_t_ref, ...), custom_call_target="tpu_custom_call" | custom-call | tf_op jit(solution)/shard_map/edges_forward/pallas_call | solution.py:244
  146.1 0.0 copy-start.7
  146.1 1.0 copy-done.7
  147.1 106.6 %all_to_all.25.arrived_ref = bf16[128,256,128]{2,1,0:T(8,128)(2,1)} all-to-all(bf16[128,256,128]{2,1,0:T(8,128)(2,1)} %get-tuple-element.16), channel_id=1, replica_groups=mesh['wide'=64,'narrow'=2] {'wide','narrow'}, dimensions={0} | all-to-all | bytes 16777216 | tf_op jit(solution)/shard_map/all_to_all | solution.py:370
  253.6 0.0 copy-start.3
  253.6 4.2 node_sums.2.mine_ref
  257.8 0.0 copy-start.1
  257.8 0.1 collective-permute-start.1
  257.9 2.6 collective-permute-done.1.other_ref
  260.6 0.0 copy-done.1
  260.6 1.0 copy-done.10
  261.6 0.0 copy-done.3
  261.6 0.0 copy-done.4
  261.6 0.0 copy-done.8
  261.6 7.3 %norm_and_select.1 = (bf16[1024,256]{1,0:T(8,128)(2,1)}, f32[8,256]{1,0:T(8,128)S(1)}, bf16[128,128,256]{2,1,0:T(8,128)(2,1)}) custom-call(s32[128]{0:T(128)S(1)} %select_n.42.send_ref, f32[1024,256]{1,0:T(8,128)} %copy-done.1, f32[1024,256]{1,0:T(8,128)} %copy-done.10, bf16[1024,256]{1,0:T(8,128)(2,1)S(1)} %copy-done.3, bf16[1024,256]{1,0:T(8,128)(2,1)S(1)} %copy-done.4, ...), custom_call_target="tpu_custom_call" | custom-call | tf_op jit(solution)/shard_map/norm_and_select/pallas_call | solution.py:353
  268.9 0.0 copy-start
  268.9 106.2 %all_to_all.26 = bf16[128,128,256]{2,1,0:T(8,128)(2,1)} all-to-all(bf16[128,128,256]{2,1,0:T(8,128)(2,1)} %get-tuple-element.18), channel_id=1, replica_groups=mesh['wide'=64,'narrow'=2] {'wide','narrow'}, dimensions={0} | all-to-all | bytes 16777216 | tf_op jit(solution)/shard_map/all_to_all | solution.py:370
  375.1 0.0 copy-done
  375.1 19.0 %edges_backward.1 = bf16[128,272,128]{2,1,0:T(8,128)(2,1)} custom-call(s32[128]{0:T(128)S(1)} %reshape.49.recv_ref, bf16[64,256,256]{2,1,0:T(8,128)(2,1)} %bitcast.31, bf16[128,128,128]{2,1,0:T(8,128)(2,1)} %get-tuple-element.14.mask_t_ref, bf16[128,128,128]{2,1,0:T(8,128)(2,1)} %get-tuple-element.15.mask_ref, f32[2048,1]{1,0:T(8,128)S(1)} %copy-done, ...), custom_call_target="tpu_custom_call" | custom-call | tf_op jit(solution)/shard_map/edges_backward/pallas_call | solution.py:266
  394.2 8.1 %all-to-all-start.3 = ((bf16[128,272,128]{2,1,0:T(8,128)(2,1)}), bf16[128,272,128]{2,1,0:T(8,128)(2,1)}, u32[]{:S(2)}, u32[]{:S(2)}) async-start(bf16[128,272,128]{2,1,0:T(8,128)(2,1)} %edges_backward.1), calls=%async_computation.3 | async-start | bytes 17825792 | tf_op jit(solution)/shard_map/all_to_all | solution.py:370
  402.3 112.3 %all-to-all-done.3.arrived_ref = bf16[128,272,128]{2,1,0:T(8,128)(2,1)} async-done(((bf16[128,272,128]{2,1,0:T(8,128)(2,1)}), bf16[128,272,128]{2,1,0:T(8,128)(2,1)}, u32[]{:S(2)}, u32[]{:S(2)}) %all-to-all-start.3) | async-done | bytes 8912928 | tf_op jit(solution)/shard_map/all_to_all | solution.py:370
  514.6 1.2 weight_sums.1
  515.9 0.9 broadcast_in_dim.14
  516.8 9.1 %all-to-all-start.4 = ((f32[64,24,128]{2,1,0:T(8,128)}), f32[64,24,128]{2,1,0:T(8,128)S(1)}, u32[]{:S(2)}, u32[]{:S(2)}) async-start(f32[64,24,128]{2,1,0:T(8,128)} %broadcast_in_dim.14), calls=%async_computation.4 | async-start | bytes 1572864 | tf_op jit(solution)/shard_map/all_to_all | solution.py:417
  525.9 4.3 node_sums.3
  530.2 0.1 collective-permute-start.2
  530.3 11.2 %all-to-all-done.4 = f32[64,24,128]{2,1,0:T(8,128)S(1)} async-done(((f32[64,24,128]{2,1,0:T(8,128)}), f32[64,24,128]{2,1,0:T(8,128)S(1)}, u32[]{:S(2)}, u32[]{:S(2)}) %all-to-all-start.4) | async-done | bytes 786464 | tf_op jit(solution)/shard_map/all_to_all | solution.py:417
  541.6 0.1 collective-permute-start.3
  541.7 0.1 slice_reduce_fusion
  541.8 0.6 multiply_bitcast_fusion
  542.3 0.0 collective-permute-done.2
  542.3 2.4 add_add_fusion
  544.7 0.0 collective-permute-done.3
  544.7 0.1 select_bitcast_fusion.1
  544.9 0.8 maximum_multiply_fusion.1
  545.7 0.8 maximum_multiply_fusion
  (12 shorter events, 0.2 us)
Async XLA Ops:
  1.4 1.1 collective-permute-start
  2.8 1.0 copy-start.2
  7.6 11.8 %copy-start.13 = (s32[1,1,64,2]{2,3,1,0:T(2,128)S(1)}, s32[1,1,64,2]{2,3,1,0:T(2,128)}, u32[]{:S(2)}) copy-start(s32[1,1,64,2]{2,3,1,0:T(2,128)} %param.12) | copy-start | bytes 1540
  7.6 12.0 %copy-start.12 = (s32[2048]{0:T(1024)S(1)}, s32[2048]{0:T(1024)}, u32[]{:S(2)}) copy-start(s32[2048]{0:T(1024)} %param.15) | copy-start | bytes 24580
  7.6 13.4 %copy-start.11 = (s32[1,1,64,2,9,128]{5,3,4,2,1,0:T(2,128)S(1)}, s32[1,1,64,2,9,128]{5,3,4,2,1,0:T(2,128)}, u32[]{:S(2)}) copy-start(s32[1,1,64,2,9,128]{5,3,4,2,1,0:T(2,128)} %param.14) | copy-start | bytes 1769476
  7.6 13.6 %copy-start.9 = (s32[1,1,64]{2,1,0:T(1,128)S(1)}, s32[1,1,64]{2,1,0:T(1,128)}, u32[]{:S(2)}) copy-start(s32[1,1,64]{2,1,0:T(1,128)} %param.13) | copy-start | bytes 772
  7.6 117.9 %copy-start.5 = (bf16[256,512]{1,0:T(8,128)(2,1)S(1)}, bf16[256,512]{1,0:T(8,128)(2,1)}, u32[]{:S(2)}) copy-start(bf16[256,512]{1,0:T(8,128)(2,1)} %w_in_ref.3) | copy-start | bytes 786436
  7.7 117.9 %copy-start.6 = (bf16[512,256]{1,0:T(8,128)(2,1)S(1)}, bf16[512,256]{1,0:T(8,128)(2,1)}, u32[]{:S(2)}) copy-start(bf16[512,256]{1,0:T(8,128)(2,1)} %w_out_ref.3) | copy-start | bytes 786436
  7.7 117.9 %all-to-all-start = ((bf16[128,128,256]{2,1,0:T(8,128)(2,1)}), bf16[128,128,256]{2,1,0:T(8,128)(2,1)}, u32[]{:S(2)}, u32[]{:S(2)}) async-start(bf16[128,128,256]{2,1,0:T(8,128)(2,1)} %select_blocks.1), calls=%async_computation | async-start | bytes 16777216 | tf_op jit(solution)/shard_map/all_to_all | solution.py:370
  146.1 1.0 copy-start.7
  253.6 7.9 %copy-start.3 = (bf16[1024,256]{1,0:T(8,128)(2,1)S(1)}, bf16[1024,256]{1,0:T(8,128)(2,1)}, u32[]{:S(2)}) copy-start(bf16[1024,256]{1,0:T(8,128)(2,1)} %feats_ref.1) | copy-start | bytes 1572868
  253.6 7.9 %copy-start.4 = (bf16[1024,256]{1,0:T(8,128)(2,1)S(1)}, bf16[1024,256]{1,0:T(8,128)(2,1)}, u32[]{:S(2)}) copy-start(bf16[1024,256]{1,0:T(8,128)(2,1)} %cot_ref.1) | copy-start | bytes 1572868
  253.6 7.9 %copy-start.8 = (f32[256]{0:T(256)S(1)}, f32[256]{0:T(256)}, u32[]{:S(2)}) copy-start(f32[256]{0:T(256)} %param.18) | copy-start | bytes 3076
  257.8 2.8 copy-start.1
  257.8 2.7 collective-permute-start.1
  260.6 1.0 copy-start.10
  268.9 106.2 %copy-start = (f32[2048,1]{1,0:T(8,128)S(1)}, f32[2048,1]{1,0:T(8,128)}, u32[]{:S(2)}) copy-start(f32[2048,1]{1,0:T(8,128)} %copy.22.scale_ref) | copy-start | bytes 24580
  394.2 120.5 %all-to-all-start.3 = ((bf16[128,272,128]{2,1,0:T(8,128)(2,1)}), bf16[128,272,128]{2,1,0:T(8,128)(2,1)}, u32[]{:S(2)}, u32[]{:S(2)}) async-start(bf16[128,272,128]{2,1,0:T(8,128)(2,1)} %edges_backward.1), calls=%async_computation.3 | async-start | bytes 17825792 | tf_op jit(solution)/shard_map/all_to_all | solution.py:370
  516.8 24.8 %all-to-all-start.4 = ((f32[64,24,128]{2,1,0:T(8,128)}), f32[64,24,128]{2,1,0:T(8,128)S(1)}, u32[]{:S(2)}, u32[]{:S(2)}) async-start(f32[64,24,128]{2,1,0:T(8,128)} %broadcast_in_dim.14), calls=%async_computation.4 | async-start | bytes 1572864 | tf_op jit(solution)/shard_map/all_to_all | solution.py:417
  530.2 12.1 %collective-permute-start.2 = (f32[1024,256]{1,0:T(8,128)S(1)}, f32[1024,256]{1,0:T(8,128)}, u32[]{:S(2)}, u32[]{:S(2)}) collective-permute-start(f32[1024,256]{1,0:T(8,128)S(1)} %node_sums.3), channel_id=1, source_target_pairs={{0,1},{1,0},{2,3},{3,2},{4,5},{5,4},{6,7},{7,6},{8,9},{9,8},{10,11... | collective-permute-start | bytes 3145736 | tf_op jit(solution)/shard_map/ppermute | solution.py:374
  541.6 3.1 collective-permute-start.3

commit v5 on v4

v5 whole, which is shorter than its diff:
```python
import functools

import jax
import jax.numpy as jnp
from jax import lax
from jax.experimental import pallas as pl
from jax.experimental.pallas import tpu as pltpu
from jax.sharding import PartitionSpec as P

F32 = jnp.float32
BF16 = jnp.bfloat16
TILE = 128
LANES = 128
STEP_TILES = 8
PARAMS = pltpu.CompilerParams(vmem_limit_bytes=12 * 1024 * 1024)


SMEM = pl.BlockSpec(memory_space=pltpu.SMEM)
VMEM = pl.BlockSpec(memory_space=pltpu.VMEM)


def dot(a, b, dims=((1,), (0,))):
    return lax.dot_general(a, b, (dims, ((), ())), preferred_element_type=F32)


def rows_at(block):
    return pl.ds(pl.multiple_of(block * TILE, TILE), TILE)


def unpack_kernel(count_ref, words_ref, mask_ref, mask_t_ref):
    step = pl.program_id(0)
    owners, words, slots, _ = words_ref.shape
    row = lax.broadcasted_iota(jnp.int32, (8, TILE), 0)
    for owner in range(owners):
        count = count_ref[step * owners + owner]
        for slot in range(slots):
            live = jnp.where(count > slot, jnp.int32(-1), jnp.int32(0))
            word = [jnp.broadcast_to(words_ref[owner, j, slot : slot + 1], (8, TILE)) & live for j in range(words)]
            groups = []
            for first in range(0, TILE, 8):
                low, high = first // 15, (first + 7) // 15
                picked = word[low]
                shift = row + (first - low * 15)
                if high != low:
                    later = row >= high * 15 - first
                    picked = jnp.where(later, word[high], picked)
                    shift = jnp.where(later, shift - 15, shift)
                groups.append((jnp.right_shift(picked, shift) & 1).astype(F32))
            mask = jnp.concatenate(groups, axis=0)
            mask_ref[owner * slots + slot] = mask.astype(BF16)
            mask_t_ref[owner * slots + slot] = mask.T.astype(BF16)


def unpack(count, words):
    owners, _, slots, _ = words.shape
    per = 8
    out = jax.ShapeDtypeStruct((owners * slots, TILE, TILE), BF16)
    block = pl.BlockSpec((per * slots, TILE, TILE), lambda i, c: (i, 0, 0))
    return pl.pallas_call(
        unpack_kernel,
        out_shape=(out, out),
        grid_spec=pltpu.PrefetchScalarGridSpec(
            num_scalar_prefetch=1,
            grid=(owners // per,),
            in_specs=[pl.BlockSpec((per,) + words.shape[1:], lambda i, c: (i, 0, 0, 0))],
            out_specs=(block, block),
        ),
        compiler_params=PARAMS,
        name="unpack_masks",
    )(count, words)


def steps_of(tiles):
    return tiles.shape[0] // STEP_TILES


def select_kernel(send_ref, rows_ref, out_ref):
    def body(i, carry):
        for tile in range(STEP_TILES):
            out_ref[i * STEP_TILES + tile] = rows_ref[rows_at(send_ref[i * STEP_TILES + tile])]
        return carry

    lax.fori_loop(0, steps_of(out_ref), body, 0)


def select(send, rows):
    return pl.pallas_call(
        select_kernel,
        out_shape=jax.ShapeDtypeStruct((send.shape[0], TILE, rows.shape[1]), BF16),
        in_specs=[SMEM, VMEM],
        out_specs=VMEM,
        compiler_params=PARAMS,
        name="select_blocks",
    )(send, rows)


def collect(recv_ref, arrived, mask_t, acc):
    acc[...] = jnp.zeros_like(acc)

    def body(i, carry):
        for tile in range(STEP_TILES):
            where = rows_at(recv_ref[i * STEP_TILES + tile])
            acc[where] += dot(mask_t[i * STEP_TILES + tile], arrived[i * STEP_TILES + tile])
        return carry

    lax.fori_loop(0, steps_of(arrived), body, 0)


def spread(recv_ref, mask, values, made, grads=None):
    def body(i, carry):
        for tile in range(STEP_TILES):
            where = rows_at(recv_ref[i * STEP_TILES + tile])
            product = dot(mask[i * STEP_TILES + tile], values[where]).astype(BF16)
            for h in range(product.shape[1] // LANES):
                made[i * STEP_TILES + tile, h * TILE : (h + 1) * TILE] = product[:, h * LANES : (h + 1) * LANES]
            if grads is not None:
                first = product.shape[1] // LANES * TILE
                extra = made.shape[1] - first
                at = pl.ds(pl.multiple_of((i * STEP_TILES + tile) * extra, extra), extra)
                made[i * STEP_TILES + tile, first:] = grads[at].astype(BF16)
        return carry

    lax.fori_loop(0, steps_of(made), body, 0)


def scaled(rows, degree_ref, i):
    blocks = rows.shape[0] // TILE
    parts = []
    for k in range(blocks):
        scale = lax.rsqrt(degree_ref[pl.ds(i * blocks + k, 1)].astype(F32))
        scale = jnp.broadcast_to(scale, (TILE, LANES)).T
        lanes = [rows[k * TILE : (k + 1) * TILE, j : j + LANES] * scale for j in range(0, rows.shape[1], LANES)]
        parts.append(jnp.concatenate(lanes, axis=1))
    return jnp.concatenate(parts, axis=0)


def forward_kernel(
    recv_ref, arrived, mask_t, mask, degree_ref, w_in_ref, w_out_ref, made, feats, act, gate, acc, values
):
    collect(recv_ref, arrived, mask_t, acc)
    chunk = 256

    def body(i, carry):
        at = pl.ds(pl.multiple_of(i * chunk, chunk), chunk)
        rows = scaled(acc[at], degree_ref, i).astype(BF16)
        feats[at] = rows
        pre = dot(rows, w_in_ref[...])
        sig = jax.nn.sigmoid(pre)
        hidden = (pre * sig).astype(BF16)
        act[at] = hidden
        gate[at] = sig * (1.0 + pre * (1.0 - sig))
        values[at] = dot(hidden, w_out_ref[...]).astype(BF16)
        return carry

    lax.fori_loop(0, acc.shape[0] // chunk, body, 0)
    spread(recv_ref, mask, values, made)


def backward_kernel(
    recv_ref, arrived, mask_t, mask, degree_ref, w_in_ref, w_out_ref, feats, act, gate, made, acc, values, grads
):
    grads[...] = jnp.zeros_like(grads)
    collect(recv_ref, arrived, mask_t, acc)
    chunk = 256

    def body(i, carry):
        at = pl.ds(pl.multiple_of(i * chunk, chunk), chunk)
        d_edge = acc[at].astype(BF16)
        d_act = dot(d_edge, w_out_ref[...], ((1,), (1,)))
        d_pre = (d_act * gate[at]).astype(BF16)
        values[at] = scaled(dot(d_pre, w_in_ref[...], ((1,), (1,))), degree_ref, i).astype(BF16)
        first = 0
        for grad in (dot(act[at], d_edge, ((0,), (0,))), dot(feats[at], d_pre, ((0,), (0,)))):
            for lane in range(0, grad.shape[1], LANES):
                grads[first : first + grad.shape[0]] += grad[:, lane : lane + LANES]
                first += grad.shape[0]
        return carry

    lax.fori_loop(0, acc.shape[0] // chunk, body, 0)
    spread(recv_ref, mask, values, made, grads)


def edges_forward(recv, arrived, mask_t, mask, degree, w_in, w_out):
    tiles = arrived.shape[0]
    edges, width, inner = degree.size, w_in.shape[0], w_in.shape[1]
    rows = width // LANES * TILE
    return pl.pallas_call(
        forward_kernel,
        out_shape=(
            jax.ShapeDtypeStruct((tiles, rows, LANES), BF16),
            jax.ShapeDtypeStruct((edges, width), BF16),
            jax.ShapeDtypeStruct((edges, inner), BF16),
            jax.ShapeDtypeStruct((edges, inner), F32),
        ),
        in_specs=[SMEM] + [VMEM] * 6,
        out_specs=(VMEM,) * 4,
        scratch_shapes=[
            pltpu.VMEM((edges, width), F32),
            pltpu.VMEM((edges, width), BF16),
        ],
        compiler_params=PARAMS,
        name="edges_forward",
    )(recv, arrived, mask_t, mask, degree, w_in, w_out)


def edges_backward(recv, arrived, mask_t, mask, degree, w_in, w_out, feats, act, gate):
    tiles = arrived.shape[0]
    edges, width, inner = degree.size, w_in.shape[0], w_in.shape[1]
    grad_rows = 2 * inner * width // LANES
    rows = width // LANES * TILE + grad_rows // tiles
    return pl.pallas_call(
        backward_kernel,
        out_shape=jax.ShapeDtypeStruct((tiles, rows, LANES), BF16),
        in_specs=[SMEM] + [VMEM] * 9,
        out_specs=VMEM,
        scratch_shapes=[
            pltpu.VMEM((edges, width), F32),
            pltpu.VMEM((edges, width), BF16),
            pltpu.VMEM((grad_rows, LANES), F32),
        ],
        compiler_params=PARAMS,
        name="edges_backward",
    )(recv, arrived, mask_t, mask, degree, w_in, w_out, feats, act, gate)


def gather_sum_kernel(send_ref, arrived, out_ref):
    out_ref[...] = jnp.zeros_like(out_ref)

    def body(i, carry):
        for tile in range(STEP_TILES):
            where = rows_at(send_ref[i * STEP_TILES + tile])
            for h in range(out_ref.shape[1] // LANES):
                rows = arrived[i * STEP_TILES + tile, h * TILE : (h + 1) * TILE]
                out_ref[where, h * LANES : (h + 1) * LANES] += rows.astype(F32)
        return carry

    lax.fori_loop(0, steps_of(arrived), body, 0)


def gather_sum(send, arrived, nodes, width):
    return pl.pallas_call(
        gather_sum_kernel,
        out_shape=jax.ShapeDtypeStruct((nodes, width), F32),
        in_specs=[SMEM, VMEM],
        out_specs=VMEM,
        compiler_params=PARAMS,
        name="node_sums",
    )(send, arrived)


def tail_sum_kernel(arrived_ref, out_ref):
    rows = out_ref.shape[0]
    out_ref[...] = jnp.sum(arrived_ref[:, arrived_ref.shape[1] - rows :].astype(F32), axis=0)


def tail_sum(arrived, rows):
    return pl.pallas_call(
        tail_sum_kernel,
        out_shape=jax.ShapeDtypeStruct((arrived.shape[1] - rows, arrived.shape[2]), F32),
        in_specs=[VMEM],
        out_specs=VMEM,
        compiler_params=PARAMS,
        name="weight_sums",
    )(arrived)


def norm_kernel(
    send_ref, mine_ref, other_ref, feats_ref, cot_ref, gain_ref, updated_ref, part_ref, out_ref, d_summed
):
    gain = gain_ref[...]

    def body(i, part):
        at = rows_at(i)
        summed = mine_ref[at] + other_ref[at]
        inv_rms = lax.rsqrt(jnp.mean(summed * summed, axis=-1, keepdims=True) + 1e-05)
        normed = summed * inv_rms
        updated_ref[at] = (feats_ref[at].astype(F32) + normed * gain).astype(BF16)
        upstream = cot_ref[at].astype(F32)
        d_normed = upstream * gain
        inner = jnp.mean(d_normed * normed, axis=-1, keepdims=True)
        d_summed[at] = (inv_rms * (d_normed - normed * inner)).astype(BF16)
        return part + jnp.sum((upstream * normed).reshape(TILE // 8, 8, -1), axis=0)

    parts = lax.fori_loop(0, mine_ref.shape[0] // TILE, body, jnp.zeros((8, mine_ref.shape[1]), F32))
    row = jnp.sum(parts, axis=0, keepdims=True)
    part_ref[...] = jnp.zeros_like(part_ref)
    for i in range(row.shape[1] // LANES):
        part_ref[i : i + 1] = row[:, i * LANES : (i + 1) * LANES]

    select_kernel(send_ref, d_summed, out_ref)


def norm_and_select(send, mine, other, feats, cot, gain):
    nodes, width = feats.shape
    updated, gain_part, out = pl.pallas_call(
        norm_kernel,
        out_shape=(
            jax.ShapeDtypeStruct((nodes, width), BF16),
            jax.ShapeDtypeStruct((8, LANES), F32),
            jax.ShapeDtypeStruct((send.shape[0], TILE, width), BF16),
        ),
        in_specs=[SMEM] + [VMEM] * 5,
        out_specs=(VMEM,) * 3,
        scratch_shapes=[pltpu.VMEM((nodes, width), BF16)],
        compiler_params=PARAMS,
        name="norm_and_select",
    )(send, mine, other, feats, cot, gain)
    return updated, gain_part, out


def exchange(tiles):
    return lax.all_to_all(tiles, ("wide", "narrow"), split_axis=0, concat_axis=0, tiled=True)


def swap(rows):
    return lax.ppermute(rows, "narrow", [(0, 1), (1, 0)])


def shards(
    node_feats,
    send_block,
    recv_block,
    tile_count,
    mask_bits,
    degree,
    weight_in,
    weight_out,
    norm_gain,
    cotangent,
):
    owners = lax.axis_size("wide")
    nodes, width = node_feats.shape
    inner = weight_in.shape[1]
    core = lax.axis_index("narrow")
    my_slots = send_block[0, :, 0, :]
    own = lax.dynamic_index_in_dim(my_slots, core, 1, keepdims=False)
    theirs = swap(lax.dynamic_index_in_dim(my_slots, 1 - core, 1, keepdims=False))
    send = jnp.where(core == 0, jnp.stack([own, theirs], 1), jnp.stack([theirs, own], 1)).reshape(-1)
    recv = recv_block.reshape(-1)
    count = tile_count.reshape(-1)
    words = mask_bits[0, 0].transpose(0, 2, 1, 3)
    degree_rows = degree.reshape(-1, LANES)
    gain = norm_gain[None, :]

    picked, mask, mask_t, recv = lax.optimization_barrier((select(send, node_feats), *unpack(count, words), recv))
    arrived = exchange(picked)
    products, feats, act, gate = edges_forward(recv, arrived, mask_t, mask, degree_rows, weight_in, weight_out)
    mine = gather_sum(send, exchange(products), nodes, width)
    updated, gain_part, picked = norm_and_select(send, mine, swap(mine), node_feats, cotangent, gain)
    arrived = exchange(picked)
    products = edges_backward(recv, arrived, mask_t, mask, degree_rows, weight_in, weight_out, feats, act, gate)
    arrived = exchange(products)

    weight_sums = tail_sum(arrived, width // LANES * TILE)
    extra = weight_sums.shape[0]
    chunk = jnp.concatenate([weight_sums, gain_part], 0)
    mine = gather_sum(send, arrived, nodes, width)
    both, chunk = lax.optimization_barrier((mine + swap(mine), chunk))
    everyone = lax.all_to_all(
        jnp.broadcast_to(chunk[None], (owners,) + chunk.shape), "wide", split_axis=0, concat_axis=0, tiled=True
    )
    grad_nodes = cotangent.astype(F32) + both

    grad_gain = everyone[:, extra : extra + width // LANES].sum(0).reshape(width)
    held = everyone[:, :extra]
    theirs = swap(held)
    grads = jnp.stack([jnp.where(core == 0, held, theirs), jnp.where(core == 0, theirs, held)], 1)
    grads = grads.reshape(-1, LANES)
    grad_out = jnp.concatenate(jnp.split(grads[: inner * width // LANES], width // LANES), 1)
    grad_in = jnp.concatenate(jnp.split(grads[inner * width // LANES :], inner // LANES), 1)

    edge_factor = (degree.shape[0] * owners * lax.axis_size("narrow")) ** (-0.5)
    return (
        updated,
        grad_nodes,
        grad_in * edge_factor,
        grad_out * edge_factor,
        grad_gain * (nodes * owners) ** (-0.5),
    )


def solution(mesh):
    return jax.shard_map(
        shards,
        mesh=mesh,
        in_specs=(
            P("wide", None),
            P("wide", None, "narrow", None),
            P("wide", "narrow", None, None),
            P("wide", "narrow", None),
            P("wide", "narrow", None, None, None, None),
            P(("wide", "narrow")),
            P(),
            P(),
            P(),
            P("wide", None),
        ),
        out_specs=(P("wide", None), P("wide", None), P(), P(), P()),
        check_vma=False,
    )
```

time: 549 us -> 519 us (0.945)
  blocking collectives: 213 us -> 457 us
  waiting for transfers between devices: 224 us -> 5.14 us
  starting transfers between devices: 29.1 us -> 0.43 us
  Pallas kernels: 68.3 us -> 41 us
    all_to_all x2 -> x4, blocking collectives: 213 us -> 433 us  [exchange(): lax.all_to_all(tiles, ('wide', 'narrow'), split_axis=0, concat_axis=0, ti...]
    all_to_all x3 -> x0, waiting for transfers between devices: 220 us -> none  [the longest x2 209 us: exchange(): lax.all_to_all(tiles, ('wide', 'narrow'), split_axis=0, concat_axis=0, ti...]
    all_to_all x3 -> x0, starting transfers between devices: 28.9 us -> none  [the longest x2 19.8 us: exchange(): lax.all_to_all(tiles, ('wide', 'narrow'), split_axis=0, concat_axis=0, ti...]
    all_to_all x0 -> x1, blocking collectives: none -> 24 us  [shards(): lax.all_to_all(jnp.broadcast_to(chunk[None], (owners,) + chunk.shape), 'w...]
    pallas_call x4, Pallas kernels: 44.5 us -> 29.9 us  [the longest x1 14.5 us: edges_backward(): pl.pallas_call(backward_kernel, out_shape=jax.ShapeDtypeStruct((tiles, ro...]
  transfers between devices with their start and end apart: 7 -> 4, of which waited for: 5 -> 3; matrix products, arithmetic and copies ran while one was open for 1% -> 1% of each run, Pallas kernels for 2% -> 1%
where the time goes in v5:
time: 519 us; the launch traced here: 517 us
  blocking collectives  457 us (88%)
  Pallas kernels  41 us (8%)
  local copies, waits for them, and re-layouts  8.71 us (2%)
    all_to_all x4, blocking collectives, exchange(): lax.all_to_all(tiles, ('wide', 'narrow'), split_axis=0, concat_axis=0, ti...  433 us
    all_to_all x1, blocking collectives, shards(): lax.all_to_all(jnp.broadcast_to(chunk[None], (owners,) + chunk.shape), 'w...  24 us
    pallas_call x1, Pallas kernels, edges_backward(): pl.pallas_call(backward_kernel, out_shape=jax.ShapeDtypeStruct((tiles, ro...  14.5 us
    pallas_call x1, Pallas kernels, edges_forward(): pl.pallas_call(forward_kernel, out_shape=(jax.ShapeDtypeStruct((tiles, ro...  14.1 us
  transfers between devices with their start and end apart: 4, of which 3 were waited for; matrix products, arithmetic and copies ran while one was open for 1% of the time, Pallas kernels for 1%

profile of v5, /device:TPU:0, one launch (start us, length us, event | category | flops | bytes accessed | tf_op | source)
XLA Modules:
  0.0 516.9 jit_solution(17133361721395643577)
XLA Ops:
  0.6 0.8 dynamic-slice_bitcast_fusion.1
  1.4 0.0 collective-permute-start
  1.4 0.8 copy.19
  2.2 0.1 reshape.41.recv_ref
  2.3 0.0 copy-start.9
  2.3 1.1 copy-done.9
  3.4 0.0 copy-start.12
  3.4 0.7 copy-done.12
  4.0 2.8 unpack_masks.1
  6.9 0.0 copy-start
  6.9 2.0 copy-done
  8.9 0.0 copy-start.2
  8.9 1.9 copy-done.2
  10.8 0.0 collective-permute-done
  10.8 0.1 copy.18
  10.9 0.1 select_n.35.send_ref
  11.1 0.0 copy-start.4
  11.1 1.0 copy-done.4
  12.1 1.2 select_blocks.1
  13.3 0.0 copy-start.1
  13.3 0.0 copy-start.3
  13.3 0.0 copy-start.7
  13.3 0.0 copy-start.8
  13.3 0.0 copy-start.10
  13.3 109.5 %all_to_all.25.arrived = bf16[128,128,256]{2,1,0:T(8,128)(2,1)S(1)} all-to-all(bf16[128,128,256]{2,1,0:T(8,128)(2,1)S(1)} %select_blocks.1), channel_id=1, replica_groups=mesh['wide'=64,'narrow'=2] {'wide','narrow'}, dimensions={0} | all-to-all | bytes 16777216 | tf_op jit(solution)/shard_map/all_to_all | solution.py:312
  122.8 0.0 copy-done.1
  122.8 0.0 copy-done.3
  122.8 0.0 copy-done.7
  122.8 0.0 copy-done.8
  122.8 0.0 copy-done.10
  122.9 14.1 %edges_forward.1 = (bf16[128,256,128]{2,1,0:T(8,128)(2,1)S(1)}, bf16[2048,256]{1,0:T(8,128)(2,1)S(1)}, bf16[2048,512]{1,0:T(8,128)(2,1)S(1)}, f32[2048,512]{1,0:T(8,128)S(1)}) custom-call(s32[128]{0:T(128)S(1)} %reshape.41.recv_ref, bf16[128,128,256]{2,1,0:T(8,128)(2,1)S(1)} %all_to_all.25.arrived, bf16[128,128,128]{2,1,0:T(8,128)(2,1)S(1)} %copy-done.3, ...), custom_call_target="tpu_custom_call" | custom-call | tf_op jit(solution)/shard_map/edges_forward/pallas_call | solution.py:187
  137.0 105.9 %all_to_all.26.arrived = bf16[128,256,128]{2,1,0:T(8,128)(2,1)S(1)} all-to-all(bf16[128,256,128]{2,1,0:T(8,128)(2,1)S(1)} %get-tuple-element.26), channel_id=1, replica_groups=mesh['wide'=64,'narrow'=2] {'wide','narrow'}, dimensions={0} | all-to-all | bytes 16777216 | tf_op jit(solution)/shard_map/all_to_all | solution.py:312
  242.9 0.0 copy-start.5
  242.9 0.0 copy-start.6
  242.9 0.0 copy-start.11
  242.9 2.3 node_sums.2.mine_ref
  245.2 0.1 collective-permute-start.1
  245.3 2.6 collective-permute-done.1.other_ref
  247.9 0.0 copy-done.5
  247.9 0.0 copy-done.6
  247.9 0.0 copy-done.11
  247.9 3.6 norm_and_select.1
  251.6 105.9 %all_to_all.27.arrived = bf16[128,128,256]{2,1,0:T(8,128)(2,1)S(1)} all-to-all(bf16[128,128,256]{2,1,0:T(8,128)(2,1)S(1)} %get-tuple-element.28), channel_id=1, replica_groups=mesh['wide'=64,'narrow'=2] {'wide','narrow'}, dimensions={0} | all-to-all | bytes 16777216 | tf_op jit(solution)/shard_map/all_to_all | solution.py:312
  357.5 14.5 %edges_backward.1 = bf16[128,272,128]{2,1,0:T(8,128)(2,1)S(1)} custom-call(s32[128]{0:T(128)S(1)} %reshape.41.recv_ref, bf16[128,128,256]{2,1,0:T(8,128)(2,1)S(1)} %all_to_all.27.arrived, bf16[128,128,128]{2,1,0:T(8,128)(2,1)S(1)} %copy-done.3, bf16[128,128,128]{2,1,0:T(8,128)(2,1)S(1)} %copy-done.1, s32[16,128]{1,0:T(8,128)S(1)} %bitcast.29, ...), custom_call_target="tpu_custom_call" | custom-call | tf_op jit(solution)/shard_map/edges_backward/pallas_call | solution.py:211
  372.0 111.9 %all_to_all.28.arrived.arrived_ref = bf16[128,272,128]{2,1,0:T(8,128)(2,1)S(1)} all-to-all(bf16[128,272,128]{2,1,0:T(8,128)(2,1)S(1)} %edges_backward.1), channel_id=1, replica_groups=mesh['wide'=64,'narrow'=2] {'wide','narrow'}, dimensions={0} | all-to-all | bytes 17825792 | tf_op jit(solution)/shard_map/all_to_all | solution.py:312
  483.8 2.3 node_sums.3
  486.1 0.3 collective-permute-start.2
  486.4 0.2 weight_sums.1
  486.5 2.3 collective-permute-done.2
  488.9 0.1 add.16
  489.0 0.1 broadcast_in_dim.10
  489.1 24.0 %all_to_all.29 = f32[64,24,128]{2,1,0:T(8,128)S(1)} all-to-all(f32[64,24,128]{2,1,0:T(8,128)S(1)} %broadcast_in_dim.10), channel_id=1, replica_groups=mesh['wide'=64,'narrow'=2] {'wide'}, dimensions={0} | all-to-all | bytes 1572864 | tf_op jit(solution)/shard_map/all_to_all | solution.py:359
  513.1 0.1 collective-permute-start.3
  513.2 1.1 convert_add_fusion
  514.3 0.1 slice_reduce_fusion
  514.3 0.6 multiply_bitcast_fusion
  514.9 0.2 collective-permute-done.3
  515.1 0.1 select_bitcast_fusion.1
  515.3 0.8 maximum_multiply_fusion.1
  516.1 0.8 maximum_multiply_fusion
  (5 shorter events, 0.1 us)
Async XLA Ops:
  1.4 9.4 %collective-permute-start = (s32[64]{0:T(128)S(1)}, s32[64]{0:T(128)S(1)}, u32[]{:S(2)}, u32[]{:S(2)}) collective-permute-start(s32[64]{0:T(128)S(1)} %get-tuple-element.44), channel_id=1, source_target_pairs={{0,1},{1,0},{2,3},{3,2},{4,5},{5,4},{6,7},{7,6},{8,9},{9,8},{10,11... | collective-permute-start | bytes 776 | tf_op jit(solution)/shard_map/ppermute | solution.py:316
  2.3 1.1 copy-start.9
  3.4 0.7 copy-start.12
  6.9 2.0 copy-start
  8.9 1.9 copy-start.2
  11.1 1.0 copy-start.4
  13.3 109.6 %copy-start.1 = (bf16[128,128,128]{2,1,0:T(8,128)(2,1)S(1)}, bf16[128,128,128]{2,1,0:T(8,128)(2,1)}, u32[]{:S(2)}) copy-start(bf16[128,128,128]{2,1,0:T(8,128)(2,1)} %copy-done) | copy-start | bytes 12582916
  13.3 109.6 %copy-start.3 = (bf16[128,128,128]{2,1,0:T(8,128)(2,1)S(1)}, bf16[128,128,128]{2,1,0:T(8,128)(2,1)}, u32[]{:S(2)}) copy-start(bf16[128,128,128]{2,1,0:T(8,128)(2,1)} %copy-done.2) | copy-start | bytes 12582916
  13.3 109.5 %copy-start.7 = (bf16[256,512]{1,0:T(8,128)(2,1)S(1)}, bf16[256,512]{1,0:T(8,128)(2,1)}, u32[]{:S(2)}) copy-start(bf16[256,512]{1,0:T(8,128)(2,1)} %w_in_ref.3) | copy-start | bytes 786436
  13.3 109.5 %copy-start.8 = (bf16[512,256]{1,0:T(8,128)(2,1)S(1)}, bf16[512,256]{1,0:T(8,128)(2,1)}, u32[]{:S(2)}) copy-start(bf16[512,256]{1,0:T(8,128)(2,1)} %w_out_ref.3) | copy-start | bytes 786436
  13.3 109.5 %copy-start.10 = (s32[2048]{0:T(1024)S(1)}, s32[2048]{0:T(1024)}, u32[]{:S(2)}) copy-start(s32[2048]{0:T(1024)} %param.15) | copy-start | bytes 24580
  242.9 5.0 copy-start.5
  242.9 5.0 copy-start.6
  242.9 5.0 copy-start.11
  245.2 2.7 collective-permute-start.1
  486.1 2.7 collective-permute-start.2
  513.1 2.0 collective-permute-start.3

commit v6 on v5

--- a/solution.py
+++ b/solution.py
@@ -12,7 +12,9 @@
 TILE = 128
 LANES = 128
 STEP_TILES = 8
-PARAMS = pltpu.CompilerParams(vmem_limit_bytes=12 * 1024 * 1024)
+EDGE_TILES = 64
+EDGE_CHUNK = 1024
+PARAMS = pltpu.CompilerParams(vmem_limit_bytes=14 * 1024 * 1024)
 
 
 SMEM = pl.BlockSpec(memory_space=pltpu.SMEM)
@@ -27,7 +29,8 @@
     return pl.ds(pl.multiple_of(block * TILE, TILE), TILE)
 
 
-def unpack_kernel(count_ref, words_ref, mask_ref, mask_t_ref):
+def unpack_kernel(count_ref, words_ref, mask_ref, mask_t_ref, done_ref):
+    done_ref[...] = jnp.zeros_like(done_ref)
     step = pl.program_id(0)
     owners, words, slots, _ = words_ref.shape
     row = lax.broadcasted_iota(jnp.int32, (8, TILE), 0)
@@ -58,23 +61,23 @@
     block = pl.BlockSpec((per * slots, TILE, TILE), lambda i, c: (i, 0, 0))
     return pl.pallas_call(
         unpack_kernel,
-        out_shape=(out, out),
+        out_shape=(out, out, jax.ShapeDtypeStruct((8, LANES), F32)),
         grid_spec=pltpu.PrefetchScalarGridSpec(
             num_scalar_prefetch=1,
             grid=(owners // per,),
             in_specs=[pl.BlockSpec((per,) + words.shape[1:], lambda i, c: (i, 0, 0, 0))],
-            out_specs=(block, block),
+            out_specs=(block, block, pl.BlockSpec((8, LANES), lambda i, c: (0, 0))),
         ),
         compiler_params=PARAMS,
         name="unpack_masks",
     )(count, words)
 
 
-def steps_of(tiles):
-    return tiles.shape[0] // STEP_TILES
-
-
-def select_kernel(send_ref, rows_ref, out_ref):
+def steps_of(tiles, size=STEP_TILES):
+    return tiles.shape[0] // size
+
+
+def select_kernel(send_ref, rows_ref, _, out_ref):
     def body(i, carry):
         for tile in range(STEP_TILES):
             out_ref[i * STEP_TILES + tile] = rows_ref[rows_at(send_ref[i * STEP_TILES + tile])]
@@ -83,44 +86,44 @@
     lax.fori_loop(0, steps_of(out_ref), body, 0)
 
 
-def select(send, rows):
+def select(send, rows, after):
     return pl.pallas_call(
         select_kernel,
         out_shape=jax.ShapeDtypeStruct((send.shape[0], TILE, rows.shape[1]), BF16),
-        in_specs=[SMEM, VMEM],
+        in_specs=[SMEM, VMEM, VMEM],
         out_specs=VMEM,
         compiler_params=PARAMS,
         name="select_blocks",
-    )(send, rows)
+    )(send, rows, after)
 
 
 def collect(recv_ref, arrived, mask_t, acc):
     acc[...] = jnp.zeros_like(acc)
 
     def body(i, carry):
-        for tile in range(STEP_TILES):
-            where = rows_at(recv_ref[i * STEP_TILES + tile])
-            acc[where] += dot(mask_t[i * STEP_TILES + tile], arrived[i * STEP_TILES + tile])
-        return carry
-
-    lax.fori_loop(0, steps_of(arrived), body, 0)
+        for tile in range(EDGE_TILES):
+            where = rows_at(recv_ref[i * EDGE_TILES + tile])
+            acc[where] += dot(mask_t[i * EDGE_TILES + tile], arrived[i * EDGE_TILES + tile])
+        return carry
+
+    lax.fori_loop(0, steps_of(arrived, EDGE_TILES), body, 0)
 
 
 def spread(recv_ref, mask, values, made, grads=None):
     def body(i, carry):
-        for tile in range(STEP_TILES):
-            where = rows_at(recv_ref[i * STEP_TILES + tile])
-            product = dot(mask[i * STEP_TILES + tile], values[where]).astype(BF16)
+        for tile in range(EDGE_TILES):
+            where = rows_at(recv_ref[i * EDGE_TILES + tile])
+            product = dot(mask[i * EDGE_TILES + tile], values[where]).astype(BF16)
             for h in range(product.shape[1] // LANES):
-                made[i * STEP_TILES + tile, h * TILE : (h + 1) * TILE] = product[:, h * LANES : (h + 1) * LANES]
+                made[i * EDGE_TILES + tile, h * TILE : (h + 1) * TILE] = product[:, h * LANES : (h + 1) * LANES]
             if grads is not None:
                 first = product.shape[1] // LANES * TILE
                 extra = made.shape[1] - first
-                at = pl.ds(pl.multiple_of((i * STEP_TILES + tile) * extra, extra), extra)
-                made[i * STEP_TILES + tile, first:] = grads[at].astype(BF16)
-        return carry
-
-    lax.fori_loop(0, steps_of(made), body, 0)
+                at = pl.ds(pl.multiple_of((i * EDGE_TILES + tile) * extra, extra), extra)
+                made[i * EDGE_TILES + tile, first:] = grads[at].astype(BF16)
+        return carry
+
+    lax.fori_loop(0, steps_of(made, EDGE_TILES), body, 0)
 
 
 def scaled(rows, degree_ref, i):
@@ -138,7 +141,7 @@
     recv_ref, arrived, mask_t, mask, degree_ref, w_in_ref, w_out_ref, made, feats, act, gate, acc, values
 ):
     collect(recv_ref, arrived, mask_t, acc)
-    chunk = 256
+    chunk = min(EDGE_CHUNK, acc.shape[0])
 
     def body(i, carry):
         at = pl.ds(pl.multiple_of(i * chunk, chunk), chunk)
@@ -161,7 +164,7 @@
 ):
     grads[...] = jnp.zeros_like(grads)
     collect(recv_ref, arrived, mask_t, acc)
-    chunk = 256
+    chunk = min(EDGE_CHUNK, acc.shape[0])
 
     def body(i, carry):
         at = pl.ds(pl.multiple_of(i * chunk, chunk), chunk)
@@ -283,11 +286,12 @@
 
     parts = lax.fori_loop(0, mine_ref.shape[0] // TILE, body, jnp.zeros((8, mine_ref.shape[1]), F32))
     row = jnp.sum(parts, axis=0, keepdims=True)
-    part_ref[...] = jnp.zeros_like(part_ref)
-    for i in range(row.shape[1] // LANES):
-        part_ref[i : i + 1] = row[:, i * LANES : (i + 1) * LANES]
-
-    select_kernel(send_ref, d_summed, out_ref)
+    high = row.astype(BF16).astype(F32)
+    rows = [part[:, i : i + LANES] for part in (high, row - high) for i in range(0, row.shape[1], LANES)]
+    rows.append(jnp.zeros((part_ref.shape[0] - len(rows), LANES), F32))
+    part_ref[...] = jnp.concatenate(rows, axis=0).astype(BF16)
+
+    select_kernel(send_ref, d_summed, None, out_ref)
 
 
 def norm_and_select(send, mine, other, feats, cot, gain):
@@ -296,7 +300,7 @@
         norm_kernel,
         out_shape=(
             jax.ShapeDtypeStruct((nodes, width), BF16),
-            jax.ShapeDtypeStruct((8, LANES), F32),
+            jax.ShapeDtypeStruct((16, LANES), BF16),
             jax.ShapeDtypeStruct((send.shape[0], TILE, width), BF16),
         ),
         in_specs=[SMEM] + [VMEM] * 5,
@@ -342,7 +346,8 @@
     degree_rows = degree.reshape(-1, LANES)
     gain = norm_gain[None, :]
 
-    picked, mask, mask_t, recv = lax.optimization_barrier((select(send, node_feats), *unpack(count, words), recv))
+    mask, mask_t, unpacked = unpack(count, words)
+    picked, recv = lax.optimization_barrier((select(send, node_feats, unpacked), recv))
     arrived = exchange(picked)
     products, feats, act, gate = edges_forward(recv, arrived, mask_t, mask, degree_rows, weight_in, weight_out)
     mine = gather_sum(send, exchange(products), nodes, width)
@@ -353,19 +358,21 @@
 
     weight_sums = tail_sum(arrived, width // LANES * TILE)
     extra = weight_sums.shape[0]
-    chunk = jnp.concatenate([weight_sums, gain_part], 0)
+    gain_rows = width // LANES
+    chunk = jnp.concatenate([weight_sums.astype(BF16), gain_part[: max(8, 2 * gain_rows)]], 0)
     mine = gather_sum(send, arrived, nodes, width)
-    both, chunk = lax.optimization_barrier((mine + swap(mine), chunk))
+    grad_nodes = cotangent.astype(F32) + (mine + swap(mine))
+    grad_nodes, chunk = lax.optimization_barrier((grad_nodes, chunk))
     everyone = lax.all_to_all(
         jnp.broadcast_to(chunk[None], (owners,) + chunk.shape), "wide", split_axis=0, concat_axis=0, tiled=True
     )
-    grad_nodes = cotangent.astype(F32) + both
-
-    grad_gain = everyone[:, extra : extra + width // LANES].sum(0).reshape(width)
+
+    gains = everyone[:, extra : extra + 2 * gain_rows].astype(F32).sum(0)
+    grad_gain = (gains[:gain_rows] + gains[gain_rows:]).reshape(width)
     held = everyone[:, :extra]
     theirs = swap(held)
     grads = jnp.stack([jnp.where(core == 0, held, theirs), jnp.where(core == 0, theirs, held)], 1)
-    grads = grads.reshape(-1, LANES)
+    grads = grads.reshape(-1, LANES).astype(F32)
     grad_out = jnp.concatenate(jnp.split(grads[: inner * width // LANES], width // LANES), 1)
     grad_in = jnp.concatenate(jnp.split(grads[inner * width // LANES :], inner // LANES), 1)
 

time: 519 us -> 504 us (0.971)
  Pallas kernels: 41 us -> 28.9 us
    pallas_call x1, Pallas kernels: 14.1 us -> 7.93 us  [edges_forward(): pl.pallas_call(forward_kernel, out_shape=(jax.ShapeDtypeStruct((tiles, ro...]
    pallas_call x1, Pallas kernels: 14.5 us -> 8.62 us  [edges_backward(): pl.pallas_call(backward_kernel, out_shape=jax.ShapeDtypeStruct((tiles, ro...]
  transfers between devices with their start and end apart: 4 -> 4, of which waited for: 3 -> 3; matrix products, arithmetic and copies ran while one was open for 1% -> 0% of each run, Pallas kernels for 1% -> 1%
where the time goes in v6:
time: 504 us; the launch traced here: 503 us
  blocking collectives  454 us (90%)
  Pallas kernels  28.9 us (6%)
  local copies, waits for them, and re-layouts  8.7 us (2%)
  waiting for transfers between devices  5.81 us (1%)
    all_to_all x4, blocking collectives, exchange(): lax.all_to_all(tiles, ('wide', 'narrow'), split_axis=0, concat_axis=0, ti...  433 us
    all_to_all x1, blocking collectives, shards(): lax.all_to_all(jnp.broadcast_to(chunk[None], (owners,) + chunk.shape), 'w...  20.8 us
  transfers between devices with their start and end apart: 4, of which 3 were waited for; matrix products, arithmetic and copies ran while one was open for 0% of the time, Pallas kernels for 1%

profile of v6, /device:TPU:0, one launch (start us, length us, event | category | flops | bytes accessed | tf_op | source)
XLA Modules:
  0.0 502.5 jit_solution(8659167322668125157)
XLA Ops:
  0.6 0.8 dynamic-slice_bitcast_fusion.1
  1.4 0.0 collective-permute-start
  1.4 0.8 copy.19
  2.2 0.1 reshape.40.recv_ref
  2.3 0.0 copy-start.9
  2.3 1.1 copy-done.9
  3.4 0.0 copy-start.12
  3.4 0.7 copy-done.12
  4.0 2.8 unpack_masks.1
  6.9 0.0 copy-start
  6.9 2.0 copy-done
  8.9 0.0 copy-start.2
  8.9 1.9 copy-done.2
  10.8 0.0 collective-permute-done
  10.8 0.1 copy.18
  10.9 0.1 select_n.35.send_ref
  11.1 0.0 copy-start.4
  11.1 1.0 copy-done.4
  12.1 1.2 select_blocks.1
  13.3 0.0 copy-start.1
  13.3 0.0 copy-start.3
  13.3 0.0 copy-start.7
  13.3 0.0 copy-start.8
  13.3 0.0 copy-start.10
  13.3 109.5 %all_to_all.25.arrived = bf16[128,128,256]{2,1,0:T(8,128)(2,1)S(1)} all-to-all(bf16[128,128,256]{2,1,0:T(8,128)(2,1)S(1)} %select_blocks.1), channel_id=1, replica_groups=mesh['wide'=64,'narrow'=2] {'wide','narrow'}, dimensions={0} | all-to-all | bytes 16777216 | tf_op jit(solution)/shard_map/all_to_all | solution.py:316
  122.8 0.0 copy-done.1
  122.8 0.0 copy-done.3
  122.8 0.0 copy-done.7
  122.8 0.0 copy-done.8
  122.8 0.0 copy-done.10
  122.9 7.9 %edges_forward.1 = (bf16[128,256,128]{2,1,0:T(8,128)(2,1)S(1)}, bf16[2048,256]{1,0:T(8,128)(2,1)S(1)}, bf16[2048,512]{1,0:T(8,128)(2,1)S(1)}, f32[2048,512]{1,0:T(8,128)S(1)}) custom-call(s32[128]{0:T(128)S(1)} %reshape.40.recv_ref, bf16[128,128,256]{2,1,0:T(8,128)(2,1)S(1)} %all_to_all.25.arrived, bf16[128,128,128]{2,1,0:T(8,128)(2,1)S(1)} %copy-done.3, ...), custom_call_target="tpu_custom_call" | custom-call | tf_op jit(solution)/shard_map/edges_forward/pallas_call | solution.py:190
  130.8 105.9 %all_to_all.26.arrived = bf16[128,256,128]{2,1,0:T(8,128)(2,1)S(1)} all-to-all(bf16[128,256,128]{2,1,0:T(8,128)(2,1)S(1)} %get-tuple-element.24), channel_id=1, replica_groups=mesh['wide'=64,'narrow'=2] {'wide','narrow'}, dimensions={0} | all-to-all | bytes 16777216 | tf_op jit(solution)/shard_map/all_to_all | solution.py:316
  236.7 0.0 copy-start.5
  236.7 0.0 copy-start.6
  236.7 0.0 copy-start.11
  236.7 2.3 node_sums.2.mine_ref
  239.0 0.1 collective-permute-start.1
  239.1 2.6 collective-permute-done.1.other_ref
  241.7 0.0 copy-done.5
  241.7 0.0 copy-done.6
  241.7 0.0 copy-done.11
  241.7 3.7 norm_and_select.1
  245.4 105.9 %all_to_all.27.arrived = bf16[128,128,256]{2,1,0:T(8,128)(2,1)S(1)} all-to-all(bf16[128,128,256]{2,1,0:T(8,128)(2,1)S(1)} %get-tuple-element.26), channel_id=1, replica_groups=mesh['wide'=64,'narrow'=2] {'wide','narrow'}, dimensions={0} | all-to-all | bytes 16777216 | tf_op jit(solution)/shard_map/all_to_all | solution.py:316
  351.3 8.6 %edges_backward.1 = bf16[128,272,128]{2,1,0:T(8,128)(2,1)S(1)} custom-call(s32[128]{0:T(128)S(1)} %reshape.40.recv_ref, bf16[128,128,256]{2,1,0:T(8,128)(2,1)S(1)} %all_to_all.27.arrived, bf16[128,128,128]{2,1,0:T(8,128)(2,1)S(1)} %copy-done.3, bf16[128,128,128]{2,1,0:T(8,128)(2,1)S(1)} %copy-done.1, s32[16,128]{1,0:T(8,128)S(1)} %bitcast.29, ...), custom_call_target="tpu_custom_call" | custom-call | tf_op jit(solution)/shard_map/edges_backward/pallas_call | solution.py:214
  359.9 112.1 %all_to_all.28.arrived.arrived_ref = bf16[128,272,128]{2,1,0:T(8,128)(2,1)S(1)} all-to-all(bf16[128,272,128]{2,1,0:T(8,128)(2,1)S(1)} %edges_backward.1), channel_id=1, replica_groups=mesh['wide'=64,'narrow'=2] {'wide','narrow'}, dimensions={0} | all-to-all | bytes 17825792 | tf_op jit(solution)/shard_map/all_to_all | solution.py:316
  472.0 2.3 node_sums.3
  474.3 0.3 collective-permute-start.2
  474.6 0.2 weight_sums.1
  474.8 2.3 collective-permute-done.2
  477.0 1.1 add_add_fusion
  478.2 0.1 broadcast_in_dim.10
  478.2 20.8 %all_to_all.29 = bf16[64,24,128]{2,1,0:T(8,128)(2,1)S(1)} all-to-all(bf16[64,24,128]{2,1,0:T(8,128)(2,1)S(1)} %broadcast_in_dim.10), channel_id=1, replica_groups=mesh['wide'=64,'narrow'=2] {'wide'}, dimensions={0} | all-to-all | bytes 786432 | tf_op jit(solution)/shard_map/all_to_all | solution.py:366
  499.1 0.1 collective-permute-start.3
  499.2 0.1 convert_reduce_fusion
  499.3 0.6 multiply_bitcast_fusion
  499.8 0.9 collective-permute-done.3
  500.9 0.8 maximum_multiply_fusion.1
  501.7 0.8 maximum_multiply_fusion
  (8 shorter events, 0.2 us)
Async XLA Ops:
  1.4 9.4 %collective-permute-start = (s32[64]{0:T(128)S(1)}, s32[64]{0:T(128)S(1)}, u32[]{:S(2)}, u32[]{:S(2)}) collective-permute-start(s32[64]{0:T(128)S(1)} %get-tuple-element.42), channel_id=1, source_target_pairs={{0,1},{1,0},{2,3},{3,2},{4,5},{5,4},{6,7},{7,6},{8,9},{9,8},{10,11... | collective-permute-start | bytes 776 | tf_op jit(solution)/shard_map/ppermute | solution.py:320
  2.3 1.1 copy-start.9
  3.4 0.7 copy-start.12
  6.9 2.0 copy-start
  8.9 1.9 copy-start.2
  11.1 1.0 copy-start.4
  13.3 109.6 %copy-start.1 = (bf16[128,128,128]{2,1,0:T(8,128)(2,1)S(1)}, bf16[128,128,128]{2,1,0:T(8,128)(2,1)}, u32[]{:S(2)}) copy-start(bf16[128,128,128]{2,1,0:T(8,128)(2,1)} %copy-done) | copy-start | bytes 12582916
  13.3 109.6 %copy-start.3 = (bf16[128,128,128]{2,1,0:T(8,128)(2,1)S(1)}, bf16[128,128,128]{2,1,0:T(8,128)(2,1)}, u32[]{:S(2)}) copy-start(bf16[128,128,128]{2,1,0:T(8,128)(2,1)} %copy-done.2) | copy-start | bytes 12582916
  13.3 109.5 %copy-start.7 = (bf16[256,512]{1,0:T(8,128)(2,1)S(1)}, bf16[256,512]{1,0:T(8,128)(2,1)}, u32[]{:S(2)}) copy-start(bf16[256,512]{1,0:T(8,128)(2,1)} %w_in_ref.3) | copy-start | bytes 786436
  13.3 109.5 %copy-start.8 = (bf16[512,256]{1,0:T(8,128)(2,1)S(1)}, bf16[512,256]{1,0:T(8,128)(2,1)}, u32[]{:S(2)}) copy-start(bf16[512,256]{1,0:T(8,128)(2,1)} %w_out_ref.3) | copy-start | bytes 786436
  13.3 109.5 %copy-start.10 = (s32[2048]{0:T(1024)S(1)}, s32[2048]{0:T(1024)}, u32[]{:S(2)}) copy-start(s32[2048]{0:T(1024)} %param.15) | copy-start | bytes 24580
  236.7 5.0 %copy-start.5 = (bf16[1024,256]{1,0:T(8,128)(2,1)S(1)}, bf16[1024,256]{1,0:T(8,128)(2,1)}, u32[]{:S(2)}) copy-start(bf16[1024,256]{1,0:T(8,128)(2,1)} %feats_ref.1) | copy-start | bytes 1572868
  236.7 5.0 %copy-start.6 = (bf16[1024,256]{1,0:T(8,128)(2,1)S(1)}, bf16[1024,256]{1,0:T(8,128)(2,1)}, u32[]{:S(2)}) copy-start(bf16[1024,256]{1,0:T(8,128)(2,1)} %cot_ref.1) | copy-start | bytes 1572868
  236.7 5.0 %copy-start.11 = (f32[256]{0:T(256)S(1)}, f32[256]{0:T(256)}, u32[]{:S(2)}) copy-start(f32[256]{0:T(256)} %param.18) | copy-start | bytes 3076
  239.0 2.7 collective-permute-start.1
  474.3 2.7 collective-permute-start.2
  499.1 1.6 collective-permute-start.3

commit v7 on v6

v7 whole, which is shorter than its diff:
```python
import functools

import jax
import jax.numpy as jnp
from jax import lax
from jax.experimental import pallas as pl
from jax.experimental.pallas import tpu as pltpu
from jax.sharding import PartitionSpec as P

F32 = jnp.float32
BF16 = jnp.bfloat16
TILE = 128
HALF = TILE // 2
LANES = 128
STEP_TILES = 8
EDGE_TILES = 64
EDGE_CHUNK = 1024
PARAMS = pltpu.CompilerParams(vmem_limit_bytes=14 * 1024 * 1024)


SMEM = pl.BlockSpec(memory_space=pltpu.SMEM)
VMEM = pl.BlockSpec(memory_space=pltpu.VMEM)


def dot(a, b, dims=((1,), (0,))):
    return lax.dot_general(a, b, (dims, ((), ())), preferred_element_type=F32)


def rows_at(block):
    return pl.ds(pl.multiple_of(block * TILE, TILE), TILE)


def unpack_tile(word, row):
    groups = []
    for first in range(0, TILE, 8):
        low, high = first // 15, (first + 7) // 15
        picked = word[low]
        shift = row + (first - low * 15)
        if high != low:
            later = row >= high * 15 - first
            picked = jnp.where(later, word[high], picked)
            shift = jnp.where(later, shift - 15, shift)
        groups.append((jnp.right_shift(picked, shift) & 1).astype(F32))
    return jnp.concatenate(groups, axis=0)


def unpack(count_ref, words_ref, mask_ref, mask_t_ref):
    owners, words, slots, _ = words_ref.shape
    per = 8

    def body(i, carry):
        row = lax.broadcasted_iota(jnp.int32, (8, TILE), 0)
        for k in range(per):
            owner = i * per + k
            count = count_ref[owner]
            for slot in range(slots):
                live = jnp.where(count > slot, jnp.int32(-1), jnp.int32(0))
                word = [
                    jnp.broadcast_to(words_ref[owner, j, slot : slot + 1], (8, TILE)) & live for j in range(words)
                ]
                mask = unpack_tile(word, row)
                mask_ref[owner * slots + slot] = mask.astype(BF16)
                mask_t_ref[owner * slots + slot] = mask.T.astype(BF16)
        return carry

    lax.fori_loop(0, owners // per, body, 0)


def steps_of(tiles, size=STEP_TILES):
    return tiles.shape[0] // size


def half_at(block):
    return pl.ds(pl.multiple_of(block * HALF, HALF), HALF)


def select_kernel(send_ref, rows_ref, out_ref):
    slots = out_ref.shape[1] // HALF

    def body(i, carry):
        for tile in range(STEP_TILES):
            for k in range(slots):
                block = send_ref[(i * STEP_TILES + tile) * slots + k]
                out_ref[i * STEP_TILES + tile, k * HALF : (k + 1) * HALF] = rows_ref[half_at(block)]
        return carry

    lax.fori_loop(0, steps_of(out_ref), body, 0)


def select(send, rows, devices):
    return pl.pallas_call(
        select_kernel,
        out_shape=jax.ShapeDtypeStruct((devices, send.shape[0] // devices * HALF, rows.shape[1]), BF16),
        in_specs=[SMEM, VMEM],
        out_specs=VMEM,
        compiler_params=PARAMS,
        name="select_blocks",
    )(send, rows)


def collect(recv_ref, arrived, mask_t, acc):
    acc[...] = jnp.zeros_like(acc)

    def body(i, carry):
        for k in range(EDGE_TILES):
            tile = i * EDGE_TILES + k
            owner, slot = i * (EDGE_TILES // 2) + k // 2, k % 2
            halves = [arrived[2 * owner + c, slot * HALF : (slot + 1) * HALF] for c in range(2)]
            acc[rows_at(recv_ref[tile])] += dot(mask_t[tile], jnp.concatenate(halves, axis=0))
        return carry

    lax.fori_loop(0, steps_of(arrived, EDGE_TILES), body, 0)


def spread(recv_ref, mask, values, made, grads=None):
    pieces = values.shape[1] // LANES
    first = 2 * pieces * HALF

    def body(i, carry):
        for k in range(EDGE_TILES):
            tile = i * EDGE_TILES + k
            owner, slot = i * (EDGE_TILES // 2) + k // 2, k % 2
            product = dot(mask[tile], values[rows_at(recv_ref[tile])]).astype(BF16)
            for c in range(2):
                for h in range(pieces):
                    at = (slot * pieces + h) * HALF
                    made[2 * owner + c, at : at + HALF] = product[
                        c * HALF : (c + 1) * HALF, h * LANES : (h + 1) * LANES
                    ]
            if grads is not None:
                extra = made.shape[1] - first
                made[tile, first:] = grads[pl.ds(pl.multiple_of(tile * extra, extra), extra)].astype(BF16)
        return carry

    lax.fori_loop(0, steps_of(made, EDGE_TILES), body, 0)


def scaled(rows, degree_ref, i):
    blocks = rows.shape[0] // TILE
    parts = []
    for k in range(blocks):
        scale = lax.rsqrt(degree_ref[pl.ds(i * blocks + k, 1)].astype(F32))
        scale = jnp.broadcast_to(scale, (TILE, LANES)).T
        lanes = [rows[k * TILE : (k + 1) * TILE, j : j + LANES] * scale for j in range(0, rows.shape[1], LANES)]
        parts.append(jnp.concatenate(lanes, axis=1))
    return jnp.concatenate(parts, axis=0)


def forward_kernel(
    recv_ref, count_ref, arrived, words_ref, degree_ref, w_in_ref, w_out_ref,
    made, mask_t, mask, feats, act, gate, acc, values,
):
    unpack(count_ref, words_ref, mask, mask_t)
    collect(recv_ref, arrived, mask_t, acc)
    chunk = min(EDGE_CHUNK, acc.shape[0])

    def body(i, carry):
        at = pl.ds(pl.multiple_of(i * chunk, chunk), chunk)
        rows = scaled(acc[at], degree_ref, i).astype(BF16)
        feats[at] = rows
        pre = dot(rows, w_in_ref[...])
        sig = jax.nn.sigmoid(pre)
        hidden = (pre * sig).astype(BF16)
        act[at] = hidden
        gate[at] = sig * (1.0 + pre * (1.0 - sig))
        values[at] = dot(hidden, w_out_ref[...]).astype(BF16)
        return carry

    lax.fori_loop(0, acc.shape[0] // chunk, body, 0)
    spread(recv_ref, mask, values, made)


def backward_kernel(
    recv_ref, arrived, mask_t, mask, degree_ref, w_in_ref, w_out_ref, feats, act, gate, made, acc, values, grads
):
    grads[...] = jnp.zeros_like(grads)
    collect(recv_ref, arrived, mask_t, acc)
    chunk = min(EDGE_CHUNK, acc.shape[0])

    def body(i, carry):
        at = pl.ds(pl.multiple_of(i * chunk, chunk), chunk)
        d_edge = acc[at].astype(BF16)
        d_act = dot(d_edge, w_out_ref[...], ((1,), (1,)))
        d_pre = (d_act * gate[at]).astype(BF16)
        values[at] = scaled(dot(d_pre, w_in_ref[...], ((1,), (1,))), degree_ref, i).astype(BF16)
        first = 0
        for grad in (dot(act[at], d_edge, ((0,), (0,))), dot(feats[at], d_pre, ((0,), (0,)))):
            for lane in range(0, grad.shape[1], LANES):
                grads[first : first + grad.shape[0]] += grad[:, lane : lane + LANES]
                first += grad.shape[0]
        return carry

    lax.fori_loop(0, acc.shape[0] // chunk, body, 0)
    spread(recv_ref, mask, values, made, grads)


def edges_forward(recv, count, arrived, words, degree, w_in, w_out):
    tiles = arrived.shape[0]
    edges, width, inner = degree.size, w_in.shape[0], w_in.shape[1]
    rows = width // LANES * TILE
    return pl.pallas_call(
        forward_kernel,
        out_shape=(
            jax.ShapeDtypeStruct((tiles, rows, LANES), BF16),
            jax.ShapeDtypeStruct((tiles, TILE, TILE), BF16),
            jax.ShapeDtypeStruct((tiles, TILE, TILE), BF16),
            jax.ShapeDtypeStruct((edges, width), BF16),
            jax.ShapeDtypeStruct((edges, inner), BF16),
            jax.ShapeDtypeStruct((edges, inner), F32),
        ),
        in_specs=[SMEM] * 2 + [VMEM] * 5,
        out_specs=(VMEM,) * 6,
        scratch_shapes=[
            pltpu.VMEM((edges, width), F32),
            pltpu.VMEM((edges, width), BF16),
        ],
        compiler_params=PARAMS,
        name="edges_forward",
    )(recv, count, arrived, words, degree, w_in, w_out)


def edges_backward(recv, arrived, mask_t, mask, degree, w_in, w_out, feats, act, gate):
    tiles = arrived.shape[0]
    edges, width, inner = degree.size, w_in.shape[0], w_in.shape[1]
    grad_rows = 2 * inner * width // LANES
    rows = width // LANES * TILE + grad_rows // tiles
    return pl.pallas_call(
        backward_kernel,
        out_shape=jax.ShapeDtypeStruct((tiles, rows, LANES), BF16),
        in_specs=[SMEM] + [VMEM] * 9,
        out_specs=VMEM,
        scratch_shapes=[
            pltpu.VMEM((edges, width), F32),
            pltpu.VMEM((edges, width), BF16),
            pltpu.VMEM((grad_rows, LANES), F32),
        ],
        compiler_params=PARAMS,
        name="edges_backward",
    )(recv, arrived, mask_t, mask, degree, w_in, w_out, feats, act, gate)


def sum_products(send_ref, arrived, acc):
    pieces = acc.shape[1] // LANES
    acc[...] = jnp.zeros_like(acc)

    def body(i, carry):
        for k in range(2 * STEP_TILES):
            source, slot = i * STEP_TILES + k // 2, k % 2
            where = half_at(send_ref[2 * source + slot])
            for h in range(pieces):
                at = (slot * pieces + h) * HALF
                acc[where, h * LANES : (h + 1) * LANES] += arrived[source, at : at + HALF].astype(F32)
        return carry

    lax.fori_loop(0, steps_of(arrived), body, 0)


def grad_kernel(send_ref, arrived, cot_ref, out_ref, acc):
    sum_products(send_ref, arrived, acc)
    out_ref[...] = cot_ref[...].astype(F32) + acc[...]


def node_grads(send, arrived, cot):
    return pl.pallas_call(
        grad_kernel,
        out_shape=jax.ShapeDtypeStruct(cot.shape, F32),
        in_specs=[SMEM, VMEM, VMEM],
        out_specs=VMEM,
        scratch_shapes=[pltpu.VMEM(cot.shape, F32)],
        compiler_params=PARAMS,
        name="node_grads",
    )(send, arrived, cot)


def tail_sum_kernel(arrived_ref, out_ref):
    rows = out_ref.shape[0]
    out_ref[...] = jnp.sum(arrived_ref[:, arrived_ref.shape[1] - rows :].astype(F32), axis=0)


def tail_sum(arrived, rows):
    return pl.pallas_call(
        tail_sum_kernel,
        out_shape=jax.ShapeDtypeStruct((arrived.shape[1] - rows, arrived.shape[2]), F32),
        in_specs=[VMEM],
        out_specs=VMEM,
        compiler_params=PARAMS,
        name="weight_sums",
    )(arrived)


def norm_kernel(
    send_ref, arrived, feats_ref, cot_ref, gain_ref, updated_ref, part_ref, out_ref, acc, d_summed
):
    sum_products(send_ref, arrived, acc)
    gain = gain_ref[...]

    def body(i, part):
        at = rows_at(i)
        summed = acc[at]
        inv_rms = lax.rsqrt(jnp.mean(summed * summed, axis=-1, keepdims=True) + 1e-05)
        normed = summed * inv_rms
        updated_ref[at] = (feats_ref[at].astype(F32) + normed * gain).astype(BF16)
        upstream = cot_ref[at].astype(F32)
        d_normed = upstream * gain
        inner = jnp.mean(d_normed * normed, axis=-1, keepdims=True)
        d_summed[at] = (inv_rms * (d_normed - normed * inner)).astype(BF16)
        return part + jnp.sum((upstream * normed).reshape(TILE // 8, 8, -1), axis=0)

    parts = lax.fori_loop(0, acc.shape[0] // TILE, body, jnp.zeros((8, acc.shape[1]), F32))
    row = jnp.sum(parts, axis=0, keepdims=True)
    high = row.astype(BF16).astype(F32)
    rows = [part[:, i : i + LANES] for part in (high, row - high) for i in range(0, row.shape[1], LANES)]
    rows.append(jnp.zeros((part_ref.shape[0] - len(rows), LANES), F32))
    part_ref[...] = jnp.concatenate(rows, axis=0).astype(BF16)

    select_kernel(send_ref, d_summed, out_ref)


def norm_and_select(send, arrived, feats, cot, gain):
    nodes, width = feats.shape
    devices = arrived.shape[0]
    return pl.pallas_call(
        norm_kernel,
        out_shape=(
            jax.ShapeDtypeStruct((nodes, width), BF16),
            jax.ShapeDtypeStruct((16, LANES), BF16),
            jax.ShapeDtypeStruct((devices, send.shape[0] // devices * HALF, width), BF16),
        ),
        in_specs=[SMEM] + [VMEM] * 4,
        out_specs=(VMEM,) * 3,
        scratch_shapes=[pltpu.VMEM((nodes, width), F32), pltpu.VMEM((nodes, width), BF16)],
        compiler_params=PARAMS,
        name="norm_and_select",
    )(send, arrived, feats, cot, gain)


def exchange(tiles):
    return lax.all_to_all(tiles, ("wide", "narrow"), split_axis=0, concat_axis=0, tiled=True)


def swap(rows):
    return lax.ppermute(rows, "narrow", [(0, 1), (1, 0)])


def shards(
    node_feats,
    send_block,
    recv_block,
    tile_count,
    mask_bits,
    degree,
    weight_in,
    weight_out,
    norm_gain,
    cotangent,
):
    owners = lax.axis_size("wide")
    nodes, width = node_feats.shape
    inner = weight_in.shape[1]
    core = lax.axis_index("narrow")
    devices = 2 * owners
    by_core = lambda mine, theirs: (jnp.where(core == 0, mine, theirs), jnp.where(core == 0, theirs, mine))
    my_slots = send_block[0, :, 0, :]
    send = jnp.stack(by_core(my_slots, swap(my_slots)), 1).reshape(-1)
    recv = recv_block.reshape(-1)
    count = tile_count.reshape(-1)
    words = mask_bits[0, 0].transpose(0, 2, 1, 3)
    degree_rows = degree.reshape(-1, LANES)
    half_of = lambda rows: lax.dynamic_index_in_dim(
        rows.reshape(-1, 2, HALF, width), core, 1, keepdims=False
    ).reshape(-1, width)
    whole_of = lambda mine, theirs: jnp.stack(
        [half.reshape(-1, HALF, width) for half in by_core(mine, theirs)], 1
    ).reshape(nodes, width)

    feats_half, cot_half = half_of(node_feats), half_of(cotangent)
    picked, recv, count, words, cot_half = lax.optimization_barrier(
        (select(send, feats_half, devices), recv, count, words, cot_half)
    )
    arrived = exchange(picked)
    products, mask_t, mask, feats, act, gate = edges_forward(
        recv, count, arrived, words, degree_rows, weight_in, weight_out
    )
    updated, gain_part, picked = norm_and_select(send, exchange(products), feats_half, cot_half, norm_gain[None, :])
    arrived = exchange(picked)
    products = edges_backward(recv, arrived, mask_t, mask, degree_rows, weight_in, weight_out, feats, act, gate)
    arrived = exchange(products)

    arrived, updated, gain_part = lax.optimization_barrier((arrived, updated, gain_part))
    weight_sums = tail_sum(arrived, 2 * width // LANES * HALF)
    extra = weight_sums.shape[0]
    gain_rows = width // LANES
    chunk = jnp.concatenate([weight_sums.astype(BF16), gain_part[: max(8, 2 * gain_rows)]], 0)
    grads_half = node_grads(send, arrived, cot_half)
    grads_other, updated_other, chunk = lax.optimization_barrier((swap(grads_half), swap(updated), chunk))
    everyone = lax.all_to_all(
        jnp.broadcast_to(chunk[None], (owners,) + chunk.shape), "wide", split_axis=0, concat_axis=0, tiled=True
    )
    grad_nodes = whole_of(grads_half, grads_other)
    updated = whole_of(updated, updated_other)

    theirs = swap(everyone)
    gains = (everyone[:, extra : extra + 2 * gain_rows], theirs[:, extra : extra + 2 * gain_rows])
    gains = sum(g.astype(F32).sum(0) for g in by_core(*gains))
    grad_gain = (gains[:gain_rows] + gains[gain_rows:]).reshape(width)
    grads = jnp.stack(by_core(everyone[:, :extra], theirs[:, :extra]), 1)
    grads = grads.reshape(-1, LANES).astype(F32)
    grad_out = jnp.concatenate(jnp.split(grads[: inner * width // LANES], width // LANES), 1)
    grad_in = jnp.concatenate(jnp.split(grads[inner * width // LANES :], inner // LANES), 1)

    edge_factor = (degree.shape[0] * owners * lax.axis_size("narrow")) ** (-0.5)
    return (
        updated,
        grad_nodes,
        grad_in * edge_factor,
        grad_out * edge_factor,
        grad_gain * (nodes * owners) ** (-0.5),
    )


def solution(mesh):
    return jax.shard_map(
        shards,
        mesh=mesh,
        in_specs=(
            P("wide", None),
            P("wide", None, "narrow", None),
            P("wide", "narrow", None, None),
            P("wide", "narrow", None),
            P("wide", "narrow", None, None, None, None),
            P(("wide", "narrow")),
            P(),
            P(),
            P(),
            P("wide", None),
        ),
        out_specs=(P("wide", None), P("wide", None), P(), P(), P()),
        check_vma=False,
    )
```

time: 504 us -> 493 us (0.978)
  blocking collectives: 454 us -> 433 us
  starting transfers between devices: 0.45 us -> 8.89 us
  waiting for transfers between devices: 5.81 us -> 13.2 us
    all_to_all x1 -> x0, blocking collectives: 20.8 us -> none  [shards(): lax.all_to_all(jnp.broadcast_to(chunk[None], (owners,) + chunk.shape), 'w...]
    all_to_all x0 -> x1, waiting for transfers between devices: none -> 11.1 us  [shards(): lax.all_to_all(jnp.broadcast_to(chunk[None], (owners,) + chunk.shape), 'w...]
    all_to_all x0 -> x1, starting transfers between devices: none -> 8.03 us  [shards(): lax.all_to_all(jnp.broadcast_to(chunk[None], (owners,) + chunk.shape), 'w...]
    unnamed x27 -> x13, local copies, waits for them, and re-layouts: 7.49 us -> 0.81 us
  transfers between devices with their start and end apart: 4 -> 5, of which waited for: 3 -> 3; matrix products, arithmetic and copies ran while one was open for 0% -> 1% of each run, Pallas kernels for 1% -> 0%
where the time goes in v7:
time: 493 us; the launch traced here: 491 us
  blocking collectives  433 us (88%)
  Pallas kernels  26.7 us (5%)
  waiting for transfers between devices  13.2 us (3%)
  starting transfers between devices  8.89 us (2%)
  local copies, waits for them, and re-layouts  4.98 us (1%)
    all_to_all x4, blocking collectives, exchange(): lax.all_to_all(tiles, ('wide', 'narrow'), split_axis=0, concat_axis=0, ti...  433 us
    all_to_all x1, waiting for transfers between devices, shards(): lax.all_to_all(jnp.broadcast_to(chunk[None], (owners,) + chunk.shape), 'w...  11.1 us
    pallas_call x1, Pallas kernels, edges_forward(): pl.pallas_call(forward_kernel, out_shape=(jax.ShapeDtypeStruct((tiles, ro...  10.1 us
  transfers between devices with their start and end apart: 5, of which 3 were waited for; matrix products, arithmetic and copies ran while one was open for 1% of the time, Pallas kernels for 0%

profile of v7, /device:TPU:0, one launch (start us, length us, event | category | flops | bytes accessed | tf_op | source)
XLA Modules:
  0.0 491.1 jit_solution(17974139714262096919)
XLA Ops:
  0.6 0.1 collective-permute-start
  0.7 1.1 constant_dynamic-slice_fusion
  1.8 0.8 copy.23
  2.6 0.1 reshape.57.recv_ref
  2.7 0.0 collective-permute-done
  2.7 0.7 select_bitcast_fusion.3
  3.4 0.1 copy.21
  3.5 0.2 reshape.54.send_ref
  3.7 1.2 select_blocks.1
  4.9 0.0 copy-start
  4.9 0.0 copy-start.1
  4.9 0.0 copy-start.2
  4.9 0.0 copy-start.3
  4.9 0.0 copy-start.5
  4.9 109.5 %all_to_all.25.arrived = bf16[128,128,256]{2,1,0:T(8,128)(2,1)S(1)} all-to-all(bf16[128,128,256]{2,1,0:T(8,128)(2,1)S(1)} %select_blocks.1), channel_id=1, replica_groups=mesh['wide'=64,'narrow'=2] {'wide','narrow'}, dimensions={0} | all-to-all | bytes 16777216 | tf_op jit(solution)/shard_map/all_to_all | solution.py:338
  114.4 0.0 copy-done
  114.4 0.0 copy-done.1
  114.4 0.0 copy-done.2
  114.4 0.0 copy-done.3
  114.4 0.0 copy-done.5
  114.5 10.1 %edges_forward.1 = (bf16[128,256,128]{2,1,0:T(8,128)(2,1)S(1)}, bf16[128,128,128]{2,1,0:T(8,128)(2,1)S(1)}, bf16[128,128,128]{2,1,0:T(8,128)(2,1)S(1)}, bf16[204...) custom-call(s32[128]{0:T(128)S(1)} %reshape.57.recv_ref, s32[64]{0:T(128)S(1)} %bitcast.51, ...), custom_call_target="tpu_custom_call" | custom-call | tf_op jit(solution)/shard_map/edges_forward/pallas_call | solution.py:201
  124.6 0.0 copy-start.4
  124.6 105.9 %all_to_all.26.arrived = bf16[128,256,128]{2,1,0:T(8,128)(2,1)S(1)} all-to-all(bf16[128,256,128]{2,1,0:T(8,128)(2,1)S(1)} %get-tuple-element.29), channel_id=1, replica_groups=mesh['wide'=64,'narrow'=2] {'wide','narrow'}, dimensions={0} | all-to-all | bytes 16777216 | tf_op jit(solution)/shard_map/all_to_all | solution.py:338
  230.5 0.0 copy-done.4
  230.5 4.2 norm_and_select.1
  234.7 105.9 %all_to_all.27.arrived = bf16[128,128,256]{2,1,0:T(8,128)(2,1)S(1)} all-to-all(bf16[128,128,256]{2,1,0:T(8,128)(2,1)S(1)} %get-tuple-element.31), channel_id=1, replica_groups=mesh['wide'=64,'narrow'=2] {'wide','narrow'}, dimensions={0} | all-to-all | bytes 16777216 | tf_op jit(solution)/shard_map/all_to_all | solution.py:338
  340.6 8.5 %edges_backward.1 = bf16[128,272,128]{2,1,0:T(8,128)(2,1)S(1)} custom-call(s32[128]{0:T(128)S(1)} %reshape.57.recv_ref, bf16[128,128,256]{2,1,0:T(8,128)(2,1)S(1)} %all_to_all.27.arrived, bf16[128,128,128]{2,1,0:T(8,128)(2,1)S(1)} %get-tuple-element.32.mask_t, bf16[128,128,128]{2,1,0:T(8,128)(2,1)S(1)} %get-tuple-element.33.mask, s32[16,128]{1,0:T(8,128)S(1)} %bitcast.49, ...), custom_call_target="tpu_custom_call" | custom-call | tf_op jit(solution)/shard_map/edges_backward/pallas_call | solution.py:227
  349.1 111.9 %all_to_all.28.arrived.arrived_ref = bf16[128,272,128]{2,1,0:T(8,128)(2,1)S(1)} all-to-all(bf16[128,272,128]{2,1,0:T(8,128)(2,1)S(1)} %edges_backward.1), channel_id=1, replica_groups=mesh['wide'=64,'narrow'=2] {'wide','narrow'}, dimensions={0} | all-to-all | bytes 17825792 | tf_op jit(solution)/shard_map/all_to_all | solution.py:338
  461.0 2.5 node_grads.1
  463.5 0.4 collective-permute-start.1
  463.9 0.3 collective-permute-start.2
  464.3 0.2 weight_sums.1
  464.4 1.6 collective-permute-done.2
  466.0 0.0 collective-permute-done.1
  466.0 0.8 broadcast_in_dim.10
  466.8 8.0 %all-to-all-start.4 = ((bf16[64,24,128]{2,1,0:T(8,128)(2,1)}), bf16[64,24,128]{2,1,0:T(8,128)(2,1)S(1)}, u32[]{:S(2)}, u32[]{:S(2)}) async-start(bf16[64,24,128]{2,1,0:T(8,128)(2,1)} %broadcast_in_dim.10), calls=%async_computation.4 | async-start | bytes 786432 | tf_op jit(solution)/shard_map/all_to_all | solution.py:396
  474.9 0.1 pad_maximum_fusion.1
  475.0 0.8 copy.25
  475.8 11.1 %all-to-all-done.4 = bf16[64,24,128]{2,1,0:T(8,128)(2,1)S(1)} async-done(((bf16[64,24,128]{2,1,0:T(8,128)(2,1)}), bf16[64,24,128]{2,1,0:T(8,128)(2,1)S(1)}, u32[]{:S(2)}, u32[]{:S(2)}) %all-to-all-start.4) | async-done | bytes 393248 | tf_op jit(solution)/shard_map/all_to_all | solution.py:396
  487.0 0.0 collective-permute-start.3
  487.0 0.1 broadcast_select_fusion.1
  487.0 0.1 pad_maximum_fusion
  487.1 1.1 copy.26
  488.2 0.5 collective-permute-done.3
  488.8 0.1 convert_reduce_fusion
  488.9 0.6 multiply_bitcast_fusion
  489.5 0.8 maximum_multiply_fusion.1
  490.3 0.8 maximum_multiply_fusion
  (9 shorter events, 0.2 us)
Async XLA Ops:
  0.6 2.1 collective-permute-start
  4.9 109.5 %copy-start = (bf16[256,512]{1,0:T(8,128)(2,1)S(1)}, bf16[256,512]{1,0:T(8,128)(2,1)}, u32[]{:S(2)}) copy-start(bf16[256,512]{1,0:T(8,128)(2,1)} %w_in_ref.3) | copy-start | bytes 786436
  4.9 109.5 %copy-start.1 = (bf16[512,256]{1,0:T(8,128)(2,1)S(1)}, bf16[512,256]{1,0:T(8,128)(2,1)}, u32[]{:S(2)}) copy-start(bf16[512,256]{1,0:T(8,128)(2,1)} %w_out_ref.3) | copy-start | bytes 786436
  4.9 109.5 %copy-start.2 = (s32[1,1,64,2,9,128]{5,3,4,2,1,0:T(2,128)S(1)}, s32[1,1,64,2,9,128]{5,3,4,2,1,0:T(2,128)}, u32[]{:S(2)}) copy-start(s32[1,1,64,2,9,128]{5,3,4,2,1,0:T(2,128)} %param.14) | copy-start | bytes 1769476
  4.9 109.5 %copy-start.3 = (s32[2048]{0:T(1024)S(1)}, s32[2048]{0:T(1024)}, u32[]{:S(2)}) copy-start(s32[2048]{0:T(1024)} %param.15) | copy-start | bytes 24580
  4.9 109.5 %copy-start.5 = (s32[1,1,64]{2,1,0:T(1,128)S(1)}, s32[1,1,64]{2,1,0:T(1,128)}, u32[]{:S(2)}) copy-start(s32[1,1,64]{2,1,0:T(1,128)} %param.13) | copy-start | bytes 772
  124.6 105.9 %copy-start.4 = (f32[256]{0:T(256)S(1)}, f32[256]{0:T(256)}, u32[]{:S(2)}) copy-start(f32[256]{0:T(256)} %param.18) | copy-start | bytes 3076
  463.5 2.5 collective-permute-start.1
  463.9 2.1 collective-permute-start.2
  466.8 20.1 %all-to-all-start.4 = ((bf16[64,24,128]{2,1,0:T(8,128)(2,1)}), bf16[64,24,128]{2,1,0:T(8,128)(2,1)S(1)}, u32[]{:S(2)}, u32[]{:S(2)}) async-start(bf16[64,24,128]{2,1,0:T(8,128)(2,1)} %broadcast_in_dim.10), calls=%async_computation.4 | async-start | bytes 786432 | tf_op jit(solution)/shard_map/all_to_all | solution.py:396
  487.0 1.7 collective-permute-start.3

commit v8 on v7

--- a/solution.py
+++ b/solution.py
@@ -44,26 +44,16 @@
     return jnp.concatenate(groups, axis=0)
 
 
-def unpack(count_ref, words_ref, mask_ref, mask_t_ref):
-    owners, words, slots, _ = words_ref.shape
-    per = 8
-
-    def body(i, carry):
-        row = lax.broadcasted_iota(jnp.int32, (8, TILE), 0)
-        for k in range(per):
-            owner = i * per + k
-            count = count_ref[owner]
-            for slot in range(slots):
-                live = jnp.where(count > slot, jnp.int32(-1), jnp.int32(0))
-                word = [
-                    jnp.broadcast_to(words_ref[owner, j, slot : slot + 1], (8, TILE)) & live for j in range(words)
-                ]
-                mask = unpack_tile(word, row)
-                mask_ref[owner * slots + slot] = mask.astype(BF16)
-                mask_t_ref[owner * slots + slot] = mask.T.astype(BF16)
-        return carry
-
-    lax.fori_loop(0, owners // per, body, 0)
+def unpack(count_ref, words_ref, owner, slot):
+    live = jnp.where(count_ref[owner] > slot, jnp.int32(-1), jnp.int32(0))
+    row = lax.broadcasted_iota(jnp.int32, (8, TILE), 0)
+    return unpack_tile(
+        [
+            jnp.broadcast_to(words_ref[owner, j, slot : slot + 1], (8, TILE)) & live
+            for j in range(words_ref.shape[1])
+        ],
+        row,
+    )
 
 
 def steps_of(tiles, size=STEP_TILES):
@@ -98,7 +88,7 @@
     )(send, rows)
 
 
-def collect(recv_ref, arrived, mask_t, acc):
+def collect(recv_ref, arrived, mask_t, acc, unpacked=None):
     acc[...] = jnp.zeros_like(acc)
 
     def body(i, carry):
@@ -106,6 +96,11 @@
             tile = i * EDGE_TILES + k
             owner, slot = i * (EDGE_TILES // 2) + k // 2, k % 2
             halves = [arrived[2 * owner + c, slot * HALF : (slot + 1) * HALF] for c in range(2)]
+            if unpacked is not None:
+                count_ref, words_ref, mask = unpacked
+                bits = unpack(count_ref, words_ref, owner, slot)
+                mask[tile] = bits.astype(BF16)
+                mask_t[tile] = bits.T.astype(BF16)
             acc[rows_at(recv_ref[tile])] += dot(mask_t[tile], jnp.concatenate(halves, axis=0))
         return carry
 
@@ -150,8 +145,7 @@
     recv_ref, count_ref, arrived, words_ref, degree_ref, w_in_ref, w_out_ref,
     made, mask_t, mask, feats, act, gate, acc, values,
 ):
-    unpack(count_ref, words_ref, mask, mask_t)
-    collect(recv_ref, arrived, mask_t, acc)
+    collect(recv_ref, arrived, mask_t, acc, (count_ref, words_ref, mask))
     chunk = min(EDGE_CHUNK, acc.shape[0])
 
     def body(i, carry):
@@ -288,6 +282,63 @@
     )(arrived)
 
 
+def finish_kernel(
+    factors, core_ref, mine, theirs, grads_mine, grads_theirs, updated_mine, updated_theirs,
+    updated_ref, nodes_ref, in_ref, out_ref, gain_ref,
+):
+    edge_factor, node_factor = factors
+    owners = mine.shape[0]
+    pieces, inner = out_ref.shape[1] // LANES, out_ref.shape[0]
+    extra = pieces * inner // owners
+
+    def place(both, grads, updated):
+        for c in range(2):
+            for block in range(grads_mine.shape[0] // HALF):
+                at = (2 * block + c) * HALF
+                nodes_ref[at : at + HALF] = grads[c][block * HALF : (block + 1) * HALF]
+                updated_ref[at : at + HALF] = updated[c][block * HALF : (block + 1) * HALF]
+        for d in range(2 * owners):
+            rows = both[d % 2][d // 2, :extra].astype(F32) * edge_factor
+            at = d * extra
+            if at < pieces * inner:
+                lane = at // inner * LANES
+                out_ref[at % inner : at % inner + extra, lane : lane + LANES] = rows
+            else:
+                at -= pieces * inner
+                deep = in_ref.shape[0]
+                lane = at // deep * LANES
+                in_ref[at % deep : at % deep + extra, lane : lane + LANES] = rows
+        gains = sum(jnp.sum(half[:, extra:].astype(F32), axis=0) for half in both)
+        gain = jnp.concatenate([gains[i : i + 1] + gains[pieces + i : pieces + i + 1] for i in range(pieces)], axis=1)
+        gain_ref[...] = gain * node_factor
+
+    @pl.when(core_ref[0] == 0)
+    def _():
+        place((mine, theirs), (grads_mine, grads_theirs), (updated_mine, updated_theirs))
+
+    @pl.when(core_ref[0] != 0)
+    def _():
+        place((theirs, mine), (grads_theirs, grads_mine), (updated_theirs, updated_mine))
+
+
+def finish(core, mine, theirs, grads, updated, inner, factors):
+    nodes, width = 2 * grads[0].shape[0], grads[0].shape[1]
+    return pl.pallas_call(
+        functools.partial(finish_kernel, factors),
+        out_shape=(
+            jax.ShapeDtypeStruct((nodes, width), BF16),
+            jax.ShapeDtypeStruct((nodes, width), F32),
+            jax.ShapeDtypeStruct((width, inner), F32),
+            jax.ShapeDtypeStruct((inner, width), F32),
+            jax.ShapeDtypeStruct((1, width), F32),
+        ),
+        in_specs=[SMEM] + [VMEM] * 6,
+        out_specs=(VMEM,) * 5,
+        compiler_params=PARAMS,
+        name="finish",
+    )(core, mine, theirs, *grads, *updated)
+
+
 def norm_kernel(
     send_ref, arrived, feats_ref, cot_ref, gain_ref, updated_ref, part_ref, out_ref, acc, d_summed
 ):
@@ -336,6 +387,10 @@
 
 def exchange(tiles):
     return lax.all_to_all(tiles, ("wide", "narrow"), split_axis=0, concat_axis=0, tiled=True)
+
+
+def exchange_wide(chunks):
+    return lax.all_to_all(chunks, "wide", split_axis=0, concat_axis=0, tiled=True)
 
 
 def swap(rows):
@@ -369,9 +424,6 @@
     half_of = lambda rows: lax.dynamic_index_in_dim(
         rows.reshape(-1, 2, HALF, width), core, 1, keepdims=False
     ).reshape(-1, width)
-    whole_of = lambda mine, theirs: jnp.stack(
-        [half.reshape(-1, HALF, width) for half in by_core(mine, theirs)], 1
-    ).reshape(nodes, width)
 
     feats_half, cot_half = half_of(node_feats), half_of(cotangent)
     picked, recv, count, words, cot_half = lax.optimization_barrier(
@@ -388,34 +440,23 @@
 
     arrived, updated, gain_part = lax.optimization_barrier((arrived, updated, gain_part))
     weight_sums = tail_sum(arrived, 2 * width // LANES * HALF)
-    extra = weight_sums.shape[0]
-    gain_rows = width // LANES
-    chunk = jnp.concatenate([weight_sums.astype(BF16), gain_part[: max(8, 2 * gain_rows)]], 0)
+    chunk = jnp.concatenate([weight_sums.astype(BF16), gain_part[: max(8, 2 * width // LANES)]], 0)
     grads_half = node_grads(send, arrived, cot_half)
     grads_other, updated_other, chunk = lax.optimization_barrier((swap(grads_half), swap(updated), chunk))
-    everyone = lax.all_to_all(
-        jnp.broadcast_to(chunk[None], (owners,) + chunk.shape), "wide", split_axis=0, concat_axis=0, tiled=True
+    everyone = exchange_wide(jnp.broadcast_to(chunk[None], (owners,) + chunk.shape))
+    edge_factor = (degree.shape[0] * devices) ** (-0.5)
+    node_factor = (nodes * owners) ** (-0.5)
+    core_at = core.astype(jnp.int32).reshape(1)
+    updated, grad_nodes, grad_in, grad_out, grad_gain = finish(
+        core_at,
+        everyone,
+        swap(everyone),
+        (grads_half, grads_other),
+        (updated, updated_other),
+        inner,
+        (edge_factor, node_factor),
     )
-    grad_nodes = whole_of(grads_half, grads_other)
-    updated = whole_of(updated, updated_other)
-
-    theirs = swap(everyone)
-    gains = (everyone[:, extra : extra + 2 * gain_rows], theirs[:, extra : extra + 2 * gain_rows])
-    gains = sum(g.astype(F32).sum(0) for g in by_core(*gains))
-    grad_gain = (gains[:gain_rows] + gains[gain_rows:]).reshape(width)
-    grads = jnp.stack(by_core(everyone[:, :extra], theirs[:, :extra]), 1)
-    grads = grads.reshape(-1, LANES).astype(F32)
-    grad_out = jnp.concatenate(jnp.split(grads[: inner * width // LANES], width // LANES), 1)
-    grad_in = jnp.concatenate(jnp.split(grads[inner * width // LANES :], inner // LANES), 1)
-
-    edge_factor = (degree.shape[0] * owners * lax.axis_size("narrow")) ** (-0.5)
-    return (
-        updated,
-        grad_nodes,
-        grad_in * edge_factor,
-        grad_out * edge_factor,
-        grad_gain * (nodes * owners) ** (-0.5),
-    )
+    return updated, grad_nodes, grad_in, grad_out, grad_gain.reshape(width)
 
 
 def solution(mesh):

time: 493 us -> 491 us (level)
  blocking collectives: 433 us -> 454 us
  waiting for transfers between devices: 13.2 us -> 3.31 us
  starting transfers between devices: 8.89 us -> 0.68 us
    all_to_all x0 -> x1, blocking collectives: none -> 20.8 us  [exchange_wide(): lax.all_to_all(chunks, 'wide', split_axis=0, concat_axis=0, tiled=True)]
    all_to_all x1 -> x0, waiting for transfers between devices: 11.1 us -> none  [shards(): lax.all_to_all(jnp.broadcast_to(chunk[None], (owners,) + chunk.shape), 'w...]
    all_to_all x1 -> x0, starting transfers between devices: 8.03 us -> none  [shards(): lax.all_to_all(jnp.broadcast_to(chunk[None], (owners,) + chunk.shape), 'w...]
  transfers between devices with their start and end apart: 5 -> 4, of which waited for: 3 -> 2; matrix products, arithmetic and copies ran while one was open for 1% -> 0% of each run, Pallas kernels for 0% -> 0%
where the time goes in v8:
time: 491 us; the launch traced here: 490 us
  blocking collectives  454 us (92%)
  Pallas kernels  27.7 us (6%)
    all_to_all x4, blocking collectives, exchange(): lax.all_to_all(tiles, ('wide', 'narrow'), split_axis=0, concat_axis=0, ti...  433 us
    all_to_all x1, blocking collectives, exchange_wide(): lax.all_to_all(chunks, 'wide', split_axis=0, concat_axis=0, tiled=True)  20.8 us
  transfers between devices with their start and end apart: 4, of which 2 were waited for; matrix products, arithmetic and copies ran while one was open for 0% of the time, Pallas kernels for 0%

profile of v8, /device:TPU:0, one launch (start us, length us, event | category | flops | bytes accessed | tf_op | source)
XLA Modules:
  0.0 489.8 jit_solution(18150116877749678650)
XLA Ops:
  0.6 0.1 collective-permute-start
  0.7 1.1 constant_dynamic-slice_fusion
  1.8 0.8 copy.20
  2.6 0.1 reshape.47.recv_ref
  2.7 0.0 collective-permute-done
  2.7 0.7 select_bitcast_fusion.1
  3.4 0.1 copy.18
  3.5 0.2 reshape.44.send_ref
  3.7 1.2 select_blocks.1
  4.9 0.0 copy-start
  4.9 0.0 copy-start.1
  4.9 0.0 copy-start.2
  4.9 0.0 copy-start.3
  4.9 0.0 copy-start.5
  4.9 109.5 %all_to_all.25.arrived = bf16[128,128,256]{2,1,0:T(8,128)(2,1)S(1)} all-to-all(bf16[128,128,256]{2,1,0:T(8,128)(2,1)S(1)} %select_blocks.1), channel_id=1, replica_groups=mesh['wide'=64,'narrow'=2] {'wide','narrow'}, dimensions={0} | all-to-all | bytes 16777216 | tf_op jit(solution)/shard_map/all_to_all | solution.py:389
  114.4 0.0 copy-done
  114.4 0.0 copy-done.1
  114.4 0.0 copy-done.2
  114.4 0.0 copy-done.3
  114.4 0.0 copy-done.5
  114.5 9.4 %edges_forward.1 = (bf16[128,256,128]{2,1,0:T(8,128)(2,1)S(1)}, bf16[128,128,128]{2,1,0:T(8,128)(2,1)S(1)}, bf16[128,128,128]{2,1,0:T(8,128)(2,1)S(1)}, bf16[204...) custom-call(s32[128]{0:T(128)S(1)} %reshape.47.recv_ref, s32[64]{0:T(128)S(1)} %bitcast.33, ...), custom_call_target="tpu_custom_call" | custom-call | tf_op jit(solution)/shard_map/edges_forward/pallas_call | solution.py:195
  123.9 0.0 copy-start.4
  123.9 105.9 %all_to_all.26.arrived = bf16[128,256,128]{2,1,0:T(8,128)(2,1)S(1)} all-to-all(bf16[128,256,128]{2,1,0:T(8,128)(2,1)S(1)} %get-tuple-element.34), channel_id=1, replica_groups=mesh['wide'=64,'narrow'=2] {'wide','narrow'}, dimensions={0} | all-to-all | bytes 16777216 | tf_op jit(solution)/shard_map/all_to_all | solution.py:389
  229.8 0.0 copy-done.4
  229.8 4.2 norm_and_select.1
  234.0 105.9 %all_to_all.27.arrived = bf16[128,128,256]{2,1,0:T(8,128)(2,1)S(1)} all-to-all(bf16[128,128,256]{2,1,0:T(8,128)(2,1)S(1)} %get-tuple-element.36), channel_id=1, replica_groups=mesh['wide'=64,'narrow'=2] {'wide','narrow'}, dimensions={0} | all-to-all | bytes 16777216 | tf_op jit(solution)/shard_map/all_to_all | solution.py:389
  339.9 8.5 %edges_backward.1 = bf16[128,272,128]{2,1,0:T(8,128)(2,1)S(1)} custom-call(s32[128]{0:T(128)S(1)} %reshape.47.recv_ref, bf16[128,128,256]{2,1,0:T(8,128)(2,1)S(1)} %all_to_all.27.arrived, bf16[128,128,128]{2,1,0:T(8,128)(2,1)S(1)} %get-tuple-element.37.mask_t, bf16[128,128,128]{2,1,0:T(8,128)(2,1)S(1)} %get-tuple-element.38.mask, s32[16,128]{1,0:T(8,128)S(1)} %bitcast.31, ...), custom_call_target="tpu_custom_call" | custom-call | tf_op jit(solution)/shard_map/edges_backward/pallas_call | solution.py:221
  348.4 112.1 %all_to_all.28.arrived.arrived_ref = bf16[128,272,128]{2,1,0:T(8,128)(2,1)S(1)} all-to-all(bf16[128,272,128]{2,1,0:T(8,128)(2,1)S(1)} %edges_backward.1), channel_id=1, replica_groups=mesh['wide'=64,'narrow'=2] {'wide','narrow'}, dimensions={0} | all-to-all | bytes 17825792 | tf_op jit(solution)/shard_map/all_to_all | solution.py:389
  460.5 2.5 node_grads.1.grads_mine
  463.0 0.3 collective-permute-start.1
  463.3 0.3 collective-permute-start.2
  463.6 0.2 weight_sums.1
  463.8 1.6 collective-permute-done.2.updated_theirs
  465.4 0.0 collective-permute-done.1.grads_theirs
  465.4 0.1 broadcast_in_dim.10
  465.5 20.8 %all_to_all.29.mine = bf16[64,24,128]{2,1,0:T(8,128)(2,1)S(1)} all-to-all(bf16[64,24,128]{2,1,0:T(8,128)(2,1)S(1)} %broadcast_in_dim.10), channel_id=1, replica_groups=mesh['wide'=64,'narrow'=2] {'wide'}, dimensions={0} | all-to-all | bytes 786432 | tf_op jit(solution)/shard_map/all_to_all | solution.py:393
  486.3 0.0 collective-permute-start.3
  486.3 1.7 collective-permute-done.3.theirs
  488.0 1.8 finish.1
  (4 shorter events, 0.0 us)
Async XLA Ops:
  0.6 2.1 collective-permute-start
  4.9 109.5 %copy-start = (bf16[256,512]{1,0:T(8,128)(2,1)S(1)}, bf16[256,512]{1,0:T(8,128)(2,1)}, u32[]{:S(2)}) copy-start(bf16[256,512]{1,0:T(8,128)(2,1)} %w_in_ref.3) | copy-start | bytes 786436
  4.9 109.5 %copy-start.1 = (bf16[512,256]{1,0:T(8,128)(2,1)S(1)}, bf16[512,256]{1,0:T(8,128)(2,1)}, u32[]{:S(2)}) copy-start(bf16[512,256]{1,0:T(8,128)(2,1)} %w_out_ref.3) | copy-start | bytes 786436
  4.9 109.5 %copy-start.2 = (s32[1,1,64,2,9,128]{5,3,4,2,1,0:T(2,128)S(1)}, s32[1,1,64,2,9,128]{5,3,4,2,1,0:T(2,128)}, u32[]{:S(2)}) copy-start(s32[1,1,64,2,9,128]{5,3,4,2,1,0:T(2,128)} %param.14) | copy-start | bytes 1769476
  4.9 109.5 %copy-start.3 = (s32[2048]{0:T(1024)S(1)}, s32[2048]{0:T(1024)}, u32[]{:S(2)}) copy-start(s32[2048]{0:T(1024)} %param.15) | copy-start | bytes 24580
  4.9 109.5 %copy-start.5 = (s32[1,1,64]{2,1,0:T(1,128)S(1)}, s32[1,1,64]{2,1,0:T(1,128)}, u32[]{:S(2)}) copy-start(s32[1,1,64]{2,1,0:T(1,128)} %param.13) | copy-start | bytes 772
  123.9 105.9 %copy-start.4 = (f32[256]{0:T(256)S(1)}, f32[256]{0:T(256)}, u32[]{:S(2)}) copy-start(f32[256]{0:T(256)} %param.18) | copy-start | bytes 3076
  463.0 2.4 collective-permute-start.1
  463.3 2.1 collective-permute-start.2
  486.3 1.7 collective-permute-start.3
